TPU v7x, 512 devices: a whole 4x4x16 slice. The times are simulated.
512 devices in a mesh: section: 8 (over y, core), dp: 32 (over z, x_hi), grp: 2 (over x_lo).
Axes of the slice: x: 4 (x_hi: 2, x_lo: 2; x = x_hi * 2 + x_lo), y: 4, z: 16, core: 2. Of those that a mesh axis runs over, the one named last changes fastest.
Arguments:
- hidden: bfloat16 [14336, 14336], P('dp', ('section', 'grp')), may hold values from -6 to 6
- residual: bfloat16 [14336, 4096], P('dp', ('section', 'grp')), may hold values from -6 to 6
- down_weight: bfloat16 [14336, 4096], P(('section', 'grp'), 'dp'), may hold values from -0.09375 to 0.09375
- norm_gain: float32 [4096], replicated, may hold values from 0.3 to 3
- seq_lengths: int32 [32, 32], P('dp'), may hold values from 1 to 64, 448 in all within a row
- owner_slot: int32 [32, 32], P('dp'), may hold values from 0 to 31, each once within a row
- student_emb: bfloat16 [1024, 1024], P('dp'), may hold values from -6 to 6
- proj_weight: bfloat16 [1024, 4096], P(None, ('section', 'grp')), may hold values from -0.1875 to 0.1875
Outputs:
- grad_proj: float32 [1024, 4096], P(None, ('section', 'grp'))
- grad_student: float32 [1024, 1024], P('dp')
- loss: float32 [], replicated
Inputs may be any that keep to these rules, and one draw needn't show every extreme that they name: Each row of owner_slot holds every number of 0 to 31 once. `seq_lengths`: each row sums to 448; some entry of each row equals 64.
All inputs are finite; a program needn't handle non-finite values.
Results may differ from a plain program's by a relative error of at most 0.015.
Values may be sent and summed in bfloat16 or wider, within the bound.
No kernel may reach another device: no remote copies, remote signals or barrier semaphores. Data moves between devices by JAX's collectives and lax.ppermute only.
A program may use at most 64 MiB of HBM per device.

v0:
```python
import jax
import jax.numpy as jnp
from jax import lax
from jax.sharding import PartitionSpec as P

D = 4096


grad_scale = 262144.0


def feature_sum(values):
    return lax.psum(values, ("section", "grp"))


def membership(count, starts, lengths):
    places = jnp.arange(count, dtype=jnp.int32)
    inside = (places[None, :] >= starts[:, None]) & (places[None, :] < (starts + lengths)[:, None])
    return inside.astype(jnp.bfloat16)


def on_device(
    hidden, residual, down_weight, norm_gain, seq_lengths, owner_slot, student_emb, proj_weight
):
    column_rank = lax.axis_index(("section", "grp"))
    tok_count = hidden.shape[0]
    width = residual.shape[1]
    lengths = seq_lengths.reshape(-1)
    starts = jnp.cumsum(lengths) - lengths
    partial_value = jnp.dot(
        hidden,
        lax.all_gather(down_weight, "dp", axis=1, tiled=True),
        preferred_element_type=jnp.float32,
    )
    summed = lax.psum_scatter(
        partial_value.astype(jnp.bfloat16), ("section", "grp"), scatter_dimension=1, tiled=True
    ).astype(jnp.float32)
    y_cols = summed + residual.astype(jnp.float32)
    squares = feature_sum(jnp.sum(y_cols * y_cols, axis=1))
    gain_cols = lax.dynamic_slice_in_dim(norm_gain, column_rank * width, width)
    normed = (y_cols * lax.rsqrt(squares / D + 1e-05)[:, None] * gain_cols).astype(jnp.bfloat16)
    pooled_sum = jnp.dot(
        membership(tok_count, starts, lengths), normed, preferred_element_type=jnp.float32
    )
    pooled = (pooled_sum / lengths[:, None].astype(jnp.float32)).astype(jnp.bfloat16)
    owners = owner_slot.reshape(-1)
    select = (owners[None, :] == jnp.arange(owners.shape[0], dtype=jnp.int32)[:, None]).astype(
        jnp.bfloat16
    )
    outgoing = jnp.dot(select, pooled, preferred_element_type=jnp.float32).astype(jnp.bfloat16)
    arrived = lax.all_to_all(outgoing, "dp", split_axis=0, concat_axis=0, tiled=True)
    u_cols = jnp.dot(student_emb, proj_weight, preferred_element_type=jnp.float32)
    tch = arrived.astype(jnp.float32)
    sum_uu, sum_tt, cross = feature_sum(
        (
            jnp.sum(u_cols * u_cols, axis=1),
            jnp.sum(tch * tch, axis=1),
            jnp.sum(u_cols * tch, axis=1),
        )
    )
    root = jnp.sqrt(jnp.float32(D))
    scale_u = 1.0 / (root * jnp.sqrt(sum_uu / D + 1e-06))
    scale_t = 1.0 / (root * jnp.sqrt(sum_tt / D + 1e-06))
    uhat = u_cols * scale_u[:, None]
    that = tch * scale_t[:, None]
    cosv = cross * scale_u * scale_t
    uhat_b = uhat.astype(jnp.bfloat16)
    that_b = that.astype(jnp.bfloat16)
    all_u, all_t = (
        lax.all_gather(uhat_b, "dp", axis=0, tiled=True),
        lax.all_gather(that_b, "dp", axis=0, tiled=True),
    )
    batch_rows = all_u.shape[0]
    contract = (((1,), (1,)), ((), ()))
    part_u = lax.dot_general(uhat_b, all_u, contract, preferred_element_type=jnp.float32)
    part_t = lax.dot_general(that_b, all_t, contract, preferred_element_type=jnp.float32)
    gram_u, gram_t = feature_sum((part_u, part_t))
    diff = gram_u - gram_t
    diff_b = diff.astype(jnp.bfloat16)
    grad_hat = grad_scale * (
        -that / batch_rows
        + 4.0 / batch_rows * jnp.dot(diff_b, all_u, preferred_element_type=jnp.float32)
    )
    inner = feature_sum(jnp.sum(grad_hat * uhat, axis=1))
    du = ((grad_hat - uhat * inner[:, None]) * scale_u[:, None]).astype(jnp.bfloat16)
    grad_part = lax.dot_general(
        student_emb, du, (((0,), (0,)), ((), ())), preferred_element_type=jnp.float32
    )
    grad_student = feature_sum(
        lax.dot_general(du, proj_weight, contract, preferred_element_type=jnp.float32)
    )
    loss_part = (jnp.sum(1.0 - cosv) + jnp.sum(diff * diff)) / batch_rows
    grad_proj, loss = lax.psum((grad_part, loss_part), "dp")
    return (grad_proj, grad_student, loss)


def solution(mesh):
    placed = (
        P("dp", ("section", "grp")),
        P("dp", ("section", "grp")),
        P(("section", "grp"), "dp"),
        P(),
        P("dp", None),
        P("dp", None),
        P("dp", None),
        P(None, ("section", "grp")),
    )
    return jax.shard_map(
        on_device,
        mesh=mesh,
        in_specs=placed,
        out_specs=(P(None, ("section", "grp")), P("dp", None), P()),
        check_vma=False,
    )
```

profile of v0, /device:TPU:1, one launch (start us, length us, event | category | flops | bytes accessed | tf_op | source)
XLA Modules:
  0.0 1159.1 jit_solution(15697059699927792802)
XLA Ops:
  7.2 0.0 copy-start
  7.2 0.0 all-gather.2.cloned.1.call-start
  7.2 0.7 all-gather.2.cloned.1.call-update
  8.0 0.0 reduce-scatter.2.cloned.1.call-start
  8.0 199.1 %all-gather.2.cloned.1.call-done = bf16[896,4096]{1,0:T(8,128)(2,1)} async-done(((bf16[896,128]{1,0:T(8,128)(2,1)}), bf16[896,4096]{1,0:T(8,128)(2,1)}) %all-gather.2.cloned.1.call-update) | async-done | bytes 7340048 | tf_op jit(solution)/shard_map/all_gather | solution.py:32
  207.1 8.5 convolution_convert_fusion
  215.6 0.0 reduce-scatter.2.cloned.1.call-update
  215.7 0.1 copy.15
  215.8 0.1 reduce-window.7
  215.8 0.1 reduce
  215.9 0.8 dynamic_slice.3
  216.7 94.9 %reduce-scatter.2.cloned.1.call-done = bf16[448,256]{1,0:T(8,128)(2,1)} async-done(((bf16[448,4096]{1,0:T(8,128)(2,1)}), bf16[448,256]{1,0:T(8,128)(2,1)}) %reduce-scatter.2.cloned.1.call-update) | async-done | bytes 229392 | tf_op jit(solution)/shard_map/reduce_scatter | solution.py:35
  311.6 1.1 multiply_reduce_fusion
  312.7 28.2 %psum.70 = f32[448]{0:T(512)S(1)} all-reduce(f32[448]{0:T(512)S(1)} %multiply_reduce_fusion), channel_id=1, replica_groups=mesh['section'=8,'dp'=32,'grp'=2] {'section','grp'}, use_global_device_ids=true, to_apply=%region_3.4 | all-reduce | flops 448 | bytes 3584 | tf_op jit(solution)/shard_map/psum | solution.py:13
  341.0 1.3 fusion.3
  342.3 0.5 broadcast.51
  342.8 0.7 reduce.1
  343.4 0.6 reshape.55
  344.1 14.5 %all-to-all-start = ((bf16[32,2,128]{2,1,0:T(2,128)(2,1)}), bf16[32,2,128]{2,1,0:T(2,128)(2,1)S(1)}, u32[]{:S(2)}, u32[]{:S(2)}) async-start(bf16[32,2,128]{2,1,0:T(2,128)(2,1)} %reshape.55), calls=%async_computation.1 | async-start | bytes 32768 | tf_op jit(solution)/shard_map/all_to_all | solution.py:51
  358.6 0.0 all-reduce.11.cloned.1.call-start
  358.6 0.3 multiply_reduce_fusion.3
  358.9 13.1 %all-to-all-done = bf16[32,2,128]{2,1,0:T(2,128)(2,1)S(1)} async-done(((bf16[32,2,128]{2,1,0:T(2,128)(2,1)}), bf16[32,2,128]{2,1,0:T(2,128)(2,1)S(1)}, u32[]{:S(2)}, u32[]{:S(2)}) %all-to-all-start) | async-done | bytes 16416 | tf_op jit(solution)/shard_map/all_to_all | solution.py:51
  372.1 0.1 fusion.16
  372.2 29.4 %all-reduce.1 = (f32[32]{0:T(128)S(1)}, f32[32]{0:T(128)S(1)}) all-reduce(f32[32]{0:T(128)S(1)} %get-tuple-element.22, f32[32]{0:T(128)S(1)} %get-tuple-element.20), channel_id=1, replica_groups=mesh['section'=8,'dp'=32,'grp'=2] {'section','grp'}, use_global_device_ids=true, to_apply=%region_7.8 | all-reduce | flops 64 | bytes 512 | tf_op jit(solution)/shard_map/psum | solution.py:13
  401.6 0.1 multiply_convert_fusion.4
  401.7 60.7 %all_gather.10 = bf16[1024,256]{1,0:T(8,128)(2,1)S(1)} all-gather(bf16[32,256]{1,0:T(8,128)(2,1)S(1)} %multiply_convert_fusion.4), channel_id=1, replica_groups=mesh['section'=8,'dp'=32,'grp'=2] {'dp'}, dimensions={0}, use_global_device_ids=true | all-gather | bytes 540672 | tf_op jit(solution)/shard_map/all_gather | solution.py:70
  462.4 0.9 fusion.24
  463.4 0.1 fusion.13
  463.4 62.2 %all_gather.11 = bf16[1024,256]{1,0:T(8,128)(2,1)S(1)} all-gather(bf16[32,256]{1,0:T(8,128)(2,1)S(1)} %fusion.13), channel_id=1, replica_groups=mesh['section'=8,'dp'=32,'grp'=2] {'dp'}, dimensions={0}, use_global_device_ids=true | all-gather | bytes 540672 | tf_op jit(solution)/shard_map/all_gather | solution.py:71
  525.6 0.9 fusion.25
  526.5 0.0 all-reduce.11.cloned.1.call-update
  526.6 0.0 all-reduce.7.cloned.1.call-start
  526.6 151.0 %all-reduce.11.cloned.1.call-done = (f32[32,1024]{1,0:T(8,128)}, f32[32,1024]{1,0:T(8,128)}) async-done(((f32[32,1024]{1,0:T(8,128)}, f32[32,1024]{1,0:T(8,128)}), (f32[32,1024]{1,0:T(8,128)}, f32[32,1024]{1,0:T(8,128)})) %all-reduce.11.cloned.1.call-update) | async-done | bytes 262160 | tf_op jit(solution)/shard_map/psum | solution.py:13
  677.7 1.3 fusion.17
  678.9 29.4 %all-reduce = (f32[32]{0:T(128)S(1)}, f32[32]{0:T(128)S(1)}) all-reduce(f32[32]{0:T(128)S(1)} %get-tuple-element.13, f32[32]{0:T(128)S(1)} %get-tuple-element.12), channel_id=1, replica_groups=mesh['section'=8,'dp'=32,'grp'=2] {'section','grp'}, use_global_device_ids=true, to_apply=%region_11.12 | all-reduce | flops 64 | bytes 512 | tf_op jit(solution)/shard_map/psum | solution.py:13
  708.4 0.1 multiply_convert_fusion.3
  708.4 1.3 convolution_bitcast_fusion
  709.7 0.0 all-reduce.7.cloned.1.call-update
  709.8 0.0 all-reduce.9.cloned.1.call-start
  709.8 0.9 fusion.26
  710.7 0.0 all-reduce.9.cloned.1.call-update
  710.8 0.6 subtract_reduce_fusion
  711.4 1.6 multiply_reduce_fusion.1
  714.3 66.1 %psum.79 = f32[]{:T(128)} all-reduce(f32[]{:T(128)S(6)} %div.45), channel_id=1, replica_groups=mesh['section'=8,'dp'=32,'grp'=2] {'dp'}, use_global_device_ids=true, to_apply=%region_18.19 | all-reduce | flops 1 | bytes 8 | tf_op jit(solution)/shard_map/psum | solution.py:93
  780.4 219.5 %all-reduce.7.cloned.1.call-done = f32[1024,256]{0,1:T(8,128)} async-done(((f32[1024,256]{0,1:T(8,128)}), f32[1024,256]{0,1:T(8,128)}) %all-reduce.7.cloned.1.call-update) | async-done | bytes 1048592 | tf_op jit(solution)/shard_map/psum | solution.py:93
  999.8 2.5 copy.18
  1002.4 148.6 %all-reduce.9.cloned.1.call-done = f32[32,1024]{1,0:T(8,128)} async-done(((f32[32,1024]{1,0:T(8,128)}), f32[32,1024]{1,0:T(8,128)}) %all-reduce.9.cloned.1.call-update) | async-done | bytes 131088 | tf_op jit(solution)/shard_map/psum | solution.py:13
  1151.0 1.6 copy.25
  (17 shorter events, 0.1 us)
Async XLA Ops:
  7.2 199.9 %copy-start = (bf16[448,896]{1,0:T(8,128)(2,1)S(1)}, bf16[448,896]{1,0:T(8,128)(2,1)}, u32[]{:S(2)}) copy-start(bf16[448,896]{1,0:T(8,128)(2,1)} %param.8) | copy-start | bytes 2408452
  7.2 199.9 %all-gather.2.cloned.1.call-start = ((), (), s32[]{:S(2)}) async-start(), calls=%async_computation.2 | async-start | bytes 7569408 | tf_op jit(solution)/shard_map/all_gather | solution.py:32
  7.9 207.8 %copy-start.4 = (s32[1,32]{1,0:T(1,128)S(1)}, s32[1,32]{1,0:T(1,128)}, u32[]{:S(2)}) copy-start(s32[1,32]{1,0:T(1,128)} %param.12) | copy-start | bytes 388
  7.9 303.7 %copy-start.3 = (bf16[448,256]{1,0:T(8,128)(2,1)S(1)}, bf16[448,256]{1,0:T(8,128)(2,1)}, u32[]{:S(2)}) copy-start(bf16[448,256]{1,0:T(8,128)(2,1)} %param.9) | copy-start | bytes 688132
  7.9 333.0 %copy-start.5 = (s32[1,32]{1,0:T(1,128)S(1)}, s32[1,32]{1,0:T(1,128)}, u32[]{:S(2)}) copy-start(s32[1,32]{1,0:T(1,128)} %param.13) | copy-start | bytes 388
  7.9 350.7 %copy-start.1 = (bf16[1024,256]{1,0:T(8,128)(2,1)S(1)}, bf16[1024,256]{1,0:T(8,128)(2,1)}, u32[]{:S(2)}) copy-start(bf16[1024,256]{1,0:T(8,128)(2,1)} %param.15) | copy-start | bytes 1572868
  8.0 350.7 %copy-start.2 = (bf16[32,1024]{1,0:T(8,128)(2,1)S(1)}, bf16[32,1024]{1,0:T(8,128)(2,1)}, u32[]{:S(2)}) copy-start(bf16[32,1024]{1,0:T(8,128)(2,1)} %param.14) | copy-start | bytes 196612
  8.0 303.6 %reduce-scatter.2.cloned.1.call-start = ((), (), s32[]{:S(2)}) async-start(), calls=%async_computation.3 | async-start | bytes 3899392 | tf_op jit(solution)/shard_map/reduce_scatter | solution.py:35
  344.1 28.0 %all-to-all-start = ((bf16[32,2,128]{2,1,0:T(2,128)(2,1)}), bf16[32,2,128]{2,1,0:T(2,128)(2,1)S(1)}, u32[]{:S(2)}, u32[]{:S(2)}) async-start(bf16[32,2,128]{2,1,0:T(2,128)(2,1)} %reshape.55), calls=%async_computation.1 | async-start | bytes 32768 | tf_op jit(solution)/shard_map/all_to_all | solution.py:51
  358.6 319.1 %all-reduce.11.cloned.1.call-start = ((), (), s32[]{:S(2)}) async-start(), calls=%async_computation.6 | async-start | bytes 524288 | tf_op jit(solution)/shard_map/psum | solution.py:13
  526.6 473.3 %all-reduce.7.cloned.1.call-start = ((), (), s32[]{:S(2)}) async-start(), calls=%async_computation.4 | async-start | bytes 2097152 | tf_op jit(solution)/shard_map/psum | solution.py:93
  709.8 441.2 %all-reduce.9.cloned.1.call-start = ((), (), s32[]{:S(2)}) async-start(), calls=%async_computation.5 | async-start | bytes 262144 | tf_op jit(solution)/shard_map/psum | solution.py:13
Sparse Core Ops, SparseCore 0:
  10.9 196.1 all-gather.1
  215.8 95.7 reduce-scatter.1
  526.7 150.9 all-reduce.10
  709.9 289.9 all-reduce.6
  1003.2 147.7 all-reduce.8
where the time goes:
time: 1160 us
  waiting for transfers between devices  827 us (71%)
  blocking collectives  276 us (24%)
  matrix products  15.5 us (1%)
  between operations  15.2 us (1%)
  starting transfers between devices  14.7 us (1%)
    psum x2, waiting for transfers between devices, feature_sum(): return lax.psum(values, ('section', 'grp'))  300 us
    psum x1, waiting for transfers between devices, on_device(): grad_proj, loss = lax.psum((grad_part, loss_part), 'dp')  219 us
    all_gather x1, waiting for transfers between devices, on_device(): lax.all_gather(down_weight, 'dp', axis=1, tiled=True)  199 us
    reduce_scatter x1, waiting for transfers between devices, on_device(): lax.psum_scatter(partial_value.astype(jnp.bfloat16), ('section', 'grp'),...  94.9 us
    psum x3, blocking collectives, feature_sum(): return lax.psum(values, ('section', 'grp'))  87.1 us
    psum x1, blocking collectives, on_device(): grad_proj, loss = lax.psum((grad_part, loss_part), 'dp')  66.1 us
    all_gather x1, blocking collectives, on_device(): lax.all_gather(that_b, 'dp', axis=0, tiled=True)  62.2 us
    all_gather x1, blocking collectives, on_device(): lax.all_gather(uhat_b, 'dp', axis=0, tiled=True)  60.7 us
  transfers between devices with their start and end apart: 6, of which 6 were waited for; matrix products, arithmetic and copies ran while one was open for 1% of the time, Pallas kernels for 0%

commit v1 on v0

v1 whole, which is shorter than its diff:
```python
import jax
import jax.numpy as jnp
from jax import lax
from jax.experimental import pallas as pl
from jax.experimental.pallas import tpu as pltpu
from jax.sharding import Mesh, PartitionSpec as P

D = 4096
grad_scale = 262144.0
f32, bf16 = jnp.float32, jnp.bfloat16

ROW = ("y", "core", "xl")
HALF = ("y", "xl")
PLANE = ("y", "core", "xh", "xl")
CHIPS = ("y", "xl", "xh")
NT = (((1,), (1,)), ((), ()))
TN = (((0,), (0,)), ((), ()))


def swap(value, axis):
    return lax.ppermute(value, axis, [(0, 1), (1, 0)])


def exchange(value, axes):
    return lax.all_to_all(value, axes, split_axis=0, concat_axis=0)


def share(value, axes, count):
    return exchange(jnp.broadcast_to(value[None], (count,) + value.shape), axes)


def ordered(index, own, other):
    first = index == 0
    return jnp.where(first, own, other), jnp.where(first, other, own)


def part_kernel(core_ref, hidden_ref, weight_ref, out_ref):
    both = jnp.concatenate([weight_ref[0], weight_ref[1]], axis=1)
    got = jnp.dot(hidden_ref[...], both, preferred_element_type=f32).astype(bf16)
    out_ref[0] = got[:, :128]
    out_ref[1] = got[:, 128:]


def parts_for(core, hidden, weight):
    tokens, depth = hidden.shape
    return pl.pallas_call(
        part_kernel,
        grid_spec=pltpu.PrefetchScalarGridSpec(
            num_scalar_prefetch=1,
            grid=(4,),
            in_specs=[
                pl.BlockSpec((tokens, depth), lambda i, c: (0, 0)),
                pl.BlockSpec((2, depth, 128), lambda i, c: (2 * i + c[0], 0, 0)),
            ],
            out_specs=pl.BlockSpec((2, tokens, 128), lambda i, c: (i, 0, 0)),
        ),
        out_shape=jax.ShapeDtypeStruct((8, tokens, 128), bf16),
        compiler_params=pltpu.CompilerParams(vmem_limit_bytes=32 << 20),
        cost_estimate=pl.CostEstimate(
            flops=2 * tokens * depth * 1024, bytes_accessed=5_000_000, transcendentals=0
        ),
    )(core.reshape(1).astype(jnp.int32), hidden, weight)


def on_device(
    hidden, residual, down_weight, norm_gain, seq_lengths, owner_slot, student_emb, proj_weight
):
    core, xh, z = lax.axis_index("core"), lax.axis_index("xh"), lax.axis_index("z")
    rank = lax.axis_index(ROW)
    root = jnp.sqrt(f32(D))
    low = xh == 0

    weight = lax.all_gather(down_weight, "z", axis=0)
    hidden2 = jnp.concatenate(ordered(xh, hidden, swap(hidden, "xh")), axis=0)

    left, right = residual[:, :128], residual[:, 128:]
    mine, theirs = jnp.where(low, left, right), jnp.where(low, right, left)
    table = jnp.pad(
        jnp.concatenate([seq_lengths, owner_slot], axis=1).astype(bf16), ((0, 15), (0, 64))
    )
    came = swap(jnp.concatenate([theirs, table], axis=0), "xh")
    residual2 = jnp.concatenate(ordered(xh, mine, came[:448]), axis=0)
    table2 = jnp.concatenate(ordered(xh, table[:1], came[448:449]), axis=0).astype(jnp.int32)
    lengths, owners = table2[:, :32], table2[:, 32:64]
    starts = jnp.cumsum(lengths, axis=1) - lengths
    places = jnp.arange(448, dtype=jnp.int32)
    inside = (places[None, None, :] >= starts[:, :, None]) & (
        places[None, None, :] < (starts + lengths)[:, :, None]
    )
    slot = jnp.arange(32, dtype=jnp.int32)
    slot = (slot % 16) * 2 + slot // 16
    select = (owners[:, None, :] == slot[None, :, None]).astype(bf16)
    member = jnp.einsum("bdi,bit->bdt", select, inside.astype(bf16), preferred_element_type=f32)
    empty = jnp.zeros((32, 448), f32)
    pool = jnp.stack(
        [
            jnp.concatenate([member[0], empty], axis=1),
            jnp.concatenate([empty, member[1]], axis=1),
        ],
        axis=1,
    ).reshape(64, 896)
    count = jnp.sum(pool, axis=1, keepdims=True)
    pool = pool.astype(bf16)

    piece = lax.dynamic_slice_in_dim(student_emb, 2 * rank, 2, axis=0)
    along = share(piece, "z", 16).reshape(32, 1024)
    plane = share(along, CHIPS, 16)
    even, odd = ordered(core, plane, swap(plane, "core"))
    emb = jnp.stack([even.reshape(4, 128, 1024), odd.reshape(4, 128, 1024)], axis=1).reshape(
        1024, 1024
    )
    u = jnp.dot(emb, proj_weight, preferred_element_type=f32)
    sum_uu = jnp.sum(share(jnp.sum(u * u, axis=1).reshape(8, 128), ROW, 16), axis=0).reshape(1024)
    scale_u = (1.0 / (root * jnp.sqrt(sum_uu / D + 1e-06)))[:, None]
    uhat = u * scale_u
    uhat_b = uhat.astype(bf16)
    uhat_own = jnp.where(low, uhat[:, :128], uhat[:, 128:])
    uhat_own_b = uhat_own.astype(bf16)
    gain = lax.dynamic_slice_in_dim(norm_gain, rank * 256 + xh * 128, 128)

    part_theirs = swap(parts_for(1 - core, hidden2, weight), "core")
    part_mine = parts_for(core, hidden2, weight)
    pair = (part_mine.astype(f32) + part_theirs.astype(f32)).astype(bf16)
    y = jnp.sum(exchange(pair, HALF).astype(f32), axis=0) + residual2.astype(f32)

    squares = jnp.sum(y * y, axis=1).reshape(7, 128)
    squares = jnp.sum(share(squares, PLANE, 32), axis=0).reshape(896)
    normed = (y * lax.rsqrt(squares / D + 1e-05)[:, None] * gain).astype(bf16)
    pooled = (jnp.dot(pool, normed, preferred_element_type=f32) / count).astype(bf16)

    tch = pooled.astype(f32)
    facing = lax.dynamic_slice_in_dim(uhat_own, z * 64, 64, axis=0)
    sums = jnp.concatenate([jnp.sum(tch * tch, axis=1), jnp.sum(tch * facing, axis=1)])
    sums = jnp.sum(share(sums.reshape(1, 128), PLANE, 32), axis=0).reshape(128)
    scale_t = 1.0 / (root * jnp.sqrt(sums[:64] / D + 1e-06))
    cosv = sums[64:] * scale_t
    cos_hi = cosv.astype(bf16)
    cos_lo = (cosv - cos_hi.astype(f32)).astype(bf16)
    that_b = (tch * scale_t[:, None]).astype(bf16)
    extra = jnp.pad(jnp.concatenate([cos_hi, cos_lo])[None], ((0, 15), (0, 0)))
    gathered = share(jnp.concatenate([that_b, extra], axis=0), "z", 16)
    teach = gathered[:, :64].reshape(1024, 128)
    cos_sum = jnp.sum(gathered[:, 64:65].astype(f32))
    teach2 = jnp.concatenate(ordered(xh, teach, swap(teach, "xh")), axis=1)

    lhs = jnp.concatenate([uhat_own_b, teach], axis=1)
    rhs = jnp.concatenate([uhat_own_b, -teach], axis=1)

    def rows_of(which):
        return lax.dot_general(
            lax.dynamic_slice_in_dim(lhs, which * 512, 512, axis=0),
            rhs,
            NT,
            preferred_element_type=f32,
        )

    diff_theirs = swap(rows_of(1 - core).astype(bf16), "core")
    diff_half = (rows_of(core) + diff_theirs.astype(f32)).astype(bf16)
    diff_rows = jnp.sum(exchange(diff_half.reshape(16, 32, 1024), CHIPS).astype(f32), axis=0)
    diff_own = share(diff_rows.astype(bf16), CHIPS, 16).reshape(512, 1024)
    diff_b = jnp.concatenate(ordered(core, diff_own, swap(diff_own, "core")), axis=0)
    diff_f = diff_b.astype(f32)
    loss = 1.0 - cos_sum / 1024 + jnp.sum(diff_f * diff_f) / 1024

    grad_hat = grad_scale * (
        -teach2.astype(f32) / 1024
        + 4.0 / 1024 * jnp.dot(diff_b, uhat_b, preferred_element_type=f32)
    )
    inner = jnp.sum(grad_hat * uhat, axis=1).reshape(8, 128)
    inner = jnp.sum(share(inner, ROW, 16), axis=0).reshape(1024, 1)
    du = ((grad_hat - uhat * inner) * scale_u).astype(bf16)
    grad_proj = lax.dot_general(emb, du, TN, preferred_element_type=f32)
    du_rows = lax.dynamic_index_in_dim(
        du.reshape(16, 32, 2, 256), xh * 16 + z, axis=1, keepdims=False
    ).reshape(32, 256)
    student = lax.dot_general(du_rows, proj_weight, NT, preferred_element_type=f32)
    student = student.astype(bf16)
    student = (student.astype(f32) + swap(student, "core").astype(f32)).astype(bf16)
    grad_student = jnp.sum(share(student, HALF, 8).astype(f32), axis=0)
    return (grad_proj, grad_student, loss)


def solution(mesh):
    fine = Mesh(mesh.devices.reshape(4, 2, 16, 2, 2), ("y", "core", "z", "xh", "xl"))
    dp = ("z", "xh")
    placed = (
        P(dp, ROW),
        P(dp, ROW),
        P(ROW, dp),
        P(),
        P(dp, None),
        P(dp, None),
        P(dp, None),
        P(None, ROW),
    )
    return jax.shard_map(
        on_device,
        mesh=fine,
        in_specs=placed,
        out_specs=(P(None, ROW), P(dp, None), P()),
        check_vma=False,
    )
```

time: 1160 us -> 321 us (0.28)
  waiting for transfers between devices: 827 us -> 79.6 us
  blocking collectives: 276 us -> 94.9 us
  starting transfers between devices: 14.7 us -> 76.4 us
  other arithmetic: 4.54 us -> 17.7 us
    psum x3 -> x0, waiting for transfers between devices: 519 us -> none  [the longest x2 300 us: feature_sum(): return lax.psum(values, ('section', 'grp'))]
    all_gather x1, waiting for transfers between devices: 199 us -> 19.9 us  [on_device(): weight = lax.all_gather(down_weight, 'z', axis=0)]
    psum x4 -> x0, blocking collectives: 153 us -> none  [the longest x3 87.1 us: feature_sum(): return lax.psum(values, ('section', 'grp'))]
    all_gather x2 -> x0, blocking collectives: 123 us -> none  [the longest x1 62.2 us: on_device(): lax.all_gather(that_b, 'dp', axis=0, tiled=True)]
    all_to_all x0 -> x5, blocking collectives: none -> 94.9 us  [exchange(): return lax.all_to_all(value, axes, split_axis=0, concat_axis=0)]
    reduce_scatter x1 -> x0, waiting for transfers between devices: 94.9 us -> none  [on_device(): lax.psum_scatter(partial_value.astype(jnp.bfloat16), ('section', 'grp'),...]
    ppermute x0 -> x8, starting transfers between devices: none -> 46.7 us  [swap(): return lax.ppermute(value, axis, [(0, 1), (1, 0)])]
    all_to_all x1 -> x6, waiting for transfers between devices: 13.1 us -> 44.1 us  [exchange(): return lax.all_to_all(value, axes, split_axis=0, concat_axis=0)]
  transfers between devices with their start and end apart: 6 -> 15, of which waited for: 6 -> 11; matrix products, arithmetic and copies ran while one was open for 1% -> 7% of each run, Pallas kernels for 0% -> 2%
where the time goes in v1:
time: 321 us; the launch traced here: 319 us
  blocking collectives  94.9 us (30%)
  waiting for transfers between devices  79.6 us (25%)
  starting transfers between devices  76.4 us (24%)
  other arithmetic  17.7 us (6%)
  local copies, waits for them, and re-layouts  17.5 us (5%)
  between operations  17 us (5%)
  matrix products  10.1 us (3%)
  Pallas kernels  6.2 us (2%)
    all_to_all x5, blocking collectives, exchange(): return lax.all_to_all(value, axes, split_axis=0, concat_axis=0)  94.9 us
    ppermute x8, starting transfers between devices, swap(): return lax.ppermute(value, axis, [(0, 1), (1, 0)])  46.7 us
    all_to_all x6, waiting for transfers between devices, exchange(): return lax.all_to_all(value, axes, split_axis=0, concat_axis=0)  44.1 us
    all_to_all x6, starting transfers between devices, exchange(): return lax.all_to_all(value, axes, split_axis=0, concat_axis=0)  29.6 us
    all_gather x1, waiting for transfers between devices, on_device(): weight = lax.all_gather(down_weight, 'z', axis=0)  19.9 us
    ppermute x8, waiting for transfers between devices, swap(): return lax.ppermute(value, axis, [(0, 1), (1, 0)])  14.9 us
    unnamed x40, local copies, waits for them, and re-layouts  7.46 us
  transfers between devices with their start and end apart: 15, of which 11 were waited for; matrix products, arithmetic and copies ran while one was open for 7% of the time, Pallas kernels for 2%

profile of v1, /device:TPU:1, one launch (start us, length us, event | category | flops | bytes accessed | tf_op | source)
XLA Modules:
  0.0 319.4 jit_solution(6127344759071526992)
XLA Ops:
  7.9 5.5 %collective-permute-start.2 = (bf16[448,896]{1,0:T(8,128)(2,1)}, bf16[448,896]{1,0:T(8,128)(2,1)S(1)}, u32[]{:S(2)}, u32[]{:S(2)}) collective-permute-start(bf16[448,896]{1,0:T(8,128)(2,1)} %param.8), channel_id=1, source_target_pairs={{0,2},{2,0},{1,3},{3,1},{4,6},{6,4},{5,7},{7,5},{8,10},{10,8},{9,1... | collective-permute-start | bytes 2408456 | tf_op jit(solution)/shard_map/ppermute | solution.py:21
  14.2 26.3 %all_to_all.55 = bf16[16,2,1024]{2,1,0:T(2,128)(2,1)S(1)} all-to-all(bf16[16,2,1024]{2,1,0:T(2,128)(2,1)S(1)} %broadcast_in_dim.28), channel_id=1, replica_groups=mesh['y'=4,'core'=2,'z'=16,'xh'=2,'xl'=2] {'z'}, dimensions={0} | all-to-all | bytes 131072 | tf_op jit(solution)/shard_map/all_to_all | solution.py:25
  40.6 1.1 broadcast_in_dim.30
  41.7 4.9 %all-to-all-start.1 = ((bf16[16,32,1024]{2,1,0:T(8,128)(2,1)}), bf16[16,32,1024]{2,1,0:T(8,128)(2,1)S(1)}, u32[]{:S(2)}, u32[]{:S(2)}) async-start(bf16[16,32,1024]{2,1,0:T(8,128)(2,1)} %broadcast_in_dim.30), calls=%async_computation.1 | async-start | bytes 2097152 | tf_op jit(solution)/shard_map/all_to_all | solution.py:25
  46.9 12.7 %all-to-all-done.1 = bf16[16,32,1024]{2,1,0:T(8,128)(2,1)S(1)} async-done(((bf16[16,32,1024]{2,1,0:T(8,128)(2,1)}), bf16[16,32,1024]{2,1,0:T(8,128)(2,1)S(1)}, u32[]{:S(2)}, u32[]{:S(2)}) %all-to-all-start.1) | async-done | bytes 1048608 | tf_op jit(solution)/shard_map/all_to_all | solution.py:25
  59.6 6.0 %collective-permute-start = (bf16[16,32,1024]{2,1,0:T(8,128)(2,1)S(1)}, bf16[16,32,1024]{2,1,0:T(8,128)(2,1)}, u32[]{:S(2)}, u32[]{:S(2)}) collective-permute-start(bf16[16,32,1024]{2,1,0:T(8,128)(2,1)S(1)} %all-to-all-done.1), channel_id=1, source_target_pairs={{0,64},{64,0},{1,65},{65,1},{2,66},{66,2},{3,67},{67,3},{4,68},{68... | collective-permute-start | bytes 3145736 | tf_op jit(solution)/shard_map/ppermute | solution.py:21
  65.6 19.9 %all-gather.3.cloned.1.call-done = bf16[14336,128]{1,0:T(8,128)(2,1)} async-done(((bf16[896,128]{1,0:T(8,128)(2,1)}), bf16[14336,128]{1,0:T(8,128)(2,1)}) %all-gather.3.cloned.1.call-update) | async-done | bytes 3670032 | tf_op jit(solution)/shard_map/all_gather | solution.py:73
  85.5 2.0 copy-done.1
  87.6 3.6 %shard_map.104 = bf16[8,896,128]{2,1,0:T(8,128)(2,1)} custom-call(s32[1]{0:T(128)} %bitcast.9.core_ref, bf16[896,896]{1,0:T(8,128)(2,1)S(1)} %pad_maximum_fusion.2.hidden_ref, bf16[16,896,128]{2,1,0:T(8,128)(2,1)S(1)} %bitcast.51), custom_call_target="tpu_custom_call" | custom-call | flops 1644167168 | bytes 5000000 | tf_op jit(solution)/shard_map/pallas_call | solution.py:46
  91.1 10.6 %collective-permute-start.3 = (bf16[8,896,128]{2,1,0:T(8,128)(2,1)}, bf16[8,896,128]{2,1,0:T(8,128)(2,1)}, u32[]{:S(2)}, u32[]{:S(2)}) collective-permute-start(bf16[8,896,128]{2,1,0:T(8,128)(2,1)} %shard_map.104), channel_id=1, source_target_pairs={{0,64},{64,0},{1,65},{65,1},{2,66},{66,2},{3,67},{67,3},{4,68},{68... | collective-permute-start | bytes 5505032 | tf_op jit(solution)/shard_map/ppermute | solution.py:21
  101.8 4.2 %collective-permute-start.1 = (bf16[464,128]{1,0:T(8,128)(2,1)S(1)}, bf16[464,128]{1,0:T(8,128)(2,1)S(1)}, u32[]{:S(2)}, u32[]{:S(2)}) collective-permute-start(bf16[464,128]{1,0:T(8,128)(2,1)S(1)} %pad_maximum_fusion.12), channel_id=1, source_target_pairs={{0,2},{2,0},{1,3},{3,1},{4,6},{6,4},{5,7},{7,5},{8,10},{10,8},{9,1... | collective-permute-start | bytes 356360 | tf_op jit(solution)/shard_map/ppermute | solution.py:21
  106.9 3.2 %collective-permute-done.1 = bf16[464,128]{1,0:T(8,128)(2,1)S(1)} collective-permute-done((bf16[464,128]{1,0:T(8,128)(2,1)S(1)}, bf16[464,128]{1,0:T(8,128)(2,1)S(1)}, u32[]{:S(2)}, u32[]{:S(2)}) %collective-permute-start.1) | collective-permute-done | bytes 118816 | tf_op jit(solution)/shard_map/ppermute | solution.py:21
  110.3 1.4 broadcast_select_fusion.3
  111.9 1.3 copy-done.6
  114.7 5.6 %all-to-all-start.4 = ((f32[16,8,128]{2,1,0:T(8,128)}), f32[16,8,128]{2,1,0:T(8,128)S(1)}, u32[]{:S(2)}, u32[]{:S(2)}) async-start(f32[16,8,128]{2,1,0:T(8,128)} %broadcast_in_dim.34), calls=%async_computation.4 | async-start | bytes 131072 | tf_op jit(solution)/shard_map/all_to_all | solution.py:25
  120.3 2.0 copy-done.2
  122.4 2.6 shard_map.103
  125.0 3.2 %add_convert_fusion = bf16[8,896,128]{2,1,0:T(8,128)(2,1)} fusion(bf16[8,896,128]{2,1,0:T(8,128)(2,1)} %collective-permute-done.3, bf16[8,896,128]{2,1,0:T(8,128)(2,1)S(1)} %shard_map.103), kind=kLoop, calls=%fused_computation.2 | loop fusion | flops 3670016 | bytes 5505024 | tf_op jit(solution)/shard_map/convert_element_type | solution.py:123
  128.8 5.1 %all-to-all-start.2 = ((bf16[8,896,128]{2,1,0:T(8,128)(2,1)}), bf16[8,896,128]{2,1,0:T(8,128)(2,1)S(1)}, u32[]{:S(2)}, u32[]{:S(2)}) async-start(bf16[8,896,128]{2,1,0:T(8,128)(2,1)} %add_convert_fusion), calls=%async_computation.2 | async-start | bytes 3670016 | tf_op jit(solution)/shard_map/all_to_all | solution.py:25
  135.7 1.6 convert_element_type.106
  137.3 1.0 fusion.12
  138.5 1.7 broadcast_select_fusion.9
  141.1 1.2 broadcast_multiply_fusion
  142.2 15.3 %all-to-all-done.2 = bf16[8,896,128]{2,1,0:T(8,128)(2,1)S(1)} async-done(((bf16[8,896,128]{2,1,0:T(8,128)(2,1)}), bf16[8,896,128]{2,1,0:T(8,128)(2,1)S(1)}, u32[]{:S(2)}, u32[]{:S(2)}) %all-to-all-start.2) | async-done | bytes 1835040 | tf_op jit(solution)/shard_map/all_to_all | solution.py:25
  159.4 6.3 %all-to-all-start.3 = ((f32[32,7,128]{2,1,0:T(8,128)}), f32[32,7,128]{2,1,0:T(8,128)S(1)}, u32[]{:S(2)}, u32[]{:S(2)}) async-start(f32[32,7,128]{2,1,0:T(8,128)} %broadcast_in_dim.32), calls=%async_computation.3 | async-start | bytes 262144 | tf_op jit(solution)/shard_map/all_to_all | solution.py:25
  165.8 7.5 %all-to-all-done.3 = f32[32,7,128]{2,1,0:T(8,128)S(1)} async-done(((f32[32,7,128]{2,1,0:T(8,128)}), f32[32,7,128]{2,1,0:T(8,128)S(1)}, u32[]{:S(2)}, u32[]{:S(2)}) %all-to-all-start.3) | async-done | bytes 114720 | tf_op jit(solution)/shard_map/all_to_all | solution.py:25
  174.0 10.8 %all_to_all.56 = f32[32,1,128]{2,1,0:T(1,128)S(1)} all-to-all(f32[32,1,128]{2,1,0:T(1,128)S(1)} %broadcast_in_dim.35), channel_id=1, replica_groups=mesh['y'=4,'core'=2,'z'=16,'xh'=2,'xl'=2] {'y','core','xh','xl'}, dimensions={0} | all-to-all | bytes 32768 | tf_op jit(solution)/shard_map/all_to_all | solution.py:25
  185.1 22.3 %all_to_all.57 = bf16[16,80,128]{2,1,0:T(8,128)(2,1)S(1)} all-to-all(bf16[16,80,128]{2,1,0:T(8,128)(2,1)S(1)} %broadcast_in_dim.37), channel_id=1, replica_groups=mesh['y'=4,'core'=2,'z'=16,'xh'=2,'xl'=2] {'z'}, dimensions={0} | all-to-all | bytes 655360 | tf_op jit(solution)/shard_map/all_to_all | solution.py:25
  207.4 2.7 collective-permute-start.4
  210.2 5.9 %collective-permute-done.4 = bf16[1024,128]{1,0:T(8,128)(2,1)S(1)} collective-permute-done((bf16[1024,128]{1,0:T(8,128)(2,1)S(1)}, bf16[1024,128]{1,0:T(8,128)(2,1)S(1)}, u32[]{:S(2)}, u32[]{:S(2)}) %collective-permute-start.4) | collective-permute-done | bytes 262176 | tf_op jit(solution)/shard_map/ppermute | solution.py:21
  216.2 1.5 convolution_convert_fusion
  217.7 9.6 %collective-permute-start.5 = (bf16[512,1024]{1,0:T(8,128)(2,1)}, bf16[512,1024]{1,0:T(8,128)(2,1)}, u32[]{:S(2)}, u32[]{:S(2)}) collective-permute-start(bf16[512,1024]{1,0:T(8,128)(2,1)} %convolution_convert_fusion), channel_id=1, source_target_pairs={{0,64},{64,0},{1,65},{65,1},{2,66},{66,2},{3,67},{67,3},{4,68},{68... | collective-permute-start | bytes 3145736 | tf_op jit(solution)/shard_map/ppermute | solution.py:21
  227.3 2.6 collective-permute-done.5
  229.9 1.8 add_convert_fusion.1
  231.7 17.7 %all_to_all.58 = bf16[16,32,1024]{2,1,0:T(8,128)(2,1)S(1)} all-to-all(bf16[16,32,1024]{2,1,0:T(8,128)(2,1)S(1)} %bitcast.61), channel_id=1, replica_groups=mesh['y'=4,'core'=2,'z'=16,'xh'=2,'xl'=2] {'y','xl','xh'}, dimensions={0} | all-to-all | bytes 2097152 | tf_op jit(solution)/shard_map/all_to_all | solution.py:25
  249.7 17.8 %all_to_all.59 = bf16[16,32,1024]{2,1,0:T(8,128)(2,1)S(1)} all-to-all(bf16[16,32,1024]{2,1,0:T(8,128)(2,1)S(1)} %broadcast_in_dim.38), channel_id=1, replica_groups=mesh['y'=4,'core'=2,'z'=16,'xh'=2,'xl'=2] {'y','xl','xh'}, dimensions={0} | all-to-all | bytes 2097152 | tf_op jit(solution)/shard_map/all_to_all | solution.py:25
  267.6 5.8 %collective-permute-start.6 = (bf16[512,1024]{1,0:T(8,128)(2,1)S(1)}, bf16[512,1024]{1,0:T(8,128)(2,1)S(1)}, u32[]{:S(2)}, u32[]{:S(2)}) collective-permute-start(bf16[512,1024]{1,0:T(8,128)(2,1)S(1)} %bitcast.53), channel_id=1, source_target_pairs={{0,64},{64,0},{1,65},{65,1},{2,66},{66,2},{3,67},{67,3},{4,68},{68... | collective-permute-start | bytes 3145736 | tf_op jit(solution)/shard_map/ppermute | solution.py:21
  273.4 2.3 collective-permute-done.6
  275.9 1.8 multiply_reduce_fusion.1
  278.3 3.7 %all-to-all-start.9 = ((f32[16,8,128]{2,1,0:T(8,128)}), f32[16,8,128]{2,1,0:T(8,128)S(1)}, u32[]{:S(2)}, u32[]{:S(2)}) async-start(f32[16,8,128]{2,1,0:T(8,128)} %broadcast_in_dim.40), calls=%async_computation.9 | async-start | bytes 131072 | tf_op jit(solution)/shard_map/all_to_all | solution.py:25
  281.9 6.0 %all-to-all-done.9 = f32[16,8,128]{2,1,0:T(8,128)S(1)} async-done(((f32[16,8,128]{2,1,0:T(8,128)}), f32[16,8,128]{2,1,0:T(8,128)S(1)}, u32[]{:S(2)}, u32[]{:S(2)}) %all-to-all-start.9) | async-done | bytes 65568 | tf_op jit(solution)/shard_map/all_to_all | solution.py:25
  288.0 1.9 multiply_convert_fusion
  291.8 2.3 collective-permute-start.7
  295.9 4.1 %all-to-all-start.10 = ((bf16[8,32,1024]{2,1,0:T(8,128)(2,1)}), bf16[8,32,1024]{2,1,0:T(8,128)(2,1)}, u32[]{:S(2)}, u32[]{:S(2)}) async-start(bf16[8,32,1024]{2,1,0:T(8,128)(2,1)} %broadcast_in_dim.41), calls=%async_computation.10 | async-start | bytes 1048576 | tf_op jit(solution)/shard_map/all_to_all | solution.py:25
  301.3 1.7 multiply_reduce_fusion
  303.7 3.3 %fusion.42 = f32[1024,256]{1,0:T(8,128)} fusion(bf16[1024,1024]{1,0:T(8,128)(2,1)} %bitcast.57, bf16[1024,256]{1,0:T(8,128)(2,1)S(1)} %multiply_convert_fusion), kind=kOutput, calls=%fused_computation.112 | convolution fusion | flops 536870912 | bytes 3670016 | tf_op jit(solution)/shard_map/dot_general | solution.py:172
  307.0 2.7 all-to-all-done.10
  309.6 1.8 convert_reduce_fusion.1
  (102 shorter events, 16.6 us)
Async XLA Ops:
  7.2 106.1 %copy-start = (bf16[1024,256]{1,0:T(8,128)(2,1)S(1)}, bf16[1024,256]{1,0:T(8,128)(2,1)}, u32[]{:S(2)}) copy-start(bf16[1024,256]{1,0:T(8,128)(2,1)} %param.15) | copy-start | bytes 1572868
  7.2 39.4 %copy-start.11 = (bf16[448,896]{1,0:T(8,128)(2,1)S(1)}, bf16[448,896]{1,0:T(8,128)(2,1)}, u32[]{:S(2)}) copy-start(bf16[448,896]{1,0:T(8,128)(2,1)} %param.8) | copy-start | bytes 2408452
  7.2 39.4 %copy-start.18 = (s32[1,32]{1,0:T(1,128)S(1)}, s32[1,32]{1,0:T(1,128)}, u32[]{:S(2)}) copy-start(s32[1,32]{1,0:T(1,128)} %param.12) | copy-start | bytes 388
  7.2 39.4 %copy-start.19 = (s32[1,32]{1,0:T(1,128)S(1)}, s32[1,32]{1,0:T(1,128)}, u32[]{:S(2)}) copy-start(s32[1,32]{1,0:T(1,128)} %param.13) | copy-start | bytes 388
  7.2 78.3 %all-gather.3.cloned.1.call-start = ((), (), s32[]{:S(2)}) async-start(), calls=%async_computation.11 | async-start | bytes 3899392 | tf_op jit(solution)/shard_map/all_gather | solution.py:73
  7.9 38.7 %collective-permute-start.2 = (bf16[448,896]{1,0:T(8,128)(2,1)}, bf16[448,896]{1,0:T(8,128)(2,1)S(1)}, u32[]{:S(2)}, u32[]{:S(2)}) collective-permute-start(bf16[448,896]{1,0:T(8,128)(2,1)} %param.8), channel_id=1, source_target_pairs={{0,2},{2,0},{1,3},{3,1},{4,6},{6,4},{5,7},{7,5},{8,10},{10,8},{9,1... | collective-permute-start | bytes 2408456 | tf_op jit(solution)/shard_map/ppermute | solution.py:21
  41.7 17.9 %all-to-all-start.1 = ((bf16[16,32,1024]{2,1,0:T(8,128)(2,1)}), bf16[16,32,1024]{2,1,0:T(8,128)(2,1)S(1)}, u32[]{:S(2)}, u32[]{:S(2)}) async-start(bf16[16,32,1024]{2,1,0:T(8,128)(2,1)} %broadcast_in_dim.30), calls=%async_computation.1 | async-start | bytes 2097152 | tf_op jit(solution)/shard_map/all_to_all | solution.py:25
  59.6 50.7 %collective-permute-start = (bf16[16,32,1024]{2,1,0:T(8,128)(2,1)S(1)}, bf16[16,32,1024]{2,1,0:T(8,128)(2,1)}, u32[]{:S(2)}, u32[]{:S(2)}) collective-permute-start(bf16[16,32,1024]{2,1,0:T(8,128)(2,1)S(1)} %all-to-all-done.1), channel_id=1, source_target_pairs={{0,64},{64,0},{1,65},{65,1},{2,66},{66,2},{3,67},{67,3},{4,68},{68... | collective-permute-start | bytes 3145736 | tf_op jit(solution)/shard_map/ppermute | solution.py:21
  85.5 2.0 copy-start.1
  87.5 14.2 %copy-start.10 = (bf16[448,256]{1,0:T(8,128)(2,1)S(1)}, bf16[448,256]{1,0:T(8,128)(2,1)}, u32[]{:S(2)}) copy-start(bf16[448,256]{1,0:T(8,128)(2,1)} %param.9) | copy-start | bytes 688132
  91.1 33.9 %collective-permute-start.3 = (bf16[8,896,128]{2,1,0:T(8,128)(2,1)}, bf16[8,896,128]{2,1,0:T(8,128)(2,1)}, u32[]{:S(2)}, u32[]{:S(2)}) collective-permute-start(bf16[8,896,128]{2,1,0:T(8,128)(2,1)} %shard_map.104), channel_id=1, source_target_pairs={{0,64},{64,0},{1,65},{65,1},{2,66},{66,2},{3,67},{67,3},{4,68},{68... | collective-permute-start | bytes 5505032 | tf_op jit(solution)/shard_map/ppermute | solution.py:21
  101.8 8.3 %collective-permute-start.1 = (bf16[464,128]{1,0:T(8,128)(2,1)S(1)}, bf16[464,128]{1,0:T(8,128)(2,1)S(1)}, u32[]{:S(2)}, u32[]{:S(2)}) collective-permute-start(bf16[464,128]{1,0:T(8,128)(2,1)S(1)} %pad_maximum_fusion.12), channel_id=1, source_target_pairs={{0,2},{2,0},{1,3},{3,1},{4,6},{6,4},{5,7},{7,5},{8,10},{10,8},{9,1... | collective-permute-start | bytes 356360 | tf_op jit(solution)/shard_map/ppermute | solution.py:21
  110.1 1.6 copy-start.17
  111.9 1.3 copy-start.6
  114.0 27.0 %copy-start.3 = (f32[1024,256]{1,0:T(8,128)}, f32[1024,256]{1,0:T(8,128)S(1)}, u32[]{:S(2)}) copy-start(f32[1024,256]{1,0:T(8,128)S(1)} %get-tuple-element.27) | copy-start | bytes 3145732
  114.7 13.5 %all-to-all-start.4 = ((f32[16,8,128]{2,1,0:T(8,128)}), f32[16,8,128]{2,1,0:T(8,128)S(1)}, u32[]{:S(2)}, u32[]{:S(2)}) async-start(f32[16,8,128]{2,1,0:T(8,128)} %broadcast_in_dim.34), calls=%async_computation.4 | async-start | bytes 131072 | tf_op jit(solution)/shard_map/all_to_all | solution.py:25
  120.3 2.0 copy-start.2
  128.2 0.6 copy-start.14
  128.8 28.7 %all-to-all-start.2 = ((bf16[8,896,128]{2,1,0:T(8,128)(2,1)}), bf16[8,896,128]{2,1,0:T(8,128)(2,1)S(1)}, u32[]{:S(2)}, u32[]{:S(2)}) async-start(bf16[8,896,128]{2,1,0:T(8,128)(2,1)} %add_convert_fusion), calls=%async_computation.2 | async-start | bytes 3670016 | tf_op jit(solution)/shard_map/all_to_all | solution.py:25
  134.3 0.6 copy-start.9
  142.2 23.5 %copy-start.4 = (f32[1024,256]{1,0:T(8,128)S(1)}, f32[1024,256]{1,0:T(8,128)}, u32[]{:S(2)}) copy-start(f32[1024,256]{1,0:T(8,128)} %broadcast_multiply_fusion) | copy-start | bytes 3145732
  157.5 1.0 copy-start.12
  157.8 0.8 copy-start.7
  157.8 15.6 %copy-start.13 = (bf16[448,128]{1,0:T(8,128)(2,1)S(1)}, bf16[448,128]{1,0:T(8,128)(2,1)}, u32[]{:S(2)}) copy-start(bf16[448,128]{1,0:T(8,128)(2,1)} %get-tuple-element.18) | copy-start | bytes 344068
  157.8 15.6 %copy-start.16 = (bf16[64,896]{1,0:T(8,128)(2,1)S(1)}, bf16[64,896]{1,0:T(8,128)(2,1)}, u32[]{:S(2)}) copy-start(bf16[64,896]{1,0:T(8,128)(2,1)} %convert_element_type.106) | copy-start | bytes 344068
  158.8 14.6 %copy-start.8 = (f32[896,128]{1,0:T(8,128)S(1)}, f32[896,128]{1,0:T(8,128)}, u32[]{:S(2)}) copy-start(f32[896,128]{1,0:T(8,128)} %copy-done.7) | copy-start | bytes 1376260
  159.4 13.9 %all-to-all-start.3 = ((f32[32,7,128]{2,1,0:T(8,128)}), f32[32,7,128]{2,1,0:T(8,128)S(1)}, u32[]{:S(2)}, u32[]{:S(2)}) async-start(f32[32,7,128]{2,1,0:T(8,128)} %broadcast_in_dim.32), calls=%async_computation.3 | async-start | bytes 262144 | tf_op jit(solution)/shard_map/all_to_all | solution.py:25
  165.8 51.8 %copy-start.15 = (bf16[1024,128]{1,0:T(8,128)(2,1)}, bf16[1024,128]{1,0:T(8,128)(2,1)S(1)}, u32[]{:S(2)}) copy-start(bf16[1024,128]{1,0:T(8,128)(2,1)S(1)} %get-tuple-element.7) | copy-start | bytes 786436
  207.4 8.6 %collective-permute-start.4 = (bf16[1024,128]{1,0:T(8,128)(2,1)S(1)}, bf16[1024,128]{1,0:T(8,128)(2,1)S(1)}, u32[]{:S(2)}, u32[]{:S(2)}) collective-permute-start(bf16[1024,128]{1,0:T(8,128)(2,1)S(1)} %bitcast.58), channel_id=1, source_target_pairs={{0,2},{2,0},{1,3},{3,1},{4,6},{6,4},{5,7},{7,5},{8,10},{10,8},{9,1... | collective-permute-start | bytes 786440 | tf_op jit(solution)/shard_map/ppermute | solution.py:21
  217.7 12.2 %collective-permute-start.5 = (bf16[512,1024]{1,0:T(8,128)(2,1)}, bf16[512,1024]{1,0:T(8,128)(2,1)}, u32[]{:S(2)}, u32[]{:S(2)}) collective-permute-start(bf16[512,1024]{1,0:T(8,128)(2,1)} %convolution_convert_fusion), channel_id=1, source_target_pairs={{0,64},{64,0},{1,65},{65,1},{2,66},{66,2},{3,67},{67,3},{4,68},{68... | collective-permute-start | bytes 3145736 | tf_op jit(solution)/shard_map/ppermute | solution.py:21
  267.6 8.3 %copy-start.5 = (f32[1024,256]{1,0:T(8,128)S(1)}, f32[1024,256]{1,0:T(8,128)}, u32[]{:S(2)}) copy-start(f32[1024,256]{1,0:T(8,128)} %broadcast_multiply_fusion) | copy-start | bytes 3145732
  267.6 8.1 %collective-permute-start.6 = (bf16[512,1024]{1,0:T(8,128)(2,1)S(1)}, bf16[512,1024]{1,0:T(8,128)(2,1)S(1)}, u32[]{:S(2)}, u32[]{:S(2)}) collective-permute-start(bf16[512,1024]{1,0:T(8,128)(2,1)S(1)} %bitcast.53), channel_id=1, source_target_pairs={{0,64},{64,0},{1,65},{65,1},{2,66},{66,2},{3,67},{67,3},{4,68},{68... | collective-permute-start | bytes 3145736 | tf_op jit(solution)/shard_map/ppermute | solution.py:21
  278.3 9.7 %all-to-all-start.9 = ((f32[16,8,128]{2,1,0:T(8,128)}), f32[16,8,128]{2,1,0:T(8,128)S(1)}, u32[]{:S(2)}, u32[]{:S(2)}) async-start(f32[16,8,128]{2,1,0:T(8,128)} %broadcast_in_dim.40), calls=%async_computation.9 | async-start | bytes 131072 | tf_op jit(solution)/shard_map/all_to_all | solution.py:25
  291.8 3.2 %collective-permute-start.7 = (bf16[32,1024]{1,0:T(8,128)(2,1)S(1)}, bf16[32,1024]{1,0:T(8,128)(2,1)S(1)}, u32[]{:S(2)}, u32[]{:S(2)}) collective-permute-start(bf16[32,1024]{1,0:T(8,128)(2,1)S(1)} %convolution_convert_fusion.1), channel_id=1, source_target_pairs={{0,64},{64,0},{1,65},{65,1},{2,66},{66,2},{3,67},{67,3},{4,68},{68... | collective-permute-start | bytes 196616 | tf_op jit(solution)/shard_map/ppermute | solution.py:21
  295.9 13.7 %all-to-all-start.10 = ((bf16[8,32,1024]{2,1,0:T(8,128)(2,1)}), bf16[8,32,1024]{2,1,0:T(8,128)(2,1)}, u32[]{:S(2)}, u32[]{:S(2)}) async-start(bf16[8,32,1024]{2,1,0:T(8,128)(2,1)} %broadcast_in_dim.41), calls=%async_computation.10 | async-start | bytes 1048576 | tf_op jit(solution)/shard_map/all_to_all | solution.py:25
Sparse Core Ops, SparseCore 0:
  10.1 75.3 all-gather.2

commit v2 on v1

--- a/solution.py
+++ b/solution.py
@@ -27,6 +27,11 @@
 
 def share(value, axes, count):
     return exchange(jnp.broadcast_to(value[None], (count,) + value.shape), axes)
+
+
+def two_parts(value):
+    high = lax.reduce_precision(value, 8, 7)
+    return high.astype(bf16), (value - high).astype(bf16)
 
 
 def ordered(index, own, other):
@@ -71,8 +76,6 @@
     low = xh == 0
 
     weight = lax.all_gather(down_weight, "z", axis=0)
-    hidden2 = jnp.concatenate(ordered(xh, hidden, swap(hidden, "xh")), axis=0)
-
     left, right = residual[:, :128], residual[:, 128:]
     mine, theirs = jnp.where(low, left, right), jnp.where(low, right, left)
     table = jnp.pad(
@@ -104,6 +107,10 @@
 
     piece = lax.dynamic_slice_in_dim(student_emb, 2 * rank, 2, axis=0)
     along = share(piece, "z", 16).reshape(32, 1024)
+    along, hidden, pool, count, residual2 = lax.optimization_barrier(
+        (along, hidden, pool, count, residual2)
+    )
+    hidden2 = jnp.concatenate(ordered(xh, hidden, swap(hidden, "xh")), axis=0)
     plane = share(along, CHIPS, 16)
     even, odd = ordered(core, plane, swap(plane, "core"))
     emb = jnp.stack([even.reshape(4, 128, 1024), odd.reshape(4, 128, 1024)], axis=1).reshape(
@@ -111,12 +118,26 @@
     )
     u = jnp.dot(emb, proj_weight, preferred_element_type=f32)
     sum_uu = jnp.sum(share(jnp.sum(u * u, axis=1).reshape(8, 128), ROW, 16), axis=0).reshape(1024)
-    scale_u = (1.0 / (root * jnp.sqrt(sum_uu / D + 1e-06)))[:, None]
+    inverse_u = 1.0 / (root * jnp.sqrt(sum_uu / D + 1e-06))
+    scale_u = inverse_u[:, None]
     uhat = u * scale_u
     uhat_b = uhat.astype(bf16)
     uhat_own = jnp.where(low, uhat[:, :128], uhat[:, 128:])
-    uhat_own_b = uhat_own.astype(bf16)
+    proj_own = jnp.where(low, proj_weight[:, :128], proj_weight[:, 128:])
     gain = lax.dynamic_slice_in_dim(norm_gain, rank * 256 + xh * 128, 128)
+    pick = jnp.arange(1024, dtype=jnp.int32)
+    chosen = (pick // 64 * 2 + pick % 2)[None, :] == jnp.arange(32, dtype=jnp.int32)[:, None]
+    student_of = (pick // 2 % 32)[None, :]
+    chosen2 = jnp.concatenate([chosen & (student_of == z), chosen & (student_of == 16 + z)]).astype(bf16)
+    chosen = (chosen & (student_of == xh * 16 + z)).astype(bf16)
+    image = lax.dot_general(uhat_b, proj_weight, NT, preferred_element_type=f32).astype(bf16)
+
+    hidden2, uhat, image = lax.optimization_barrier(
+        (hidden2, uhat, image)
+    )
+    image = lax.all_gather(
+        lax.psum_scatter(image, ROW, scatter_dimension=0, tiled=True), ROW, axis=0, tiled=True
+    )
 
     part_theirs = swap(parts_for(1 - core, hidden2, weight), "core")
     part_mine = parts_for(core, hidden2, weight)
@@ -127,56 +148,98 @@
     squares = jnp.sum(share(squares, PLANE, 32), axis=0).reshape(896)
     normed = (y * lax.rsqrt(squares / D + 1e-05)[:, None] * gain).astype(bf16)
     pooled = (jnp.dot(pool, normed, preferred_element_type=f32) / count).astype(bf16)
-
-    tch = pooled.astype(f32)
-    facing = lax.dynamic_slice_in_dim(uhat_own, z * 64, 64, axis=0)
-    sums = jnp.concatenate([jnp.sum(tch * tch, axis=1), jnp.sum(tch * facing, axis=1)])
-    sums = jnp.sum(share(sums.reshape(1, 128), PLANE, 32), axis=0).reshape(128)
-    scale_t = 1.0 / (root * jnp.sqrt(sums[:64] / D + 1e-06))
-    cosv = sums[64:] * scale_t
-    cos_hi = cosv.astype(bf16)
-    cos_lo = (cosv - cos_hi.astype(f32)).astype(bf16)
-    that_b = (tch * scale_t[:, None]).astype(bf16)
-    extra = jnp.pad(jnp.concatenate([cos_hi, cos_lo])[None], ((0, 15), (0, 0)))
-    gathered = share(jnp.concatenate([that_b, extra], axis=0), "z", 16)
-    teach = gathered[:, :64].reshape(1024, 128)
-    cos_sum = jnp.sum(gathered[:, 64:65].astype(f32))
-    teach2 = jnp.concatenate(ordered(xh, teach, swap(teach, "xh")), axis=1)
-
-    lhs = jnp.concatenate([uhat_own_b, teach], axis=1)
-    rhs = jnp.concatenate([uhat_own_b, -teach], axis=1)
+    teach = share(pooled, "z", 16).reshape(1024, 128)
+    teach_other = swap(teach, "xh")
 
     def rows_of(which):
         return lax.dot_general(
-            lax.dynamic_slice_in_dim(lhs, which * 512, 512, axis=0),
-            rhs,
+            lax.dynamic_slice_in_dim(teach, which * 512, 512, axis=0),
+            teach,
             NT,
             preferred_element_type=f32,
-        )
-
-    diff_theirs = swap(rows_of(1 - core).astype(bf16), "core")
-    diff_half = (rows_of(core) + diff_theirs.astype(f32)).astype(bf16)
-    diff_rows = jnp.sum(exchange(diff_half.reshape(16, 32, 1024), CHIPS).astype(f32), axis=0)
-    diff_own = share(diff_rows.astype(bf16), CHIPS, 16).reshape(512, 1024)
-    diff_b = jnp.concatenate(ordered(core, diff_own, swap(diff_own, "core")), axis=0)
+        ).astype(bf16)
+
+    tch = teach.astype(f32)
+    sum_tt = jnp.sum(tch * tch, axis=1)
+    cross = jnp.sum(tch * uhat_own, axis=1).astype(bf16)
+    tt_hi, tt_lo = two_parts(sum_tt)
+    teach_d = jnp.dot(chosen2, teach, preferred_element_type=f32).astype(bf16)
+    image_t = lax.dot_general(teach_d, proj_own, NT, preferred_element_type=f32).astype(bf16)
+    image_l, image_r = image_t[:, :512].reshape(32, 1024), image_t[:, 512:].reshape(32, 1024)
+    even_core = core == 0
+    sums = jnp.stack([tt_hi, tt_lo, cross])
+
+    def packet(which, image_half):
+        return jnp.concatenate([rows_of(which), image_half, jnp.pad(sums, ((0, 5), (0, 0)))])
+
+    came = swap(packet(1 - core, jnp.where(even_core, image_r, image_l)), "core")
+    own = packet(core, jnp.where(even_core, image_l, image_r))
+    both = own.astype(f32) + came.astype(f32)
+    tt_hi, tt_lo = two_parts(both[544] + both[545])
+    sums = jnp.stack([tt_hi, tt_lo, both[546].astype(bf16)])
+    pair = jnp.concatenate(
+        [
+            both[:512].astype(bf16).reshape(16, 32, 1024),
+            jnp.broadcast_to(sums[None], (16, 3, 1024)),
+            both[512:544].astype(bf16).reshape(16, 2, 1024),
+            jnp.zeros((16, 3, 1024), bf16),
+        ],
+        axis=1,
+    )
+    total = jnp.sum(exchange(pair, CHIPS).astype(f32), axis=0)
+    sum_tt = total[32] + total[33]
+    scale_t = 1.0 / (root * jnp.sqrt(sum_tt / D + 1e-06))
+    cosv = total[34] * scale_t
+    first = core * 512 + lax.axis_index(CHIPS) * 32
+    gram_u = inverse_u[None, :] * lax.dot_general(
+        lax.dynamic_slice_in_dim(image, first, 32, axis=0), emb, NT, preferred_element_type=f32
+    )
+    scale_rows = lax.dynamic_slice_in_dim(scale_t, first, 32)
+    diff = (gram_u - total[:32] * scale_t[None, :] * scale_rows[:, None]).astype(bf16)
+    inner = 4.0 * jnp.sum(diff.astype(f32) * gram_u, axis=1) - lax.dynamic_slice_in_dim(
+        cosv, first, 32
+    )
+    in_hi, in_lo = two_parts(inner)
+    block = jnp.concatenate(
+        [
+            diff,
+            total[35:37].astype(bf16),
+            jnp.pad(jnp.concatenate([in_hi, in_lo])[None], ((0, 5), (0, 960))),
+        ]
+    )
+    block = share(block, CHIPS, 16)
+    even, odd = ordered(core, block, swap(block, "core"))
+    diff_b = jnp.concatenate([even[:, :32].reshape(512, 1024), odd[:, :32].reshape(512, 1024)])
+    near = lax.dynamic_slice_in_dim(even, xh * 8, 8)[:, 32:34].reshape(32, 512)
+    far = lax.dynamic_slice_in_dim(odd, xh * 8, 8)[:, 32:34].reshape(32, 512)
+    image_t = jnp.concatenate([near, far], axis=1)
+    in_hi = jnp.concatenate([even[:, 34, :32], odd[:, 34, :32]]).reshape(1024)
+    in_lo = jnp.concatenate([even[:, 34, 32:64], odd[:, 34, 32:64]]).reshape(1024)
+    inner = in_hi.astype(f32) + in_lo.astype(f32)
+    diff_b, teach_other = lax.optimization_barrier((diff_b, teach_other))
+    teach2 = jnp.concatenate(ordered(xh, teach, teach_other), axis=1)
     diff_f = diff_b.astype(f32)
-    loss = 1.0 - cos_sum / 1024 + jnp.sum(diff_f * diff_f) / 1024
-
-    grad_hat = grad_scale * (
-        -teach2.astype(f32) / 1024
-        + 4.0 / 1024 * jnp.dot(diff_b, uhat_b, preferred_element_type=f32)
-    )
-    inner = jnp.sum(grad_hat * uhat, axis=1).reshape(8, 128)
-    inner = jnp.sum(share(inner, ROW, 16), axis=0).reshape(1024, 1)
-    du = ((grad_hat - uhat * inner) * scale_u).astype(bf16)
+    loss = 1.0 - jnp.sum(cosv) / 1024 + jnp.sum(diff_f * diff_f) / 1024
+
+    grad_hat = 4.0 * jnp.dot(diff_b, uhat_b, preferred_element_type=f32) - (
+        teach2.astype(f32) * scale_t[:, None]
+    )
+    du = (grad_hat - uhat * inner[:, None]) * scale_u
+    du = (du * (grad_scale / 1024)).astype(bf16)
     grad_proj = lax.dot_general(emb, du, TN, preferred_element_type=f32)
-    du_rows = lax.dynamic_index_in_dim(
-        du.reshape(16, 32, 2, 256), xh * 16 + z, axis=1, keepdims=False
-    ).reshape(32, 256)
-    student = lax.dot_general(du_rows, proj_weight, NT, preferred_element_type=f32)
-    student = student.astype(bf16)
-    student = (student.astype(f32) + swap(student, "core").astype(f32)).astype(bf16)
-    grad_student = jnp.sum(share(student, HALF, 8).astype(f32), axis=0)
+
+    mask = chosen.astype(f32)
+    scale_t_d = jnp.sum(mask * scale_t[None, :], axis=1, keepdims=True)
+    scale_u_d = jnp.sum(mask * inverse_u[None, :], axis=1, keepdims=True)
+    inner_d = jnp.sum(mask * inner[None, :], axis=1, keepdims=True)
+    diff_d = jnp.dot(chosen, diff_b, preferred_element_type=f32).astype(bf16)
+    image_d = jnp.dot(chosen, image, preferred_element_type=f32)
+    student = (
+        4.0 * jnp.dot(diff_d, image, preferred_element_type=f32)
+        - scale_t_d * image_t.astype(f32)
+        - inner_d * image_d
+    )
+    grad_student = student * scale_u_d * (grad_scale / 1024)
     return (grad_proj, grad_student, loss)
 
 

time: 321 us -> 327 us (1.019)
  blocking collectives: 94.9 us -> 24.9 us
  waiting for transfers between devices: 79.6 us -> 141 us
  other arithmetic: 17.7 us -> 26.1 us
  matrix products: 10.1 us -> 17.8 us
  local copies, waits for them, and re-layouts: 17.5 us -> 13.5 us
    all_to_all x5 -> x1, blocking collectives: 94.9 us -> 24.9 us  [exchange(): return lax.all_to_all(value, axes, split_axis=0, concat_axis=0)]
    all_to_all x6 -> x7, waiting for transfers between devices: 44.1 us -> 96.4 us  [exchange(): return lax.all_to_all(value, axes, split_axis=0, concat_axis=0)]
    all_gather x0 -> x1, waiting for transfers between devices: none -> 27.7 us  [on_device(): lax.all_gather(lax.psum_scatter(image, ROW, scatter_dimension=0, tiled=Tr...]
    all_gather x1, waiting for transfers between devices: 19.9 us -> 0.01 us  [on_device(): weight = lax.all_gather(down_weight, 'z', axis=0)]
    all_to_all x6 -> x7, starting transfers between devices: 29.6 us -> 46.8 us  [exchange(): return lax.all_to_all(value, axes, split_axis=0, concat_axis=0)]
    ppermute x8 -> x7, starting transfers between devices: 46.7 us -> 31.4 us  [swap(): return lax.ppermute(value, axis, [(0, 1), (1, 0)])]
    dot_general x4 -> x7, matrix products: 5.35 us -> 10.2 us  [the longest x1 3.08 us: on_device(): jnp.dot(diff_d, image, preferred_element_type=f32)]
    concatenate x2 -> x5, other arithmetic: 0.08 us -> 3.58 us  [the longest x1 1.58 us: on_device(): jnp.concatenate([both[:512].astype(bf16).reshape(16, 32, 1024), jnp.broad...]
  transfers between devices with their start and end apart: 15 -> 17, of which waited for: 11 -> 13; matrix products, arithmetic and copies ran while one was open for 7% -> 11% of each run, Pallas kernels for 2% -> 1%
where the time goes in v2:
time: 327 us; the launch traced here: 325 us
  waiting for transfers between devices  141 us (43%)
  starting transfers between devices  78.3 us (24%)
  other arithmetic  26.1 us (8%)
  blocking collectives  24.9 us (8%)
  between operations  18.6 us (6%)
  matrix products  17.8 us (5%)
  local copies, waits for them, and re-layouts  13.5 us (4%)
  Pallas kernels  5.27 us (2%)
    all_to_all x7, waiting for transfers between devices, exchange(): return lax.all_to_all(value, axes, split_axis=0, concat_axis=0)  96.4 us
    all_to_all x7, starting transfers between devices, exchange(): return lax.all_to_all(value, axes, split_axis=0, concat_axis=0)  46.8 us
    ppermute x7, starting transfers between devices, swap(): return lax.ppermute(value, axis, [(0, 1), (1, 0)])  31.4 us
    all_gather x1, waiting for transfers between devices, on_device(): lax.all_gather(lax.psum_scatter(image, ROW, scatter_dimension=0, tiled=Tr...  27.7 us
    all_to_all x1, blocking collectives, exchange(): return lax.all_to_all(value, axes, split_axis=0, concat_axis=0)  24.9 us
    ppermute x7, waiting for transfers between devices, swap(): return lax.ppermute(value, axis, [(0, 1), (1, 0)])  15.3 us
  transfers between devices with their start and end apart: 17, of which 13 were waited for; matrix products, arithmetic and copies ran while one was open for 11% of the time, Pallas kernels for 1%

profile of v2, /device:TPU:1, one launch (start us, length us, event | category | flops | bytes accessed | tf_op | source)
XLA Modules:
  0.0 325.3 jit_solution(5485890748311638343)
XLA Ops:
  11.2 5.5 %collective-permute-start = (bf16[464,128]{1,0:T(8,128)(2,1)S(1)}, bf16[464,128]{1,0:T(8,128)(2,1)S(1)}, u32[]{:S(2)}, u32[]{:S(2)}) collective-permute-start(bf16[464,128]{1,0:T(8,128)(2,1)S(1)} %pad_maximum_fusion.7), channel_id=1, source_target_pairs={{0,2},{2,0},{1,3},{3,1},{4,6},{6,4},{5,7},{7,5},{8,10},{10,8},{9,1... | collective-permute-start | bytes 356360 | tf_op jit(solution)/shard_map/ppermute | solution.py:21
  17.4 14.9 %all-to-all-start = ((bf16[16,2,1024]{2,1,0:T(2,128)(2,1)}), bf16[16,2,1024]{2,1,0:T(2,128)(2,1)S(1)}, u32[]{:S(2)}, u32[]{:S(2)}) async-start(bf16[16,2,1024]{2,1,0:T(2,128)(2,1)} %broadcast_in_dim.24), calls=%async_computation | async-start | bytes 131072 | tf_op jit(solution)/shard_map/all_to_all | solution.py:25
  34.8 9.2 %all-to-all-done = bf16[16,2,1024]{2,1,0:T(2,128)(2,1)S(1)} async-done(((bf16[16,2,1024]{2,1,0:T(2,128)(2,1)}), bf16[16,2,1024]{2,1,0:T(2,128)(2,1)S(1)}, u32[]{:S(2)}, u32[]{:S(2)}) %all-to-all-start) | async-done | bytes 65568 | tf_op jit(solution)/shard_map/all_to_all | solution.py:25
  44.1 1.1 broadcast_in_dim.26
  45.2 4.7 %all-to-all-start.1 = ((bf16[16,32,1024]{2,1,0:T(8,128)(2,1)}), bf16[16,32,1024]{2,1,0:T(8,128)(2,1)S(1)}, u32[]{:S(2)}, u32[]{:S(2)}) async-start(bf16[16,32,1024]{2,1,0:T(8,128)(2,1)} %broadcast_in_dim.26), calls=%async_computation.1 | async-start | bytes 2097152 | tf_op jit(solution)/shard_map/all_to_all | solution.py:25
  49.9 4.8 %collective-permute-start.2 = (bf16[448,896]{1,0:T(8,128)(2,1)S(1)}, bf16[448,896]{1,0:T(8,128)(2,1)}, u32[]{:S(2)}, u32[]{:S(2)}) collective-permute-start(bf16[448,896]{1,0:T(8,128)(2,1)S(1)} %copy-done.10), channel_id=1, source_target_pairs={{0,2},{2,0},{1,3},{3,1},{4,6},{6,4},{5,7},{7,5},{8,10},{10,8},{9,1... | collective-permute-start | bytes 2408456 | tf_op jit(solution)/shard_map/ppermute | solution.py:21
  54.7 7.7 %all-to-all-done.1 = bf16[16,32,1024]{2,1,0:T(8,128)(2,1)S(1)} async-done(((bf16[16,32,1024]{2,1,0:T(8,128)(2,1)}), bf16[16,32,1024]{2,1,0:T(8,128)(2,1)S(1)}, u32[]{:S(2)}, u32[]{:S(2)}) %all-to-all-start.1) | async-done | bytes 1048608 | tf_op jit(solution)/shard_map/all_to_all | solution.py:25
  62.4 9.6 %collective-permute-start.1 = (bf16[16,32,1024]{2,1,0:T(8,128)(2,1)S(1)}, bf16[16,32,1024]{2,1,0:T(8,128)(2,1)S(1)}, u32[]{:S(2)}, u32[]{:S(2)}) collective-permute-start(bf16[16,32,1024]{2,1,0:T(8,128)(2,1)S(1)} %all-to-all-done.1), channel_id=1, source_target_pairs={{0,64},{64,0},{1,65},{65,1},{2,66},{66,2},{3,67},{67,3},{4,68},{68... | collective-permute-start | bytes 3145736 | tf_op jit(solution)/shard_map/ppermute | solution.py:21
  72.1 7.7 %collective-permute-done.2 = bf16[448,896]{1,0:T(8,128)(2,1)} collective-permute-done((bf16[448,896]{1,0:T(8,128)(2,1)S(1)}, bf16[448,896]{1,0:T(8,128)(2,1)}, u32[]{:S(2)}, u32[]{:S(2)}) %collective-permute-start.2) | collective-permute-done | bytes 802848 | tf_op jit(solution)/shard_map/ppermute | solution.py:21
  79.7 2.5 broadcast_select_fusion.5
  82.6 1.3 copy-done.3
  83.9 1.7 multiply_reduce_fusion.1
  86.3 7.8 %all-to-all-start.2 = ((f32[16,8,128]{2,1,0:T(8,128)}), f32[16,8,128]{2,1,0:T(8,128)S(1)}, u32[]{:S(2)}, u32[]{:S(2)}) async-start(f32[16,8,128]{2,1,0:T(8,128)} %broadcast_in_dim.28), calls=%async_computation.2 | async-start | bytes 131072 | tf_op jit(solution)/shard_map/all_to_all | solution.py:25
  94.1 1.3 pad_maximum_fusion.2.hidden_ref
  95.4 4.7 %all-to-all-done.2 = f32[16,8,128]{2,1,0:T(8,128)S(1)} async-done(((f32[16,8,128]{2,1,0:T(8,128)}), f32[16,8,128]{2,1,0:T(8,128)S(1)}, u32[]{:S(2)}, u32[]{:S(2)}) %all-to-all-start.2) | async-done | bytes 65568 | tf_op jit(solution)/shard_map/all_to_all | solution.py:25
  100.1 1.4 broadcast_multiply_fusion
  101.5 2.1 convolution_convert_fusion
  103.6 2.0 copy-done.1
  105.6 2.6 shard_map.104
  108.2 2.3 collective-permute-start.3
  110.6 2.6 shard_map.103
  113.9 1.7 add_convert_fusion
  115.7 3.6 %all-to-all-start.3 = ((bf16[8,896,128]{2,1,0:T(8,128)(2,1)}), bf16[8,896,128]{2,1,0:T(8,128)(2,1)S(1)}, u32[]{:S(2)}, u32[]{:S(2)}) async-start(bf16[8,896,128]{2,1,0:T(8,128)(2,1)} %add_convert_fusion), calls=%async_computation.4 | async-start | bytes 3670016 | tf_op jit(solution)/shard_map/all_to_all | solution.py:25
  119.9 30.2 %all-to-all-done.3 = bf16[8,896,128]{2,1,0:T(8,128)(2,1)S(1)} async-done(((bf16[8,896,128]{2,1,0:T(8,128)(2,1)}), bf16[8,896,128]{2,1,0:T(8,128)(2,1)S(1)}, u32[]{:S(2)}, u32[]{:S(2)}) %all-to-all-start.3) | async-done | bytes 1835040 | tf_op jit(solution)/shard_map/all_to_all | solution.py:25
  152.0 7.4 %all-to-all-start.4 = ((f32[32,7,128]{2,1,0:T(8,128)}), f32[32,7,128]{2,1,0:T(8,128)S(1)}, u32[]{:S(2)}, u32[]{:S(2)}) async-start(f32[32,7,128]{2,1,0:T(8,128)} %broadcast_in_dim.30), calls=%async_computation.5 | async-start | bytes 262144 | tf_op jit(solution)/shard_map/all_to_all | solution.py:25
  160.2 8.2 %all-to-all-done.4 = f32[32,7,128]{2,1,0:T(8,128)S(1)} async-done(((f32[32,7,128]{2,1,0:T(8,128)}), f32[32,7,128]{2,1,0:T(8,128)S(1)}, u32[]{:S(2)}, u32[]{:S(2)}) %all-to-all-start.4) | async-done | bytes 114720 | tf_op jit(solution)/shard_map/all_to_all | solution.py:25
  168.5 1.5 fusion.9
  170.7 3.5 %all-to-all-start.5 = ((bf16[16,64,128]{2,1,0:T(8,128)(2,1)}), bf16[16,64,128]{2,1,0:T(8,128)(2,1)S(1)}, u32[]{:S(2)}, u32[]{:S(2)}) async-start(bf16[16,64,128]{2,1,0:T(8,128)(2,1)} %broadcast_in_dim.31), calls=%async_computation.6 | async-start | bytes 524288 | tf_op jit(solution)/shard_map/all_to_all | solution.py:25
  174.7 16.6 %all-to-all-done.5 = bf16[16,64,128]{2,1,0:T(8,128)(2,1)S(1)} async-done(((bf16[16,64,128]{2,1,0:T(8,128)(2,1)}), bf16[16,64,128]{2,1,0:T(8,128)(2,1)S(1)}, u32[]{:S(2)}, u32[]{:S(2)}) %all-to-all-start.5) | async-done | bytes 262176 | tf_op jit(solution)/shard_map/all_to_all | solution.py:25
  193.9 2.3 collective-permute-start.4
  196.9 1.9 collective-permute-done.4
  198.8 1.9 convert_add_fusion
  201.8 1.6 maximum_maximum_fusion
  203.3 4.8 %all-to-all-start.6 = ((bf16[16,40,1024]{2,1,0:T(8,128)(2,1)}), bf16[16,40,1024]{2,1,0:T(8,128)(2,1)}, u32[]{:S(2)}, u32[]{:S(2)}) async-start(bf16[16,40,1024]{2,1,0:T(8,128)(2,1)} %maximum_maximum_fusion), calls=%async_computation.7 | async-start | bytes 2621440 | tf_op jit(solution)/shard_map/all_to_all | solution.py:25
  208.2 19.7 %all-to-all-done.6 = bf16[16,40,1024]{2,1,0:T(8,128)(2,1)} async-done(((bf16[16,40,1024]{2,1,0:T(8,128)(2,1)}), bf16[16,40,1024]{2,1,0:T(8,128)(2,1)}, u32[]{:S(2)}, u32[]{:S(2)}) %all-to-all-start.6) | async-done | bytes 1310752 | tf_op jit(solution)/shard_map/all_to_all | solution.py:25
  227.9 1.6 convert_reduce_fusion.1
  230.9 27.7 %all-gather.4.cloned.1.call-done = bf16[1024,1024]{1,0:T(8,128)(2,1)} async-done(((bf16[64,1024]{1,0:T(8,128)(2,1)}), bf16[1024,1024]{1,0:T(8,128)(2,1)}) %all-gather.4.cloned.1.call-update) | async-done | bytes 2097168 | tf_op jit(solution)/shard_map/all_gather | solution.py:138
  258.6 1.8 multiply_reduce_fusion.4
  260.7 24.9 %all_to_all.40 = bf16[16,40,1024]{2,1,0:T(8,128)(2,1)S(1)} all-to-all(bf16[16,40,1024]{2,1,0:T(8,128)(2,1)S(1)} %broadcast_in_dim.35), channel_id=1, replica_groups=mesh['y'=4,'core'=2,'z'=16,'xh'=2,'xl'=2] {'y','xl','xh'}, dimensions={0} | all-to-all | bytes 2621440 | tf_op jit(solution)/shard_map/all_to_all | solution.py:25
  285.6 3.9 %collective-permute-start.5 = (bf16[16,40,1024]{2,1,0:T(8,128)(2,1)S(1)}, bf16[16,40,1024]{2,1,0:T(8,128)(2,1)}, u32[]{:S(2)}, u32[]{:S(2)}) collective-permute-start(bf16[16,40,1024]{2,1,0:T(8,128)(2,1)S(1)} %all_to_all.40), channel_id=1, source_target_pairs={{0,64},{64,0},{1,65},{65,1},{2,66},{66,2},{3,67},{67,3},{4,68},{68... | collective-permute-start | bytes 3932168 | tf_op jit(solution)/shard_map/ppermute | solution.py:21
  290.1 3.0 collective-permute-start.6
  293.8 1.5 broadcast_select_fusion.1
  296.5 5.0 %collective-permute-done.6 = bf16[1024,128]{0,1:T(8,128)(2,1)} collective-permute-done((bf16[1024,128]{0,1:T(8,128)(2,1)S(1)}, bf16[1024,128]{0,1:T(8,128)(2,1)}, u32[]{:S(2)}, u32[]{:S(2)}) %collective-permute-start.6) | collective-permute-done | bytes 262176 | tf_op jit(solution)/shard_map/ppermute | solution.py:21
  301.5 1.7 multiply_reduce_fusion
  304.8 1.8 broadcast_select_fusion.7
  307.4 4.2 %fusion.10 = f32[1024,256]{1,0:T(8,128)} fusion(bf16[1024,1024]{1,0:T(8,128)(2,1)} %bitcast.60, bf16[1024,1024]{1,0:T(8,128)(2,1)S(1)} %pad_maximum_fusion.1, f32[1024,256]{0,1:T(8,128)S(1)} %broadcast_multiply_fusion, bf16[1024,128]{0,1:T(8,128)(2,1)} %get-tuple-element.47, bf16[1024,128]{0,1:T(8,128)(2,1)} %get-tuple-element.46, f32[1024]{0:T(1024)S(1)} %add.238, ...), kind=kOutput, calls=%fused_computation.37 | convolution fusion | flops 1077149696 | bytes 6828032 | tf_op jit(solution)/shard_map/dot_general | solution.py:229
  311.6 2.0 convolution_multiply_fusion.3
  313.7 3.1 fusion.8
  (128 shorter events, 21.9 us)
Async XLA Ops:
  8.0 8.7 %copy-start = (bf16[32,1024]{1,0:T(8,128)(2,1)S(1)}, bf16[32,1024]{1,0:T(8,128)(2,1)}, u32[]{:S(2)}) copy-start(bf16[32,1024]{1,0:T(8,128)(2,1)} %param.14) | copy-start | bytes 196612
  8.0 26.1 %copy-start.9 = (bf16[448,256]{1,0:T(8,128)(2,1)S(1)}, bf16[448,256]{1,0:T(8,128)(2,1)}, u32[]{:S(2)}) copy-start(bf16[448,256]{1,0:T(8,128)(2,1)} %param.9) | copy-start | bytes 688132
  8.0 95.5 %all-gather.6.cloned.1.call-start = ((), (), s32[]{:S(2)}) async-start(), calls=%async_computation.11 | async-start | bytes 3899392 | tf_op jit(solution)/shard_map/all_gather | solution.py:78
  11.2 21.1 %collective-permute-start = (bf16[464,128]{1,0:T(8,128)(2,1)S(1)}, bf16[464,128]{1,0:T(8,128)(2,1)S(1)}, u32[]{:S(2)}, u32[]{:S(2)}) collective-permute-start(bf16[464,128]{1,0:T(8,128)(2,1)S(1)} %pad_maximum_fusion.7), channel_id=1, source_target_pairs={{0,2},{2,0},{1,3},{3,1},{4,6},{6,4},{5,7},{7,5},{8,10},{10,8},{9,1... | collective-permute-start | bytes 356360 | tf_op jit(solution)/shard_map/ppermute | solution.py:21
  17.4 26.7 %all-to-all-start = ((bf16[16,2,1024]{2,1,0:T(2,128)(2,1)}), bf16[16,2,1024]{2,1,0:T(2,128)(2,1)S(1)}, u32[]{:S(2)}, u32[]{:S(2)}) async-start(bf16[16,2,1024]{2,1,0:T(2,128)(2,1)} %broadcast_in_dim.24), calls=%async_computation | async-start | bytes 131072 | tf_op jit(solution)/shard_map/all_to_all | solution.py:25
  34.1 15.8 %copy-start.10 = (bf16[448,896]{1,0:T(8,128)(2,1)S(1)}, bf16[448,896]{1,0:T(8,128)(2,1)}, u32[]{:S(2)}) copy-start(bf16[448,896]{1,0:T(8,128)(2,1)} %param.8) | copy-start | bytes 2408452
  45.2 17.2 %all-to-all-start.1 = ((bf16[16,32,1024]{2,1,0:T(8,128)(2,1)}), bf16[16,32,1024]{2,1,0:T(8,128)(2,1)S(1)}, u32[]{:S(2)}, u32[]{:S(2)}) async-start(bf16[16,32,1024]{2,1,0:T(8,128)(2,1)} %broadcast_in_dim.26), calls=%async_computation.1 | async-start | bytes 2097152 | tf_op jit(solution)/shard_map/all_to_all | solution.py:25
  49.9 29.8 %collective-permute-start.2 = (bf16[448,896]{1,0:T(8,128)(2,1)S(1)}, bf16[448,896]{1,0:T(8,128)(2,1)}, u32[]{:S(2)}, u32[]{:S(2)}) collective-permute-start(bf16[448,896]{1,0:T(8,128)(2,1)S(1)} %copy-done.10), channel_id=1, source_target_pairs={{0,2},{2,0},{1,3},{3,1},{4,6},{6,4},{5,7},{7,5},{8,10},{10,8},{9,1... | collective-permute-start | bytes 2408456 | tf_op jit(solution)/shard_map/ppermute | solution.py:21
  62.4 19.8 %collective-permute-start.1 = (bf16[16,32,1024]{2,1,0:T(8,128)(2,1)S(1)}, bf16[16,32,1024]{2,1,0:T(8,128)(2,1)S(1)}, u32[]{:S(2)}, u32[]{:S(2)}) collective-permute-start(bf16[16,32,1024]{2,1,0:T(8,128)(2,1)S(1)} %all-to-all-done.1), channel_id=1, source_target_pairs={{0,64},{64,0},{1,65},{65,1},{2,66},{66,2},{3,67},{67,3},{4,68},{68... | collective-permute-start | bytes 3145736 | tf_op jit(solution)/shard_map/ppermute | solution.py:21
  82.4 1.6 copy-start.5
  82.6 1.3 copy-start.3
  82.6 11.5 %copy-start.7 = (bf16[448,896]{1,0:T(8,128)(2,1)S(1)}, bf16[448,896]{1,0:T(8,128)(2,1)}, u32[]{:S(2)}) copy-start(bf16[448,896]{1,0:T(8,128)(2,1)} %get-tuple-element.40) | copy-start | bytes 2408452
  86.3 13.8 %all-to-all-start.2 = ((f32[16,8,128]{2,1,0:T(8,128)}), f32[16,8,128]{2,1,0:T(8,128)S(1)}, u32[]{:S(2)}, u32[]{:S(2)}) async-start(f32[16,8,128]{2,1,0:T(8,128)} %broadcast_in_dim.28), calls=%async_computation.2 | async-start | bytes 131072 | tf_op jit(solution)/shard_map/all_to_all | solution.py:25
  103.6 2.0 copy-start.1
  105.6 4.9 %copy-start.2 = (bf16[14336,128]{1,0:T(8,128)(2,1)S(1)}, bf16[14336,128]{1,0:T(8,128)(2,1)}, u32[]{:S(2)}) copy-start(bf16[14336,128]{1,0:T(8,128)(2,1)} %all-gather.6.cloned.1.call-done) | copy-start | bytes 11010052
  108.2 5.7 %collective-permute-start.3 = (bf16[8,896,128]{2,1,0:T(8,128)(2,1)S(1)}, bf16[8,896,128]{2,1,0:T(8,128)(2,1)S(1)}, u32[]{:S(2)}, u32[]{:S(2)}) collective-permute-start(bf16[8,896,128]{2,1,0:T(8,128)(2,1)S(1)} %shard_map.104), channel_id=1, source_target_pairs={{0,64},{64,0},{1,65},{65,1},{2,66},{66,2},{3,67},{67,3},{4,68},{68... | collective-permute-start | bytes 5505032 | tf_op jit(solution)/shard_map/ppermute | solution.py:21
  115.7 34.4 %all-to-all-start.3 = ((bf16[8,896,128]{2,1,0:T(8,128)(2,1)}), bf16[8,896,128]{2,1,0:T(8,128)(2,1)S(1)}, u32[]{:S(2)}, u32[]{:S(2)}) async-start(bf16[8,896,128]{2,1,0:T(8,128)(2,1)} %add_convert_fusion), calls=%async_computation.4 | async-start | bytes 3670016 | tf_op jit(solution)/shard_map/all_to_all | solution.py:25
  119.3 77.0 %reduce-scatter.2.cloned.1.call-start = ((), (), s32[]{:S(2)}) async-start(), calls=%async_computation.9 | async-start | bytes 2228224 | tf_op jit(solution)/shard_map/reduce_scatter | solution.py:139
  150.1 1.0 copy-start.8
  150.4 0.8 copy-start.6
  152.0 16.4 %all-to-all-start.4 = ((f32[32,7,128]{2,1,0:T(8,128)}), f32[32,7,128]{2,1,0:T(8,128)S(1)}, u32[]{:S(2)}, u32[]{:S(2)}) async-start(f32[32,7,128]{2,1,0:T(8,128)} %broadcast_in_dim.30), calls=%async_computation.5 | async-start | bytes 262144 | tf_op jit(solution)/shard_map/all_to_all | solution.py:25
  170.7 20.7 %all-to-all-start.5 = ((bf16[16,64,128]{2,1,0:T(8,128)(2,1)}), bf16[16,64,128]{2,1,0:T(8,128)(2,1)S(1)}, u32[]{:S(2)}, u32[]{:S(2)}) async-start(bf16[16,64,128]{2,1,0:T(8,128)(2,1)} %broadcast_in_dim.31), calls=%async_computation.6 | async-start | bytes 524288 | tf_op jit(solution)/shard_map/all_to_all | solution.py:25
  174.2 84.4 %all-gather.4.cloned.1.call-start = ((), (), s32[]{:S(2)}) async-start(), calls=%async_computation.10 | async-start | bytes 2228224 | tf_op jit(solution)/shard_map/all_gather | solution.py:138
  193.9 4.9 %collective-permute-start.4 = (bf16[552,1024]{1,0:T(8,128)(2,1)}, bf16[552,1024]{1,0:T(8,128)(2,1)S(1)}, u32[]{:S(2)}, u32[]{:S(2)}) collective-permute-start(bf16[552,1024]{1,0:T(8,128)(2,1)} %pad_maximum_fusion.3), channel_id=1, source_target_pairs={{0,64},{64,0},{1,65},{65,1},{2,66},{66,2},{3,67},{67,3},{4,68},{68... | collective-permute-start | bytes 3391496 | tf_op jit(solution)/shard_map/ppermute | solution.py:21
  203.3 55.3 %copy-start.4 = (bf16[4,2,128,1024]{3,2,1,0:T(8,128)(2,1)S(1)}, bf16[4,2,128,1024]{3,2,1,0:T(8,128)(2,1)}, u32[]{:S(2)}) copy-start(bf16[4,2,128,1024]{3,2,1,0:T(8,128)(2,1)} %copy-done.3) | copy-start | bytes 6291460
  203.3 24.6 %all-to-all-start.6 = ((bf16[16,40,1024]{2,1,0:T(8,128)(2,1)}), bf16[16,40,1024]{2,1,0:T(8,128)(2,1)}, u32[]{:S(2)}, u32[]{:S(2)}) async-start(bf16[16,40,1024]{2,1,0:T(8,128)(2,1)} %maximum_maximum_fusion), calls=%async_computation.7 | async-start | bytes 2621440 | tf_op jit(solution)/shard_map/all_to_all | solution.py:25
  229.5 0.7 copy-start.11
  285.6 8.2 %collective-permute-start.5 = (bf16[16,40,1024]{2,1,0:T(8,128)(2,1)S(1)}, bf16[16,40,1024]{2,1,0:T(8,128)(2,1)}, u32[]{:S(2)}, u32[]{:S(2)}) collective-permute-start(bf16[16,40,1024]{2,1,0:T(8,128)(2,1)S(1)} %all_to_all.40), channel_id=1, source_target_pairs={{0,64},{64,0},{1,65},{65,1},{2,66},{66,2},{3,67},{67,3},{4,68},{68... | collective-permute-start | bytes 3932168 | tf_op jit(solution)/shard_map/ppermute | solution.py:21
  290.1 11.4 %collective-permute-start.6 = (bf16[1024,128]{0,1:T(8,128)(2,1)S(1)}, bf16[1024,128]{0,1:T(8,128)(2,1)}, u32[]{:S(2)}, u32[]{:S(2)}) collective-permute-start(bf16[1024,128]{0,1:T(8,128)(2,1)S(1)} %copy.84), channel_id=1, source_target_pairs={{0,2},{2,0},{1,3},{3,1},{4,6},{6,4},{5,7},{7,5},{8,10},{10,8},{9,1... | collective-permute-start | bytes 786440 | tf_op jit(solution)/shard_map/ppermute | solution.py:21
  307.4 4.2 %copy-start.12 = (pred[1024]{0:T(1024)(128)(4,1)S(1)}, pred[1024]{0:T(1024)(128)(4,1)}, u32[]{:S(2)}) copy-start(pred[1024]{0:T(1024)(128)(4,1)} %broadcast_compare_fusion) | copy-start | bytes 3076
Sparse Core Ops, SparseCore 0:
  10.9 76.9 all-gather.5
Sparse Core Ops, SparseCore 1:
  122.6 73.7 reduce-scatter.1
  198.3 60.2 all-gather.3

commit v3 on v2

--- a/solution.py
+++ b/solution.py
@@ -48,6 +48,7 @@
 
 def parts_for(core, hidden, weight):
     tokens, depth = hidden.shape
+    assert weight.shape[1] >= depth
     return pl.pallas_call(
         part_kernel,
         grid_spec=pltpu.PrefetchScalarGridSpec(
@@ -75,7 +76,9 @@
     root = jnp.sqrt(f32(D))
     low = xh == 0
 
-    weight = lax.all_gather(down_weight, "z", axis=0)
+    slabs = student_emb.reshape(32, 8, 128).transpose(1, 0, 2).reshape(256, 128)
+    weight = lax.all_gather(jnp.concatenate([down_weight, slabs]), "z", axis=0)
+
     left, right = residual[:, :128], residual[:, 128:]
     mine, theirs = jnp.where(low, left, right), jnp.where(low, right, left)
     table = jnp.pad(
@@ -105,39 +108,35 @@
     count = jnp.sum(pool, axis=1, keepdims=True)
     pool = pool.astype(bf16)
 
-    piece = lax.dynamic_slice_in_dim(student_emb, 2 * rank, 2, axis=0)
-    along = share(piece, "z", 16).reshape(32, 1024)
-    along, hidden, pool, count, residual2 = lax.optimization_barrier(
-        (along, hidden, pool, count, residual2)
+    def product_rows(which):
+        return lax.dot_general(
+            lax.dynamic_slice_in_dim(proj_weight, which * 512, 512, axis=0),
+            proj_weight,
+            NT,
+            preferred_element_type=f32,
+        ).astype(bf16)
+
+    product = swap(product_rows(1 - core), "core").astype(f32)
+    product = (product + product_rows(core).astype(f32)).astype(bf16)
+    product, hidden, pool, count, residual2 = lax.optimization_barrier(
+        (product, hidden, pool, count, residual2)
     )
     hidden2 = jnp.concatenate(ordered(xh, hidden, swap(hidden, "xh")), axis=0)
-    plane = share(along, CHIPS, 16)
-    even, odd = ordered(core, plane, swap(plane, "core"))
-    emb = jnp.stack([even.reshape(4, 128, 1024), odd.reshape(4, 128, 1024)], axis=1).reshape(
-        1024, 1024
-    )
-    u = jnp.dot(emb, proj_weight, preferred_element_type=f32)
-    sum_uu = jnp.sum(share(jnp.sum(u * u, axis=1).reshape(8, 128), ROW, 16), axis=0).reshape(1024)
-    inverse_u = 1.0 / (root * jnp.sqrt(sum_uu / D + 1e-06))
-    scale_u = inverse_u[:, None]
-    uhat = u * scale_u
-    uhat_b = uhat.astype(bf16)
-    uhat_own = jnp.where(low, uhat[:, :128], uhat[:, 128:])
+    product = jnp.sum(exchange(product.reshape(8, 64, 1024), HALF).astype(f32), axis=0)
+    product = share(product.astype(bf16), HALF, 8).reshape(512, 1024)
+    product = jnp.concatenate(ordered(core, product, swap(product, "core")))
+    hidden2, product = lax.optimization_barrier((hidden2, product))
+
     proj_own = jnp.where(low, proj_weight[:, :128], proj_weight[:, 128:])
     gain = lax.dynamic_slice_in_dim(norm_gain, rank * 256 + xh * 128, 128)
     pick = jnp.arange(1024, dtype=jnp.int32)
+    place = pick // 2 % 32
     chosen = (pick // 64 * 2 + pick % 2)[None, :] == jnp.arange(32, dtype=jnp.int32)[:, None]
-    student_of = (pick // 2 % 32)[None, :]
+    student_of = place[None, :]
+    source = place * 32 + pick // 64 * 2 + pick % 2
+    order = (source[:, None] == pick[None, :]).astype(bf16)
     chosen2 = jnp.concatenate([chosen & (student_of == z), chosen & (student_of == 16 + z)]).astype(bf16)
     chosen = (chosen & (student_of == xh * 16 + z)).astype(bf16)
-    image = lax.dot_general(uhat_b, proj_weight, NT, preferred_element_type=f32).astype(bf16)
-
-    hidden2, uhat, image = lax.optimization_barrier(
-        (hidden2, uhat, image)
-    )
-    image = lax.all_gather(
-        lax.psum_scatter(image, ROW, scatter_dimension=0, tiled=True), ROW, axis=0, tiled=True
-    )
 
     part_theirs = swap(parts_for(1 - core, hidden2, weight), "core")
     part_mine = parts_for(core, hidden2, weight)
@@ -146,10 +145,30 @@
 
     squares = jnp.sum(y * y, axis=1).reshape(7, 128)
     squares = jnp.sum(share(squares, PLANE, 32), axis=0).reshape(896)
+    squares, slabs = lax.optimization_barrier((squares, weight[:, 896:]))
+    far = swap(lax.dynamic_slice_in_dim(slabs, core * 8, 8), "xh")
+    far = jnp.concatenate(ordered(core, far, swap(far, "core")))
+    emb = jnp.concatenate(ordered(xh, slabs, far)).reshape(32, 8, 32, 128)
+    emb = emb.transpose(0, 2, 1, 3).reshape(1024, 1024)
     normed = (y * lax.rsqrt(squares / D + 1e-05)[:, None] * gain).astype(bf16)
     pooled = (jnp.dot(pool, normed, preferred_element_type=f32) / count).astype(bf16)
     teach = share(pooled, "z", 16).reshape(1024, 128)
     teach_other = swap(teach, "xh")
+
+    emb = jnp.dot(order, emb, preferred_element_type=f32).astype(bf16)
+    u = jnp.dot(emb, proj_weight, preferred_element_type=f32)
+    u_own = jnp.where(low, u[:, :128], u[:, 128:])
+    uu_hi, uu_lo = two_parts(jnp.sum(u_own * u_own, axis=1))
+    first = core * 512 + lax.axis_index(CHIPS) * 32
+    gram_raw = lax.dot_general(
+        jnp.dot(
+            lax.dynamic_slice_in_dim(emb, first, 32), product, preferred_element_type=f32
+        ).astype(bf16),
+        emb,
+        NT,
+        preferred_element_type=f32,
+    )
+    image_d = jnp.dot(student_emb, product, preferred_element_type=f32)
 
     def rows_of(which):
         return lax.dot_general(
@@ -161,39 +180,42 @@
 
     tch = teach.astype(f32)
     sum_tt = jnp.sum(tch * tch, axis=1)
-    cross = jnp.sum(tch * uhat_own, axis=1).astype(bf16)
+    cross = jnp.sum(tch * u_own, axis=1).astype(bf16)
     tt_hi, tt_lo = two_parts(sum_tt)
     teach_d = jnp.dot(chosen2, teach, preferred_element_type=f32).astype(bf16)
     image_t = lax.dot_general(teach_d, proj_own, NT, preferred_element_type=f32).astype(bf16)
     image_l, image_r = image_t[:, :512].reshape(32, 1024), image_t[:, 512:].reshape(32, 1024)
     even_core = core == 0
-    sums = jnp.stack([tt_hi, tt_lo, cross])
+    sums = jnp.stack([tt_hi, tt_lo, uu_hi, uu_lo, cross])
 
     def packet(which, image_half):
-        return jnp.concatenate([rows_of(which), image_half, jnp.pad(sums, ((0, 5), (0, 0)))])
+        return jnp.concatenate([rows_of(which), image_half, jnp.pad(sums, ((0, 3), (0, 0)))])
 
     came = swap(packet(1 - core, jnp.where(even_core, image_r, image_l)), "core")
     own = packet(core, jnp.where(even_core, image_l, image_r))
     both = own.astype(f32) + came.astype(f32)
     tt_hi, tt_lo = two_parts(both[544] + both[545])
-    sums = jnp.stack([tt_hi, tt_lo, both[546].astype(bf16)])
+    uu_hi, uu_lo = two_parts(both[546] + both[547])
+    sums = jnp.stack([tt_hi, tt_lo, uu_hi, uu_lo, both[548].astype(bf16)])
     pair = jnp.concatenate(
         [
             both[:512].astype(bf16).reshape(16, 32, 1024),
-            jnp.broadcast_to(sums[None], (16, 3, 1024)),
+            jnp.broadcast_to(sums[None], (16, 5, 1024)),
             both[512:544].astype(bf16).reshape(16, 2, 1024),
-            jnp.zeros((16, 3, 1024), bf16),
+            jnp.zeros((16, 1, 1024), bf16),
         ],
         axis=1,
     )
     total = jnp.sum(exchange(pair, CHIPS).astype(f32), axis=0)
+    total, teach_other = lax.optimization_barrier((total, teach_other))
     sum_tt = total[32] + total[33]
     scale_t = 1.0 / (root * jnp.sqrt(sum_tt / D + 1e-06))
-    cosv = total[34] * scale_t
-    first = core * 512 + lax.axis_index(CHIPS) * 32
-    gram_u = inverse_u[None, :] * lax.dot_general(
-        lax.dynamic_slice_in_dim(image, first, 32, axis=0), emb, NT, preferred_element_type=f32
-    )
+    inverse_u = 1.0 / (root * jnp.sqrt((total[34] + total[35]) / D + 1e-06))
+    scale_u = inverse_u[:, None]
+    uhat = u * scale_u
+    uhat_b = uhat.astype(bf16)
+    cosv = total[36] * scale_t * inverse_u
+    gram_u = gram_raw * inverse_u[None, :] * lax.dynamic_slice_in_dim(inverse_u, first, 32)[:, None]
     scale_rows = lax.dynamic_slice_in_dim(scale_t, first, 32)
     diff = (gram_u - total[:32] * scale_t[None, :] * scale_rows[:, None]).astype(bf16)
     inner = 4.0 * jnp.sum(diff.astype(f32) * gram_u, axis=1) - lax.dynamic_slice_in_dim(
@@ -203,7 +225,7 @@
     block = jnp.concatenate(
         [
             diff,
-            total[35:37].astype(bf16),
+            total[37:39].astype(bf16),
             jnp.pad(jnp.concatenate([in_hi, in_lo])[None], ((0, 5), (0, 960))),
         ]
     )
@@ -216,7 +238,6 @@
     in_hi = jnp.concatenate([even[:, 34, :32], odd[:, 34, :32]]).reshape(1024)
     in_lo = jnp.concatenate([even[:, 34, 32:64], odd[:, 34, 32:64]]).reshape(1024)
     inner = in_hi.astype(f32) + in_lo.astype(f32)
-    diff_b, teach_other = lax.optimization_barrier((diff_b, teach_other))
     teach2 = jnp.concatenate(ordered(xh, teach, teach_other), axis=1)
     diff_f = diff_b.astype(f32)
     loss = 1.0 - jnp.sum(cosv) / 1024 + jnp.sum(diff_f * diff_f) / 1024
@@ -232,12 +253,12 @@
     scale_t_d = jnp.sum(mask * scale_t[None, :], axis=1, keepdims=True)
     scale_u_d = jnp.sum(mask * inverse_u[None, :], axis=1, keepdims=True)
     inner_d = jnp.sum(mask * inner[None, :], axis=1, keepdims=True)
-    diff_d = jnp.dot(chosen, diff_b, preferred_element_type=f32).astype(bf16)
-    image_d = jnp.dot(chosen, image, preferred_element_type=f32)
+    diff_d = jnp.dot(chosen, diff_b, preferred_element_type=f32) * inverse_u[None, :]
+    mixed = jnp.dot(diff_d.astype(bf16), emb, preferred_element_type=f32).astype(bf16)
     student = (
-        4.0 * jnp.dot(diff_d, image, preferred_element_type=f32)
+        4.0 * jnp.dot(mixed, product, preferred_element_type=f32)
         - scale_t_d * image_t.astype(f32)
-        - inner_d * image_d
+        - inner_d * scale_u_d * image_d
     )
     grad_student = student * scale_u_d * (grad_scale / 1024)
     return (grad_proj, grad_student, loss)

time: 327 us -> 282 us (0.86)
  waiting for transfers between devices: 141 us -> 62 us
  blocking collectives: 24.9 us -> 65.8 us
  other arithmetic: 26.1 us -> 20.5 us
    all_to_all x7 -> x4, waiting for transfers between devices: 96.4 us -> 23.4 us  [exchange(): return lax.all_to_all(value, axes, split_axis=0, concat_axis=0)]
    all_to_all x1 -> x3, blocking collectives: 24.9 us -> 65.8 us  [exchange(): return lax.all_to_all(value, axes, split_axis=0, concat_axis=0)]
    all_to_all x7 -> x4, starting transfers between devices: 46.8 us -> 20.4 us  [exchange(): return lax.all_to_all(value, axes, split_axis=0, concat_axis=0)]
    ppermute x7 -> x10, starting transfers between devices: 31.4 us -> 57.6 us  [swap(): return lax.ppermute(value, axis, [(0, 1), (1, 0)])]
    all_gather x2 -> x1, waiting for transfers between devices: 27.7 us -> 3.68 us  [on_device(): weight = lax.all_gather(jnp.concatenate([down_weight, slabs]), 'z', axis=0)]
    ppermute x7 -> x10, waiting for transfers between devices: 15.3 us -> 34.9 us  [swap(): return lax.ppermute(value, axis, [(0, 1), (1, 0)])]
    dot_general x4 -> x7, matrix products: 8.98 us -> 11.4 us  [the longest x1 2.8 us: on_device(): lax.dot_general(jnp.dot(lax.dynamic_slice_in_dim(emb, first, 32), product...]
  transfers between devices with their start and end apart: 17 -> 15, of which waited for: 13 -> 11; matrix products, arithmetic and copies ran while one was open for 11% -> 5% of each run, Pallas kernels for 1% -> 1%
where the time goes in v3:
time: 282 us; the launch traced here: 280 us
  starting transfers between devices  78 us (28%)
  blocking collectives  65.8 us (23%)
  waiting for transfers between devices  62 us (22%)
  other arithmetic  20.5 us (7%)
  matrix products  18.7 us (7%)
  between operations  17.4 us (6%)
  local copies, waits for them, and re-layouts  12.5 us (4%)
  Pallas kernels  5.58 us (2%)
    all_to_all x3, blocking collectives, exchange(): return lax.all_to_all(value, axes, split_axis=0, concat_axis=0)  65.8 us
    ppermute x10, starting transfers between devices, swap(): return lax.ppermute(value, axis, [(0, 1), (1, 0)])  57.6 us
    ppermute x10, waiting for transfers between devices, swap(): return lax.ppermute(value, axis, [(0, 1), (1, 0)])  34.9 us
    all_to_all x4, waiting for transfers between devices, exchange(): return lax.all_to_all(value, axes, split_axis=0, concat_axis=0)  23.4 us
    all_to_all x4, starting transfers between devices, exchange(): return lax.all_to_all(value, axes, split_axis=0, concat_axis=0)  20.4 us
    select_n x8, other arithmetic, ordered(): return (jnp.where(first, own, other), jnp.where(first, other, own))  6.32 us
  transfers between devices with their start and end apart: 15, of which 11 were waited for; matrix products, arithmetic and copies ran while one was open for 5% of the time, Pallas kernels for 1%

profile of v3, /device:TPU:1, one launch (start us, length us, event | category | flops | bytes accessed | tf_op | source)
XLA Modules:
  0.0 280.4 jit_solution(17950677384609566118)
XLA Ops:
  8.1 1.7 pad_maximum_fusion.8
  11.3 1.0 broadcast_select_fusion.15
  12.3 5.5 %collective-permute-start.1 = (bf16[464,128]{1,0:T(8,128)(2,1)S(1)}, bf16[464,128]{1,0:T(8,128)(2,1)S(1)}, u32[]{:S(2)}, u32[]{:S(2)}) collective-permute-start(bf16[464,128]{1,0:T(8,128)(2,1)S(1)} %pad_maximum_fusion.11), channel_id=1, source_target_pairs={{0,2},{2,0},{1,3},{3,1},{4,6},{6,4},{5,7},{7,5},{8,10},{10,8},{9,1... | collective-permute-start | bytes 356360 | tf_op jit(solution)/shard_map/ppermute | solution.py:21
  18.3 5.2 %collective-permute-start = (bf16[512,1024]{1,0:T(8,128)(2,1)S(1)}, bf16[512,1024]{1,0:T(8,128)(2,1)S(1)}, u32[]{:S(2)}, u32[]{:S(2)}) collective-permute-start(bf16[512,1024]{1,0:T(8,128)(2,1)S(1)} %convolution_convert_fusion.3), channel_id=1, source_target_pairs={{0,64},{64,0},{1,65},{65,1},{2,66},{66,2},{3,67},{67,3},{4,68},{68... | collective-permute-start | bytes 3145736 | tf_op jit(solution)/shard_map/ppermute | solution.py:21
  24.7 1.0 collective-permute-done
  26.3 15.3 %all_to_all.35 = bf16[8,64,1024]{2,1,0:T(8,128)(2,1)S(1)} all-to-all(bf16[8,64,1024]{2,1,0:T(8,128)(2,1)S(1)} %bitcast.100), channel_id=1, replica_groups=mesh['y'=4,'core'=2,'z'=16,'xh'=2,'xl'=2] {'y','xl'}, dimensions={0} | all-to-all | bytes 2097152 | tf_op jit(solution)/shard_map/all_to_all | solution.py:25
  41.8 1.1 broadcast_in_dim.19
  42.9 3.6 %all-to-all-start.1 = ((bf16[8,64,1024]{2,1,0:T(8,128)(2,1)}), bf16[8,64,1024]{2,1,0:T(8,128)(2,1)S(1)}, u32[]{:S(2)}, u32[]{:S(2)}) async-start(bf16[8,64,1024]{2,1,0:T(8,128)(2,1)} %broadcast_in_dim.19), calls=%async_computation.1 | async-start | bytes 2097152 | tf_op jit(solution)/shard_map/all_to_all | solution.py:25
  46.5 7.7 %collective-permute-start.2 = (bf16[448,896]{1,0:T(8,128)(2,1)S(1)}, bf16[448,896]{1,0:T(8,128)(2,1)S(1)}, u32[]{:S(2)}, u32[]{:S(2)}) collective-permute-start(bf16[448,896]{1,0:T(8,128)(2,1)S(1)} %copy-done.10), channel_id=1, source_target_pairs={{0,2},{2,0},{1,3},{3,1},{4,6},{6,4},{5,7},{7,5},{8,10},{10,8},{9,1... | collective-permute-start | bytes 2408456 | tf_op jit(solution)/shard_map/ppermute | solution.py:21
  54.2 4.3 %all-to-all-done.1 = bf16[8,64,1024]{2,1,0:T(8,128)(2,1)S(1)} async-done(((bf16[8,64,1024]{2,1,0:T(8,128)(2,1)}), bf16[8,64,1024]{2,1,0:T(8,128)(2,1)S(1)}, u32[]{:S(2)}, u32[]{:S(2)}) %all-to-all-start.1) | async-done | bytes 1048608 | tf_op jit(solution)/shard_map/all_to_all | solution.py:25
  58.5 10.7 %collective-permute-start.3 = (bf16[512,1024]{1,0:T(8,128)(2,1)S(1)}, bf16[512,1024]{1,0:T(8,128)(2,1)}, u32[]{:S(2)}, u32[]{:S(2)}) collective-permute-start(bf16[512,1024]{1,0:T(8,128)(2,1)S(1)} %bitcast.92), channel_id=1, source_target_pairs={{0,64},{64,0},{1,65},{65,1},{2,66},{66,2},{3,67},{67,3},{4,68},{68... | collective-permute-start | bytes 3145736 | tf_op jit(solution)/shard_map/ppermute | solution.py:21
  69.2 11.4 %collective-permute-done.2 = bf16[448,896]{1,0:T(8,128)(2,1)S(1)} collective-permute-done((bf16[448,896]{1,0:T(8,128)(2,1)S(1)}, bf16[448,896]{1,0:T(8,128)(2,1)S(1)}, u32[]{:S(2)}, u32[]{:S(2)}) %collective-permute-start.2) | collective-permute-done | bytes 802848 | tf_op jit(solution)/shard_map/ppermute | solution.py:21
  80.9 1.4 broadcast_select_fusion.3
  82.3 1.5 pad_maximum_fusion
  83.9 3.7 %all-gather.3.cloned.1.call-done = bf16[18432,128]{1,0:T(8,128)(2,1)} async-done(((bf16[1152,128]{1,0:T(8,128)(2,1)}), bf16[18432,128]{1,0:T(8,128)(2,1)}) %all-gather.3.cloned.1.call-update) | async-done | bytes 4718608 | tf_op jit(solution)/shard_map/all_gather | solution.py:80
  87.5 2.3 copy-done
  89.9 2.8 shard_map.104
  92.7 10.5 %collective-permute-start.4 = (bf16[8,896,128]{2,1,0:T(8,128)(2,1)S(1)}, bf16[8,896,128]{2,1,0:T(8,128)(2,1)S(1)}, u32[]{:S(2)}, u32[]{:S(2)}) collective-permute-start(bf16[8,896,128]{2,1,0:T(8,128)(2,1)S(1)} %shard_map.104), channel_id=1, source_target_pairs={{0,64},{64,0},{1,65},{65,1},{2,66},{66,2},{3,67},{67,3},{4,68},{68... | collective-permute-start | bytes 5505032 | tf_op jit(solution)/shard_map/ppermute | solution.py:21
  103.2 2.8 shard_map.103
  107.1 27.7 %all_to_all.36 = bf16[8,896,128]{2,1,0:T(8,128)(2,1)S(1)} all-to-all(bf16[8,896,128]{2,1,0:T(8,128)(2,1)S(1)} %add_convert_fusion), channel_id=1, replica_groups=mesh['y'=4,'core'=2,'z'=16,'xh'=2,'xl'=2] {'y','xl'}, dimensions={0} | all-to-all | bytes 3670016 | tf_op jit(solution)/shard_map/all_to_all | solution.py:25
  135.9 6.6 %all-to-all-start.3 = ((f32[32,7,128]{2,1,0:T(8,128)}), f32[32,7,128]{2,1,0:T(8,128)S(1)}, u32[]{:S(2)}, u32[]{:S(2)}) async-start(f32[32,7,128]{2,1,0:T(8,128)} %broadcast_in_dim.21), calls=%async_computation.3 | async-start | bytes 262144 | tf_op jit(solution)/shard_map/all_to_all | solution.py:25
  143.3 1.3 slice.161
  144.6 5.5 %all-to-all-done.3 = f32[32,7,128]{2,1,0:T(8,128)S(1)} async-done(((f32[32,7,128]{2,1,0:T(8,128)}), f32[32,7,128]{2,1,0:T(8,128)S(1)}, u32[]{:S(2)}, u32[]{:S(2)}) %all-to-all-start.3) | async-done | bytes 114720 | tf_op jit(solution)/shard_map/all_to_all | solution.py:25
  151.2 6.4 %all-to-all-start.4 = ((bf16[16,64,128]{2,1,0:T(8,128)(2,1)}), bf16[16,64,128]{2,1,0:T(8,128)(2,1)S(1)}, u32[]{:S(2)}, u32[]{:S(2)}) async-start(bf16[16,64,128]{2,1,0:T(8,128)(2,1)} %broadcast_in_dim.22), calls=%async_computation.4 | async-start | bytes 524288 | tf_op jit(solution)/shard_map/all_to_all | solution.py:25
  158.1 2.5 collective-permute-start.5
  160.6 13.8 %collective-permute-done.5 = bf16[8,256,128]{2,1,0:T(8,128)(2,1)} collective-permute-done((bf16[8,256,128]{2,1,0:T(8,128)(2,1)S(1)}, bf16[8,256,128]{2,1,0:T(8,128)(2,1)}, u32[]{:S(2)}, u32[]{:S(2)}) %collective-permute-start.5) | collective-permute-done | bytes 524320 | tf_op jit(solution)/shard_map/ppermute | solution.py:21
  174.5 3.5 %collective-permute-start.6 = (bf16[8,256,128]{2,1,0:T(8,128)(2,1)}, bf16[8,256,128]{2,1,0:T(8,128)(2,1)}, u32[]{:S(2)}, u32[]{:S(2)}) collective-permute-start(bf16[8,256,128]{2,1,0:T(8,128)(2,1)} %collective-permute-done.5), channel_id=1, source_target_pairs={{0,64},{64,0},{1,65},{65,1},{2,66},{66,2},{3,67},{67,3},{4,68},{68... | collective-permute-start | bytes 1572872 | tf_op jit(solution)/shard_map/ppermute | solution.py:21
  179.7 1.3 broadcast_select_fusion.9
  181.3 1.0 copy.96
  182.3 2.4 fusion.5
  186.1 1.1 fusion.20
  187.1 2.3 collective-permute-start.7
  190.0 2.0 collective-permute-done.7
  192.8 1.6 maximum_maximum_fusion
  194.4 3.8 %all-to-all-start.5 = ((bf16[16,40,1024]{2,1,0:T(8,128)(2,1)}), bf16[16,40,1024]{2,1,0:T(8,128)(2,1)S(1)}, u32[]{:S(2)}, u32[]{:S(2)}) async-start(bf16[16,40,1024]{2,1,0:T(8,128)(2,1)} %maximum_maximum_fusion), calls=%async_computation.5 | async-start | bytes 2621440 | tf_op jit(solution)/shard_map/all_to_all | solution.py:25
  198.2 4.6 %collective-permute-start.8 = (bf16[1024,128]{0,1:T(8,128)(2,1)}, bf16[1024,128]{0,1:T(8,128)(2,1)}, u32[]{:S(2)}, u32[]{:S(2)}) collective-permute-start(bf16[1024,128]{0,1:T(8,128)(2,1)} %copy-done.8), channel_id=1, source_target_pairs={{0,2},{2,0},{1,3},{3,1},{4,6},{6,4},{5,7},{7,5},{8,10},{10,8},{9,1... | collective-permute-start | bytes 786440 | tf_op jit(solution)/shard_map/ppermute | solution.py:21
  202.9 13.6 %all-to-all-done.5 = bf16[16,40,1024]{2,1,0:T(8,128)(2,1)S(1)} async-done(((bf16[16,40,1024]{2,1,0:T(8,128)(2,1)}), bf16[16,40,1024]{2,1,0:T(8,128)(2,1)S(1)}, u32[]{:S(2)}, u32[]{:S(2)}) %all-to-all-start.5) | async-done | bytes 1310752 | tf_op jit(solution)/shard_map/all_to_all | solution.py:25
  216.7 5.6 %collective-permute-done.8 = bf16[1024,128]{0,1:T(8,128)(2,1)} collective-permute-done((bf16[1024,128]{0,1:T(8,128)(2,1)}, bf16[1024,128]{0,1:T(8,128)(2,1)}, u32[]{:S(2)}, u32[]{:S(2)}) %collective-permute-start.8) | collective-permute-done | bytes 262176 | tf_op jit(solution)/shard_map/ppermute | solution.py:21
  223.2 2.8 multiply_reduce_fusion.5
  226.3 22.8 %all_to_all.37 = bf16[16,40,1024]{2,1,0:T(8,128)(2,1)S(1)} all-to-all(bf16[16,40,1024]{2,1,0:T(8,128)(2,1)S(1)} %broadcast_in_dim.26), channel_id=1, replica_groups=mesh['y'=4,'core'=2,'z'=16,'xh'=2,'xl'=2] {'y','xl','xh'}, dimensions={0} | all-to-all | bytes 2621440 | tf_op jit(solution)/shard_map/all_to_all | solution.py:25
  249.1 5.0 %collective-permute-start.9 = (bf16[16,40,1024]{2,1,0:T(8,128)(2,1)S(1)}, bf16[16,40,1024]{2,1,0:T(8,128)(2,1)}, u32[]{:S(2)}, u32[]{:S(2)}) collective-permute-start(bf16[16,40,1024]{2,1,0:T(8,128)(2,1)S(1)} %all_to_all.37), channel_id=1, source_target_pairs={{0,64},{64,0},{1,65},{65,1},{2,66},{66,2},{3,67},{67,3},{4,68},{68... | collective-permute-start | bytes 3932168 | tf_op jit(solution)/shard_map/ppermute | solution.py:21
  254.7 1.9 broadcast_select_fusion.11
  256.6 1.5 broadcast_select_fusion.1
  259.5 1.7 multiply_reduce_fusion
  262.0 1.7 fusion.21
  264.0 2.5 fusion.17
  266.4 1.1 fusion.16
  267.7 4.8 %fusion.23 = f32[1024,256]{1,0:T(8,128)} fusion(bf16[1024,1024]{1,0:T(8,128)(2,1)} %copy-done.2, f32[1024,256]{0,1:T(8,128)S(1)} %copy-done.5, bf16[512,1024]{1,0:T(8,128)(2,1)} %bitcast.95, bf16[512,1024]{1,0:T(8,128)(2,1)} %bitcast.98, bf16[1024,128]{0,1:T(8,128)(2,1)} %get-tuple-element.59, bf16[1024,128]{0,1:T(8,128)(2,1)} %get-tuple-element.58, ...), kind=kOutput, calls=%fused_computation.56 | convolution fusion | flops 1081868288 | bytes 6828032 | tf_op jit(solution)/shard_map/dot_general | solution.py:250
  (133 shorter events, 17.2 us)
Async XLA Ops:
  7.2 10.6 %copy-start.3 = (bf16[1024,256]{1,0:T(8,128)(2,1)S(1)}, bf16[1024,256]{1,0:T(8,128)(2,1)}, u32[]{:S(2)}) copy-start(bf16[1024,256]{1,0:T(8,128)(2,1)} %param.15) | copy-start | bytes 1572868
  7.2 80.4 %all-gather.3.cloned.1.call-start = ((), (), s32[]{:S(2)}) async-start(), calls=%async_computation.7 | async-start | bytes 5013504 | tf_op jit(solution)/shard_map/all_gather | solution.py:80
  9.9 14.8 %copy-start.9 = (bf16[448,256]{1,0:T(8,128)(2,1)S(1)}, bf16[448,256]{1,0:T(8,128)(2,1)}, u32[]{:S(2)}) copy-start(bf16[448,256]{1,0:T(8,128)(2,1)} %param.9) | copy-start | bytes 688132
  12.3 11.2 %collective-permute-start.1 = (bf16[464,128]{1,0:T(8,128)(2,1)S(1)}, bf16[464,128]{1,0:T(8,128)(2,1)S(1)}, u32[]{:S(2)}, u32[]{:S(2)}) collective-permute-start(bf16[464,128]{1,0:T(8,128)(2,1)S(1)} %pad_maximum_fusion.11), channel_id=1, source_target_pairs={{0,2},{2,0},{1,3},{3,1},{4,6},{6,4},{5,7},{7,5},{8,10},{10,8},{9,1... | collective-permute-start | bytes 356360 | tf_op jit(solution)/shard_map/ppermute | solution.py:21
  18.3 7.5 %collective-permute-start = (bf16[512,1024]{1,0:T(8,128)(2,1)S(1)}, bf16[512,1024]{1,0:T(8,128)(2,1)S(1)}, u32[]{:S(2)}, u32[]{:S(2)}) collective-permute-start(bf16[512,1024]{1,0:T(8,128)(2,1)S(1)} %convolution_convert_fusion.3), channel_id=1, source_target_pairs={{0,64},{64,0},{1,65},{65,1},{2,66},{66,2},{3,67},{67,3},{4,68},{68... | collective-permute-start | bytes 3145736 | tf_op jit(solution)/shard_map/ppermute | solution.py:21
  41.8 4.7 %copy-start.10 = (bf16[448,896]{1,0:T(8,128)(2,1)S(1)}, bf16[448,896]{1,0:T(8,128)(2,1)}, u32[]{:S(2)}) copy-start(bf16[448,896]{1,0:T(8,128)(2,1)} %param.8) | copy-start | bytes 2408452
  42.9 15.6 %all-to-all-start.1 = ((bf16[8,64,1024]{2,1,0:T(8,128)(2,1)}), bf16[8,64,1024]{2,1,0:T(8,128)(2,1)S(1)}, u32[]{:S(2)}, u32[]{:S(2)}) async-start(bf16[8,64,1024]{2,1,0:T(8,128)(2,1)} %broadcast_in_dim.19), calls=%async_computation.1 | async-start | bytes 2097152 | tf_op jit(solution)/shard_map/all_to_all | solution.py:25
  46.5 34.2 %collective-permute-start.2 = (bf16[448,896]{1,0:T(8,128)(2,1)S(1)}, bf16[448,896]{1,0:T(8,128)(2,1)S(1)}, u32[]{:S(2)}, u32[]{:S(2)}) collective-permute-start(bf16[448,896]{1,0:T(8,128)(2,1)S(1)} %copy-done.10), channel_id=1, source_target_pairs={{0,2},{2,0},{1,3},{3,1},{4,6},{6,4},{5,7},{7,5},{8,10},{10,8},{9,1... | collective-permute-start | bytes 2408456 | tf_op jit(solution)/shard_map/ppermute | solution.py:21
  58.5 22.5 %collective-permute-start.3 = (bf16[512,1024]{1,0:T(8,128)(2,1)S(1)}, bf16[512,1024]{1,0:T(8,128)(2,1)}, u32[]{:S(2)}, u32[]{:S(2)}) collective-permute-start(bf16[512,1024]{1,0:T(8,128)(2,1)S(1)} %bitcast.92), channel_id=1, source_target_pairs={{0,64},{64,0},{1,65},{65,1},{2,66},{66,2},{3,67},{67,3},{4,68},{68... | collective-permute-start | bytes 3145736 | tf_op jit(solution)/shard_map/ppermute | solution.py:21
  87.5 2.3 copy-start
  92.7 13.9 %collective-permute-start.4 = (bf16[8,896,128]{2,1,0:T(8,128)(2,1)S(1)}, bf16[8,896,128]{2,1,0:T(8,128)(2,1)S(1)}, u32[]{:S(2)}, u32[]{:S(2)}) collective-permute-start(bf16[8,896,128]{2,1,0:T(8,128)(2,1)S(1)} %shard_map.104), channel_id=1, source_target_pairs={{0,64},{64,0},{1,65},{65,1},{2,66},{66,2},{3,67},{67,3},{4,68},{68... | collective-permute-start | bytes 5505032 | tf_op jit(solution)/shard_map/ppermute | solution.py:21
  135.9 14.2 %all-to-all-start.3 = ((f32[32,7,128]{2,1,0:T(8,128)}), f32[32,7,128]{2,1,0:T(8,128)S(1)}, u32[]{:S(2)}, u32[]{:S(2)}) async-start(f32[32,7,128]{2,1,0:T(8,128)} %broadcast_in_dim.21), calls=%async_computation.3 | async-start | bytes 262144 | tf_op jit(solution)/shard_map/all_to_all | solution.py:25
  151.2 26.7 %all-to-all-start.4 = ((bf16[16,64,128]{2,1,0:T(8,128)(2,1)}), bf16[16,64,128]{2,1,0:T(8,128)(2,1)S(1)}, u32[]{:S(2)}, u32[]{:S(2)}) async-start(bf16[16,64,128]{2,1,0:T(8,128)(2,1)} %broadcast_in_dim.22), calls=%async_computation.4 | async-start | bytes 524288 | tf_op jit(solution)/shard_map/all_to_all | solution.py:25
  158.1 16.4 %collective-permute-start.5 = (bf16[8,256,128]{2,1,0:T(8,128)(2,1)S(1)}, bf16[8,256,128]{2,1,0:T(8,128)(2,1)}, u32[]{:S(2)}, u32[]{:S(2)}) collective-permute-start(bf16[8,256,128]{2,1,0:T(8,128)(2,1)S(1)} %constant_dynamic-slice_fusion.4), channel_id=1, source_target_pairs={{0,2},{2,0},{1,3},{3,1},{4,6},{6,4},{5,7},{7,5},{8,10},{10,8},{9,1... | collective-permute-start | bytes 1572872 | tf_op jit(solution)/shard_map/ppermute | solution.py:21
  174.5 5.2 %collective-permute-start.6 = (bf16[8,256,128]{2,1,0:T(8,128)(2,1)}, bf16[8,256,128]{2,1,0:T(8,128)(2,1)}, u32[]{:S(2)}, u32[]{:S(2)}) collective-permute-start(bf16[8,256,128]{2,1,0:T(8,128)(2,1)} %collective-permute-done.5), channel_id=1, source_target_pairs={{0,64},{64,0},{1,65},{65,1},{2,66},{66,2},{3,67},{67,3},{4,68},{68... | collective-permute-start | bytes 1572872 | tf_op jit(solution)/shard_map/ppermute | solution.py:21
  178.7 6.7 %copy-start.8 = (bf16[1024,128]{0,1:T(8,128)(2,1)}, bf16[1024,128]{0,1:T(8,128)(2,1)S(1)}, u32[]{:S(2)}) copy-start(bf16[1024,128]{0,1:T(8,128)(2,1)S(1)} %copy.99) | copy-start | bytes 786436
  184.7 1.3 copy-start.2
  185.5 4.5 %copy-start.4 = (f32[1024,256]{0,1:T(8,128)}, f32[1024,256]{0,1:T(8,128)S(1)}, u32[]{:S(2)}) copy-start(f32[1024,256]{0,1:T(8,128)S(1)} %fusion.121) | copy-start | bytes 3145732
  187.1 4.9 %collective-permute-start.7 = (bf16[552,1024]{1,0:T(8,128)(2,1)}, bf16[552,1024]{1,0:T(8,128)(2,1)S(1)}, u32[]{:S(2)}, u32[]{:S(2)}) collective-permute-start(bf16[552,1024]{1,0:T(8,128)(2,1)} %fusion.20), channel_id=1, source_target_pairs={{0,64},{64,0},{1,65},{65,1},{2,66},{66,2},{3,67},{67,3},{4,68},{68... | collective-permute-start | bytes 3391496 | tf_op jit(solution)/shard_map/ppermute | solution.py:21
  194.4 28.8 %copy-start.1 = (bf16[1024,1024]{1,0:T(8,128)(2,1)S(1)}, bf16[1024,1024]{1,0:T(8,128)(2,1)}, u32[]{:S(2)}) copy-start(bf16[1024,1024]{1,0:T(8,128)(2,1)} %pad_maximum_fusion) | copy-start | bytes 6291460
  194.4 22.1 %all-to-all-start.5 = ((bf16[16,40,1024]{2,1,0:T(8,128)(2,1)}), bf16[16,40,1024]{2,1,0:T(8,128)(2,1)S(1)}, u32[]{:S(2)}, u32[]{:S(2)}) async-start(bf16[16,40,1024]{2,1,0:T(8,128)(2,1)} %maximum_maximum_fusion), calls=%async_computation.5 | async-start | bytes 2621440 | tf_op jit(solution)/shard_map/all_to_all | solution.py:25
  198.2 24.1 %collective-permute-start.8 = (bf16[1024,128]{0,1:T(8,128)(2,1)}, bf16[1024,128]{0,1:T(8,128)(2,1)}, u32[]{:S(2)}, u32[]{:S(2)}) collective-permute-start(bf16[1024,128]{0,1:T(8,128)(2,1)} %copy-done.8), channel_id=1, source_target_pairs={{0,2},{2,0},{1,3},{3,1},{4,6},{6,4},{5,7},{7,5},{8,10},{10,8},{9,1... | collective-permute-start | bytes 786440 | tf_op jit(solution)/shard_map/ppermute | solution.py:21
  216.7 5.6 %copy-start.11 = (f32[40,1024]{1,0:T(8,128)}, f32[40,1024]{1,0:T(8,128)S(1)}, u32[]{:S(2)}) copy-start(f32[40,1024]{1,0:T(8,128)S(1)} %convert_reduce_fusion.1) | copy-start | bytes 491524
  249.1 7.6 %collective-permute-start.9 = (bf16[16,40,1024]{2,1,0:T(8,128)(2,1)S(1)}, bf16[16,40,1024]{2,1,0:T(8,128)(2,1)}, u32[]{:S(2)}, u32[]{:S(2)}) collective-permute-start(bf16[16,40,1024]{2,1,0:T(8,128)(2,1)S(1)} %all_to_all.37), channel_id=1, source_target_pairs={{0,64},{64,0},{1,65},{65,1},{2,66},{66,2},{3,67},{67,3},{4,68},{68... | collective-permute-start | bytes 3932168 | tf_op jit(solution)/shard_map/ppermute | solution.py:21
  258.2 5.7 %copy-start.6 = (bf16[16,32,1024]{2,1,0:T(8,128)(2,1)}, bf16[16,32,1024]{2,1,0:T(8,128)(2,1)S(1)}, u32[]{:S(2)}) copy-start(bf16[16,32,1024]{2,1,0:T(8,128)(2,1)S(1)} %slice.175) | copy-start | bytes 3145732
  258.4 1.1 copy-start.7
  263.9 2.5 copy-start.12
  266.4 1.2 copy-start.5
Sparse Core Ops, SparseCore 0:
  10.1 77.4 all-gather.2

commit v4 on v3

--- a/solution.py
+++ b/solution.py
@@ -14,7 +14,6 @@
 PLANE = ("y", "core", "xh", "xl")
 CHIPS = ("y", "xl", "xh")
 NT = (((1,), (1,)), ((), ()))
-TN = (((0,), (0,)), ((), ()))
 
 
 def swap(value, axis):
@@ -39,16 +38,18 @@
     return jnp.where(first, own, other), jnp.where(first, other, own)
 
 
-def part_kernel(core_ref, hidden_ref, weight_ref, out_ref):
+def part_kernel(core_ref, hidden_ref, weight_ref, weight_b_ref, out_ref):
     both = jnp.concatenate([weight_ref[0], weight_ref[1]], axis=1)
-    got = jnp.dot(hidden_ref[...], both, preferred_element_type=f32).astype(bf16)
+    got = jnp.dot(hidden_ref[:, :512], both, preferred_element_type=f32)
+    both = jnp.concatenate([weight_b_ref[0], weight_b_ref[1]], axis=1)
+    got = got + jnp.dot(hidden_ref[:, 512:], both, preferred_element_type=f32)
+    got = got.astype(bf16)
     out_ref[0] = got[:, :128]
     out_ref[1] = got[:, 128:]
 
 
-def parts_for(core, hidden, weight):
+def parts_for(core, hidden, weight, weight_b):
     tokens, depth = hidden.shape
-    assert weight.shape[1] >= depth
     return pl.pallas_call(
         part_kernel,
         grid_spec=pltpu.PrefetchScalarGridSpec(
@@ -56,7 +57,8 @@
             grid=(4,),
             in_specs=[
                 pl.BlockSpec((tokens, depth), lambda i, c: (0, 0)),
-                pl.BlockSpec((2, depth, 128), lambda i, c: (2 * i + c[0], 0, 0)),
+                pl.BlockSpec((2, 512, 128), lambda i, c: (2 * i + c[0], 0, 0)),
+                pl.BlockSpec((2, depth - 512, 128), lambda i, c: (2 * i + c[0], 0, 0)),
             ],
             out_specs=pl.BlockSpec((2, tokens, 128), lambda i, c: (i, 0, 0)),
         ),
@@ -65,7 +67,7 @@
         cost_estimate=pl.CostEstimate(
             flops=2 * tokens * depth * 1024, bytes_accessed=5_000_000, transcendentals=0
         ),
-    )(core.reshape(1).astype(jnp.int32), hidden, weight)
+    )(core.reshape(1).astype(jnp.int32), hidden, weight, weight_b)
 
 
 def on_device(
@@ -77,7 +79,8 @@
     low = xh == 0
 
     slabs = student_emb.reshape(32, 8, 128).transpose(1, 0, 2).reshape(256, 128)
-    weight = lax.all_gather(jnp.concatenate([down_weight, slabs]), "z", axis=0)
+    weight = lax.all_gather(down_weight[:512], "z", axis=0)
+    weight_b = lax.all_gather(jnp.concatenate([down_weight[512:], slabs]), "z", axis=0)
 
     left, right = residual[:, :128], residual[:, 128:]
     mine, theirs = jnp.where(low, left, right), jnp.where(low, right, left)
@@ -138,16 +141,18 @@
     chosen2 = jnp.concatenate([chosen & (student_of == z), chosen & (student_of == 16 + z)]).astype(bf16)
     chosen = (chosen & (student_of == xh * 16 + z)).astype(bf16)
 
-    part_theirs = swap(parts_for(1 - core, hidden2, weight), "core")
-    part_mine = parts_for(core, hidden2, weight)
+    slabs = weight_b[:, 384:]
+    far = swap(lax.dynamic_slice_in_dim(slabs, core * 8, 8), "xh")
+    part_theirs = swap(parts_for(1 - core, hidden2, weight, weight_b), "core")
+    part_mine = parts_for(core, hidden2, weight, weight_b)
     pair = (part_mine.astype(f32) + part_theirs.astype(f32)).astype(bf16)
     y = jnp.sum(exchange(pair, HALF).astype(f32), axis=0) + residual2.astype(f32)
 
+    y, far = lax.optimization_barrier((y, far))
     squares = jnp.sum(y * y, axis=1).reshape(7, 128)
     squares = jnp.sum(share(squares, PLANE, 32), axis=0).reshape(896)
-    squares, slabs = lax.optimization_barrier((squares, weight[:, 896:]))
-    far = swap(lax.dynamic_slice_in_dim(slabs, core * 8, 8), "xh")
     far = jnp.concatenate(ordered(core, far, swap(far, "core")))
+    squares, far = lax.optimization_barrier((squares, far))
     emb = jnp.concatenate(ordered(xh, slabs, far)).reshape(32, 8, 32, 128)
     emb = emb.transpose(0, 2, 1, 3).reshape(1024, 1024)
     normed = (y * lax.rsqrt(squares / D + 1e-05)[:, None] * gain).astype(bf16)
@@ -155,6 +160,8 @@
     teach = share(pooled, "z", 16).reshape(1024, 128)
     teach_other = swap(teach, "xh")
 
+    emb_t = lax.dot_general(emb, order, (((0,), (1,)), ((), ())), preferred_element_type=f32)
+    emb_t = emb_t.astype(bf16)
     emb = jnp.dot(order, emb, preferred_element_type=f32).astype(bf16)
     u = jnp.dot(emb, proj_weight, preferred_element_type=f32)
     u_own = jnp.where(low, u[:, :128], u[:, 128:])
@@ -191,7 +198,10 @@
     def packet(which, image_half):
         return jnp.concatenate([rows_of(which), image_half, jnp.pad(sums, ((0, 3), (0, 0)))])
 
-    came = swap(packet(1 - core, jnp.where(even_core, image_r, image_l)), "core")
+    going, teach_other = lax.optimization_barrier(
+        (packet(1 - core, jnp.where(even_core, image_r, image_l)), teach_other)
+    )
+    came = swap(going, "core")
     own = packet(core, jnp.where(even_core, image_l, image_r))
     both = own.astype(f32) + came.astype(f32)
     tt_hi, tt_lo = two_parts(both[544] + both[545])
@@ -207,7 +217,7 @@
         axis=1,
     )
     total = jnp.sum(exchange(pair, CHIPS).astype(f32), axis=0)
-    total, teach_other = lax.optimization_barrier((total, teach_other))
+    total, emb_t = lax.optimization_barrier((total, emb_t))
     sum_tt = total[32] + total[33]
     scale_t = 1.0 / (root * jnp.sqrt(sum_tt / D + 1e-06))
     inverse_u = 1.0 / (root * jnp.sqrt((total[34] + total[35]) / D + 1e-06))
@@ -247,7 +257,7 @@
     )
     du = (grad_hat - uhat * inner[:, None]) * scale_u
     du = (du * (grad_scale / 1024)).astype(bf16)
-    grad_proj = lax.dot_general(emb, du, TN, preferred_element_type=f32)
+    grad_proj = jnp.dot(emb_t, du, preferred_element_type=f32)
 
     mask = chosen.astype(f32)
     scale_t_d = jnp.sum(mask * scale_t[None, :], axis=1, keepdims=True)

time: 282 us -> 365 us (1.29)
  waiting for transfers between devices: 62 us -> 142 us
  blocking collectives: 65.8 us -> 38.5 us
  local copies, waits for them, and re-layouts: 12.5 us -> 22 us
  starting transfers between devices: 78 us -> 86.6 us
  matrix products: 18.7 us -> 25.5 us
  other arithmetic: 20.5 us -> 27 us
    all_gather x1 -> x2, waiting for transfers between devices: 3.68 us -> 67.4 us  [the longest x1 67.4 us: on_device(): lax.all_gather(jnp.concatenate([down_weight[512:], slabs]), 'z', axis=0)]
    all_to_all x3 -> x2, blocking collectives: 65.8 us -> 38.5 us  [exchange(): return lax.all_to_all(value, axes, split_axis=0, concat_axis=0)]
    all_to_all x4 -> x5, waiting for transfers between devices: 23.4 us -> 46.1 us  [exchange(): return lax.all_to_all(value, axes, split_axis=0, concat_axis=0)]
    ppermute x10, waiting for transfers between devices: 34.9 us -> 28.1 us  [swap(): return lax.ppermute(value, axis, [(0, 1), (1, 0)])]
    unnamed x33 -> x61, local copies, waits for them, and re-layouts: 5 us -> 10.7 us
    dot_general x1 -> x2, matrix products: 4.8 us -> 10.5 us  [the longest x1 5.68 us: on_device(): lax.dot_general(emb, order, (((0,), (1,)), ((), ())), preferred_element_t...]
    all_to_all x4 -> x5, starting transfers between devices: 20.4 us -> 25.5 us  [exchange(): return lax.all_to_all(value, axes, split_axis=0, concat_axis=0)]
  transfers between devices with their start and end apart: 15 -> 17, of which waited for: 11 -> 11; matrix products, arithmetic and copies ran while one was open for 5% -> 11% of each run, Pallas kernels for 1% -> 1%
where the time goes in v4:
time: 365 us; the launch traced here: 364 us
  waiting for transfers between devices  142 us (39%)
  starting transfers between devices  86.6 us (24%)
  blocking collectives  38.5 us (11%)
  other arithmetic  27 us (7%)
  matrix products  25.5 us (7%)
  local copies, waits for them, and re-layouts  22 us (6%)
  between operations  17.5 us (5%)
  Pallas kernels  5.35 us (1%)
    all_gather x1, waiting for transfers between devices, on_device(): lax.all_gather(jnp.concatenate([down_weight[512:], slabs]), 'z', axis=0)  67.4 us
    ppermute x10, starting transfers between devices, swap(): return lax.ppermute(value, axis, [(0, 1), (1, 0)])  61 us
    all_to_all x5, waiting for transfers between devices, exchange(): return lax.all_to_all(value, axes, split_axis=0, concat_axis=0)  46.1 us
    all_to_all x2, blocking collectives, exchange(): return lax.all_to_all(value, axes, split_axis=0, concat_axis=0)  38.5 us
    ppermute x10, waiting for transfers between devices, swap(): return lax.ppermute(value, axis, [(0, 1), (1, 0)])  28.1 us
    all_to_all x5, starting transfers between devices, exchange(): return lax.all_to_all(value, axes, split_axis=0, concat_axis=0)  25.5 us
    unnamed x61, local copies, waits for them, and re-layouts  10.7 us
    select_n x8, other arithmetic, ordered(): return (jnp.where(first, own, other), jnp.where(first, other, own))  7.86 us
  transfers between devices with their start and end apart: 17, of which 11 were waited for; matrix products, arithmetic and copies ran while one was open for 11% of the time, Pallas kernels for 1%

profile of v4, /device:TPU:1, one launch (start us, length us, event | category | flops | bytes accessed | tf_op | source)
XLA Modules:
  0.0 364.0 jit_solution(3013713178747258967)
XLA Ops:
  7.2 1.6 slice.133
  11.3 5.5 %collective-permute-start.1 = (bf16[464,128]{1,0:T(8,128)(2,1)S(1)}, bf16[464,128]{1,0:T(8,128)(2,1)S(1)}, u32[]{:S(2)}, u32[]{:S(2)}) collective-permute-start(bf16[464,128]{1,0:T(8,128)(2,1)S(1)} %pad_maximum_fusion.11), channel_id=1, source_target_pairs={{0,2},{2,0},{1,3},{3,1},{4,6},{6,4},{5,7},{7,5},{8,10},{10,8},{9,1... | collective-permute-start | bytes 356360 | tf_op jit(solution)/shard_map/ppermute | solution.py:20
  16.8 1.6 convolution_convert_fusion.3
  18.5 5.4 %collective-permute-start = (bf16[512,1024]{1,0:T(8,128)(2,1)S(1)}, bf16[512,1024]{1,0:T(8,128)(2,1)S(1)}, u32[]{:S(2)}, u32[]{:S(2)}) collective-permute-start(bf16[512,1024]{1,0:T(8,128)(2,1)S(1)} %convolution_convert_fusion.3), channel_id=1, source_target_pairs={{0,64},{64,0},{1,65},{65,1},{2,66},{66,2},{3,67},{67,3},{4,68},{68... | collective-permute-start | bytes 3145736 | tf_op jit(solution)/shard_map/ppermute | solution.py:20
  27.5 16.4 %all_to_all.35 = bf16[8,64,1024]{2,1,0:T(8,128)(2,1)S(1)} all-to-all(bf16[8,64,1024]{2,1,0:T(8,128)(2,1)S(1)} %bitcast.108), channel_id=1, replica_groups=mesh['y'=4,'core'=2,'z'=16,'xh'=2,'xl'=2] {'y','xl'}, dimensions={0} | all-to-all | bytes 2097152 | tf_op jit(solution)/shard_map/all_to_all | solution.py:24
  45.2 3.6 all-to-all-start.1
  48.7 6.8 %collective-permute-start.2 = (bf16[448,896]{1,0:T(8,128)(2,1)}, bf16[448,896]{1,0:T(8,128)(2,1)}, u32[]{:S(2)}, u32[]{:S(2)}) collective-permute-start(bf16[448,896]{1,0:T(8,128)(2,1)} %param.8), channel_id=1, source_target_pairs={{0,2},{2,0},{1,3},{3,1},{4,6},{6,4},{5,7},{7,5},{8,10},{10,8},{9,1... | collective-permute-start | bytes 2408456 | tf_op jit(solution)/shard_map/ppermute | solution.py:20
  55.5 6.3 %all-to-all-done.1 = bf16[8,64,1024]{2,1,0:T(8,128)(2,1)S(1)} async-done(((bf16[8,64,1024]{2,1,0:T(8,128)(2,1)}), bf16[8,64,1024]{2,1,0:T(8,128)(2,1)S(1)}, u32[]{:S(2)}, u32[]{:S(2)}) %all-to-all-start.1) | async-done | bytes 1048608 | tf_op jit(solution)/shard_map/all_to_all | solution.py:24
  61.8 8.7 %collective-permute-start.3 = (bf16[512,1024]{1,0:T(8,128)(2,1)S(1)}, bf16[512,1024]{1,0:T(8,128)(2,1)S(1)}, u32[]{:S(2)}, u32[]{:S(2)}) collective-permute-start(bf16[512,1024]{1,0:T(8,128)(2,1)S(1)} %bitcast.100), channel_id=1, source_target_pairs={{0,64},{64,0},{1,65},{65,1},{2,66},{66,2},{3,67},{67,3},{4,68},{68... | collective-permute-start | bytes 3145736 | tf_op jit(solution)/shard_map/ppermute | solution.py:20
  70.5 11.8 %collective-permute-done.2 = bf16[448,896]{1,0:T(8,128)(2,1)} collective-permute-done((bf16[448,896]{1,0:T(8,128)(2,1)}, bf16[448,896]{1,0:T(8,128)(2,1)}, u32[]{:S(2)}, u32[]{:S(2)}) %collective-permute-start.2) | collective-permute-done | bytes 802848 | tf_op jit(solution)/shard_map/ppermute | solution.py:20
  82.3 1.5 broadcast_select_fusion.7
  85.4 1.5 pad_maximum_fusion
  86.9 67.4 %all-gather.7.cloned.1.call-done = bf16[10240,128]{1,0:T(8,128)(2,1)} async-done(((bf16[640,128]{1,0:T(8,128)(2,1)}), bf16[10240,128]{1,0:T(8,128)(2,1)}) %all-gather.7.cloned.1.call-update) | async-done | bytes 2621456 | tf_op jit(solution)/shard_map/all_gather | solution.py:83
  154.3 1.7 copy-done
  157.4 1.6 copy-done.4
  159.0 2.7 shard_map.104
  161.7 11.5 %collective-permute-start.4 = (bf16[8,896,128]{2,1,0:T(8,128)(2,1)S(1)}, bf16[8,896,128]{2,1,0:T(8,128)(2,1)S(1)}, u32[]{:S(2)}, u32[]{:S(2)}) collective-permute-start(bf16[8,896,128]{2,1,0:T(8,128)(2,1)S(1)} %shard_map.104), channel_id=1, source_target_pairs={{0,64},{64,0},{1,65},{65,1},{2,66},{66,2},{3,67},{67,3},{4,68},{68... | collective-permute-start | bytes 5505032 | tf_op jit(solution)/shard_map/ppermute | solution.py:20
  173.2 2.7 shard_map.103
  176.6 1.8 add_convert_fusion
  178.4 4.9 %all-to-all-start.2 = ((bf16[8,896,128]{2,1,0:T(8,128)(2,1)}), bf16[8,896,128]{2,1,0:T(8,128)(2,1)}, u32[]{:S(2)}, u32[]{:S(2)}) async-start(bf16[8,896,128]{2,1,0:T(8,128)(2,1)} %add_convert_fusion), calls=%async_computation.2 | async-start | bytes 3670016 | tf_op jit(solution)/shard_map/all_to_all | solution.py:24
  185.1 4.3 %collective-permute-start.5 = (bf16[8,256,128]{2,1,0:T(8,128)(2,1)}, bf16[8,256,128]{2,1,0:T(8,128)(2,1)}, u32[]{:S(2)}, u32[]{:S(2)}) collective-permute-start(bf16[8,256,128]{2,1,0:T(8,128)(2,1)} %constant_dynamic-slice_fusion.4), channel_id=1, source_target_pairs={{0,2},{2,0},{1,3},{3,1},{4,6},{6,4},{5,7},{7,5},{8,10},{10,8},{9,1... | collective-permute-start | bytes 1572872 | tf_op jit(solution)/shard_map/ppermute | solution.py:20
  189.4 17.6 %all-to-all-done.2 = bf16[8,896,128]{2,1,0:T(8,128)(2,1)} async-done(((bf16[8,896,128]{2,1,0:T(8,128)(2,1)}), bf16[8,896,128]{2,1,0:T(8,128)(2,1)}, u32[]{:S(2)}, u32[]{:S(2)}) %all-to-all-start.2) | async-done | bytes 1835040 | tf_op jit(solution)/shard_map/all_to_all | solution.py:24
  207.0 1.8 convert_reduce_fusion
  208.9 8.8 %collective-permute-done.5 = bf16[8,256,128]{2,1,0:T(8,128)(2,1)} collective-permute-done((bf16[8,256,128]{2,1,0:T(8,128)(2,1)}, bf16[8,256,128]{2,1,0:T(8,128)(2,1)}, u32[]{:S(2)}, u32[]{:S(2)}) %collective-permute-start.5) | collective-permute-done | bytes 524320 | tf_op jit(solution)/shard_map/ppermute | solution.py:20
  217.7 3.1 collective-permute-start.6
  221.7 6.0 %all-to-all-start.3 = ((f32[32,7,128]{2,1,0:T(8,128)}), f32[32,7,128]{2,1,0:T(8,128)S(1)}, u32[]{:S(2)}, u32[]{:S(2)}) async-start(f32[32,7,128]{2,1,0:T(8,128)} %broadcast_in_dim.21), calls=%async_computation.3 | async-start | bytes 262144 | tf_op jit(solution)/shard_map/all_to_all | solution.py:24
  229.5 1.8 copy.111
  232.5 2.8 all-to-all-done.3
  239.4 7.1 %all-to-all-start.4 = ((bf16[16,64,128]{2,1,0:T(8,128)(2,1)}), bf16[16,64,128]{2,1,0:T(8,128)(2,1)S(1)}, u32[]{:S(2)}, u32[]{:S(2)}) async-start(bf16[16,64,128]{2,1,0:T(8,128)(2,1)} %broadcast_in_dim.22), calls=%async_computation.4 | async-start | bytes 524288 | tf_op jit(solution)/shard_map/all_to_all | solution.py:24
  249.0 2.4 fusion.7
  253.5 7.1 %all-to-all-done.4 = bf16[16,64,128]{2,1,0:T(8,128)(2,1)S(1)} async-done(((bf16[16,64,128]{2,1,0:T(8,128)(2,1)}), bf16[16,64,128]{2,1,0:T(8,128)(2,1)S(1)}, u32[]{:S(2)}, u32[]{:S(2)}) %all-to-all-start.4) | async-done | bytes 262176 | tf_op jit(solution)/shard_map/all_to_all | solution.py:24
  261.3 1.9 collective-permute-start.7
  265.3 4.8 %collective-permute-done.7 = bf16[1024,128]{0,1:T(8,128)(2,1)} collective-permute-done((bf16[1024,128]{0,1:T(8,128)(2,1)S(1)}, bf16[1024,128]{0,1:T(8,128)(2,1)}, u32[]{:S(2)}, u32[]{:S(2)}) %collective-permute-start.7) | collective-permute-done | bytes 262176 | tf_op jit(solution)/shard_map/ppermute | solution.py:20
  270.0 8.1 %collective-permute-start.8 = (bf16[552,1024]{1,0:T(8,128)(2,1)}, bf16[552,1024]{1,0:T(8,128)(2,1)S(1)}, u32[]{:S(2)}, u32[]{:S(2)}) collective-permute-start(bf16[552,1024]{1,0:T(8,128)(2,1)} %fusion.27), channel_id=1, source_target_pairs={{0,64},{64,0},{1,65},{65,1},{2,66},{66,2},{3,67},{67,3},{4,68},{68... | collective-permute-start | bytes 3391496 | tf_op jit(solution)/shard_map/ppermute | solution.py:20
  278.7 2.0 collective-permute-done.8
  281.5 1.6 maximum_maximum_fusion
  283.1 3.9 %all-to-all-start.5 = ((bf16[16,40,1024]{2,1,0:T(8,128)(2,1)}), bf16[16,40,1024]{2,1,0:T(8,128)(2,1)S(1)}, u32[]{:S(2)}, u32[]{:S(2)}) async-start(bf16[16,40,1024]{2,1,0:T(8,128)(2,1)} %maximum_maximum_fusion), calls=%async_computation.5 | async-start | bytes 2621440 | tf_op jit(solution)/shard_map/all_to_all | solution.py:24
  287.0 5.7 %fusion.10 = bf16[1024,1024]{1,0:T(8,128)(2,1)} fusion(s32[1024]{0:T(1024)S(1)} %get-tuple-element.89, bf16[128,8,8,128]{3,2,1,0:T(8,128)(2,1)} %bitcast.110), kind=kOutput, calls=%fused_computation.19 | convolution fusion | flops 2149580800 | bytes 4198400 | tf_op jit(solution)/shard_map/dot_general | solution.py:163
  292.7 12.3 %all-to-all-done.5 = bf16[16,40,1024]{2,1,0:T(8,128)(2,1)S(1)} async-done(((bf16[16,40,1024]{2,1,0:T(8,128)(2,1)}), bf16[16,40,1024]{2,1,0:T(8,128)(2,1)S(1)}, u32[]{:S(2)}, u32[]{:S(2)}) %all-to-all-start.5) | async-done | bytes 1310752 | tf_op jit(solution)/shard_map/all_to_all | solution.py:24
  306.6 2.8 multiply_reduce_fusion.5
  309.8 22.1 %all_to_all.36 = bf16[16,40,1024]{2,1,0:T(8,128)(2,1)S(1)} all-to-all(bf16[16,40,1024]{2,1,0:T(8,128)(2,1)S(1)} %broadcast_in_dim.26), channel_id=1, replica_groups=mesh['y'=4,'core'=2,'z'=16,'xh'=2,'xl'=2] {'y','xl','xh'}, dimensions={0} | all-to-all | bytes 2621440 | tf_op jit(solution)/shard_map/all_to_all | solution.py:24
  331.9 5.8 %collective-permute-start.9 = (bf16[16,40,1024]{2,1,0:T(8,128)(2,1)S(1)}, bf16[16,40,1024]{2,1,0:T(8,128)(2,1)}, u32[]{:S(2)}, u32[]{:S(2)}) collective-permute-start(bf16[16,40,1024]{2,1,0:T(8,128)(2,1)S(1)} %all_to_all.36), channel_id=1, source_target_pairs={{0,64},{64,0},{1,65},{65,1},{2,66},{66,2},{3,67},{67,3},{4,68},{68... | collective-permute-start | bytes 3932168 | tf_op jit(solution)/shard_map/ppermute | solution.py:20
  337.6 1.9 broadcast_select_fusion.11
  340.2 1.5 broadcast_select_fusion.1
  343.1 1.7 multiply_reduce_fusion
  345.6 1.7 fusion.28
  347.5 2.5 fusion.24
  351.3 4.8 %fusion.30 = f32[1024,256]{1,0:T(8,128)} fusion(bf16[1024,1024]{1,0:T(8,128)(2,1)} %fusion.10, f32[1024,256]{0,1:T(8,128)S(1)} %copy-done.9, bf16[512,1024]{1,0:T(8,128)(2,1)} %bitcast.103, bf16[512,1024]{1,0:T(8,128)(2,1)} %bitcast.106, bf16[1024,128]{0,1:T(8,128)(2,1)} %get-tuple-element.67, bf16[1024,128]{0,1:T(8,128)(2,1)} %get-tuple-element.66, ...), kind=kOutput, calls=%fused_computation.61 | convolution fusion | flops 1081868288 | bytes 6828032 | tf_op jit(solution)/shard_map/dot_general | solution.py:260
  (170 shorter events, 34.0 us)
Async XLA Ops:
  7.2 16.7 %slice-start = ((bf16[896,128]{1,0:T(8,128)(2,1)}), bf16[384,128]{1,0:T(8,128)(2,1)S(1)}, s32[]{:S(2)}) async-start(bf16[896,128]{1,0:T(8,128)(2,1)} %param.10), calls=%async_computation.9 | async-start | bytes 196608 | tf_op jit(solution)/shard_map/slice | solution.py:83
  7.2 16.7 %copy-start.21 = (bf16[32,1024]{1,0:T(8,128)(2,1)S(1)}, bf16[32,1024]{1,0:T(8,128)(2,1)}, u32[]{:S(2)}) copy-start(bf16[32,1024]{1,0:T(8,128)(2,1)} %param.14) | copy-start | bytes 196612
  7.2 79.7 %all-gather.5.cloned.1.call-start = ((), (), s32[]{:S(2)}) async-start(), calls=%async_computation.7 | async-start | bytes 2228224 | tf_op jit(solution)/shard_map/all_gather | solution.py:82
  8.9 145.4 %all-gather.7.cloned.1.call-start = ((), (), s32[]{:S(2)}) async-start(), calls=%async_computation.8 | async-start | bytes 2785280 | tf_op jit(solution)/shard_map/all_gather | solution.py:83
  11.3 13.3 %collective-permute-start.1 = (bf16[464,128]{1,0:T(8,128)(2,1)S(1)}, bf16[464,128]{1,0:T(8,128)(2,1)S(1)}, u32[]{:S(2)}, u32[]{:S(2)}) collective-permute-start(bf16[464,128]{1,0:T(8,128)(2,1)S(1)} %pad_maximum_fusion.11), channel_id=1, source_target_pairs={{0,2},{2,0},{1,3},{3,1},{4,6},{6,4},{5,7},{7,5},{8,10},{10,8},{9,1... | collective-permute-start | bytes 356360 | tf_op jit(solution)/shard_map/ppermute | solution.py:20
  16.8 10.2 %copy-start.18 = (bf16[448,256]{1,0:T(8,128)(2,1)S(1)}, bf16[448,256]{1,0:T(8,128)(2,1)}, u32[]{:S(2)}) copy-start(bf16[448,256]{1,0:T(8,128)(2,1)} %param.9) | copy-start | bytes 688132
  18.4 8.6 %copy-start.7 = (bf16[1024,256]{1,0:T(8,128)(2,1)S(1)}, bf16[1024,256]{1,0:T(8,128)(2,1)}, u32[]{:S(2)}) copy-start(bf16[1024,256]{1,0:T(8,128)(2,1)} %param.15) | copy-start | bytes 1572868
  18.5 8.6 %collective-permute-start = (bf16[512,1024]{1,0:T(8,128)(2,1)S(1)}, bf16[512,1024]{1,0:T(8,128)(2,1)S(1)}, u32[]{:S(2)}, u32[]{:S(2)}) collective-permute-start(bf16[512,1024]{1,0:T(8,128)(2,1)S(1)} %convolution_convert_fusion.3), channel_id=1, source_target_pairs={{0,64},{64,0},{1,65},{65,1},{2,66},{66,2},{3,67},{67,3},{4,68},{68... | collective-permute-start | bytes 3145736 | tf_op jit(solution)/shard_map/ppermute | solution.py:20
  45.2 16.6 %all-to-all-start.1 = ((bf16[8,64,1024]{2,1,0:T(8,128)(2,1)}), bf16[8,64,1024]{2,1,0:T(8,128)(2,1)S(1)}, u32[]{:S(2)}, u32[]{:S(2)}) async-start(bf16[8,64,1024]{2,1,0:T(8,128)(2,1)} %broadcast_in_dim.19), calls=%async_computation.1 | async-start | bytes 2097152 | tf_op jit(solution)/shard_map/all_to_all | solution.py:24
  48.7 33.5 %collective-permute-start.2 = (bf16[448,896]{1,0:T(8,128)(2,1)}, bf16[448,896]{1,0:T(8,128)(2,1)}, u32[]{:S(2)}, u32[]{:S(2)}) collective-permute-start(bf16[448,896]{1,0:T(8,128)(2,1)} %param.8), channel_id=1, source_target_pairs={{0,2},{2,0},{1,3},{3,1},{4,6},{6,4},{5,7},{7,5},{8,10},{10,8},{9,1... | collective-permute-start | bytes 2408456 | tf_op jit(solution)/shard_map/ppermute | solution.py:20
  61.8 23.4 %collective-permute-start.3 = (bf16[512,1024]{1,0:T(8,128)(2,1)S(1)}, bf16[512,1024]{1,0:T(8,128)(2,1)S(1)}, u32[]{:S(2)}, u32[]{:S(2)}) collective-permute-start(bf16[512,1024]{1,0:T(8,128)(2,1)S(1)} %bitcast.100), channel_id=1, source_target_pairs={{0,64},{64,0},{1,65},{65,1},{2,66},{66,2},{3,67},{67,3},{4,68},{68... | collective-permute-start | bytes 3145736 | tf_op jit(solution)/shard_map/ppermute | solution.py:20
  154.3 1.7 copy-start
  156.0 1.4 copy-start.2
  157.4 1.6 copy-start.4
  159.0 14.2 %copy-start.1 = (bf16[10240,128]{1,0:T(8,128)(2,1)S(1)}, bf16[10240,128]{1,0:T(8,128)(2,1)}, u32[]{:S(2)}) copy-start(bf16[10240,128]{1,0:T(8,128)(2,1)} %all-gather.7.cloned.1.call-done) | copy-start | bytes 7864324
  159.0 14.2 %copy-start.3 = (bf16[896,896]{1,0:T(8,128)(2,1)S(1)}, bf16[896,896]{1,0:T(8,128)(2,1)}, u32[]{:S(2)}) copy-start(bf16[896,896]{1,0:T(8,128)(2,1)} %pad_maximum_fusion.3.hidden_ref) | copy-start | bytes 4816900
  161.7 14.9 %collective-permute-start.4 = (bf16[8,896,128]{2,1,0:T(8,128)(2,1)S(1)}, bf16[8,896,128]{2,1,0:T(8,128)(2,1)S(1)}, u32[]{:S(2)}, u32[]{:S(2)}) collective-permute-start(bf16[8,896,128]{2,1,0:T(8,128)(2,1)S(1)} %shard_map.104), channel_id=1, source_target_pairs={{0,64},{64,0},{1,65},{65,1},{2,66},{66,2},{3,67},{67,3},{4,68},{68... | collective-permute-start | bytes 5505032 | tf_op jit(solution)/shard_map/ppermute | solution.py:20
  178.4 28.6 %all-to-all-start.2 = ((bf16[8,896,128]{2,1,0:T(8,128)(2,1)}), bf16[8,896,128]{2,1,0:T(8,128)(2,1)}, u32[]{:S(2)}, u32[]{:S(2)}) async-start(bf16[8,896,128]{2,1,0:T(8,128)(2,1)} %add_convert_fusion), calls=%async_computation.2 | async-start | bytes 3670016 | tf_op jit(solution)/shard_map/all_to_all | solution.py:24
  185.1 32.6 %collective-permute-start.5 = (bf16[8,256,128]{2,1,0:T(8,128)(2,1)}, bf16[8,256,128]{2,1,0:T(8,128)(2,1)}, u32[]{:S(2)}, u32[]{:S(2)}) collective-permute-start(bf16[8,256,128]{2,1,0:T(8,128)(2,1)} %constant_dynamic-slice_fusion.4), channel_id=1, source_target_pairs={{0,2},{2,0},{1,3},{3,1},{4,6},{6,4},{5,7},{7,5},{8,10},{10,8},{9,1... | collective-permute-start | bytes 1572872 | tf_op jit(solution)/shard_map/ppermute | solution.py:20
  208.9 12.0 %copy-start.13 = (f32[896,128]{1,0:T(8,128)}, f32[896,128]{1,0:T(8,128)S(1)}, u32[]{:S(2)}) copy-start(f32[896,128]{1,0:T(8,128)S(1)} %convert_add_fusion.1) | copy-start | bytes 1376260
  217.7 17.7 %collective-permute-start.6 = (bf16[8,256,128]{2,1,0:T(8,128)(2,1)}, bf16[8,256,128]{2,1,0:T(8,128)(2,1)}, u32[]{:S(2)}, u32[]{:S(2)}) collective-permute-start(bf16[8,256,128]{2,1,0:T(8,128)(2,1)} %collective-permute-done.5), channel_id=1, source_target_pairs={{0,64},{64,0},{1,65},{65,1},{2,66},{66,2},{3,67},{67,3},{4,68},{68... | collective-permute-start | bytes 1572872 | tf_op jit(solution)/shard_map/ppermute | solution.py:20
  221.7 13.6 %all-to-all-start.3 = ((f32[32,7,128]{2,1,0:T(8,128)}), f32[32,7,128]{2,1,0:T(8,128)S(1)}, u32[]{:S(2)}, u32[]{:S(2)}) async-start(f32[32,7,128]{2,1,0:T(8,128)} %broadcast_in_dim.21), calls=%async_computation.3 | async-start | bytes 262144 | tf_op jit(solution)/shard_map/all_to_all | solution.py:24
  236.8 1.5 copy-start.14
  236.8 1.5 copy-start.20
  236.8 1.5 copy-start.25
  236.8 1.5 copy-start.26
  238.3 8.3 %copy-start.12 = (bf16[16,256,128]{2,1,0:T(8,128)(2,1)S(1)}, bf16[16,256,128]{2,1,0:T(8,128)(2,1)}, u32[]{:S(2)}) copy-start(bf16[16,256,128]{2,1,0:T(8,128)(2,1)} %get-tuple-element.48) | copy-start | bytes 3145732
  239.4 21.2 %all-to-all-start.4 = ((bf16[16,64,128]{2,1,0:T(8,128)(2,1)}), bf16[16,64,128]{2,1,0:T(8,128)(2,1)S(1)}, u32[]{:S(2)}, u32[]{:S(2)}) async-start(bf16[16,64,128]{2,1,0:T(8,128)(2,1)} %broadcast_in_dim.22), calls=%async_computation.4 | async-start | bytes 524288 | tf_op jit(solution)/shard_map/all_to_all | solution.py:24
  249.0 2.4 copy-start.16
  251.4 1.3 copy-start.6
  253.5 10.5 %copy-start.8 = (f32[1024,256]{0,1:T(8,128)}, f32[1024,256]{0,1:T(8,128)S(1)}, u32[]{:S(2)}) copy-start(f32[1024,256]{0,1:T(8,128)S(1)} %fusion.128) | copy-start | bytes 3145732
  253.5 10.2 %copy-start.17 = (bf16[1024,128]{0,1:T(8,128)(2,1)S(1)}, bf16[1024,128]{0,1:T(8,128)(2,1)}, u32[]{:S(2)}) copy-start(bf16[1024,128]{0,1:T(8,128)(2,1)} %copy.111) | copy-start | bytes 786436
  253.5 10.2 %copy-start.23 = (pred[32,1024]{1,0:T(32,128)(4,1)S(1)}, pred[32,1024]{1,0:T(32,128)(4,1)}, u32[]{:S(2)}) copy-start(pred[32,1024]{1,0:T(32,128)(4,1)} %get-tuple-element.81) | copy-start | bytes 98308
  253.5 10.2 %copy-start.24 = (pred[32,1024]{1,0:T(32,128)(4,1)S(1)}, pred[32,1024]{1,0:T(32,128)(4,1)}, u32[]{:S(2)}) copy-start(pred[32,1024]{1,0:T(32,128)(4,1)} %get-tuple-element.82) | copy-start | bytes 98308
  260.8 3.3 copy-start.15
  261.3 8.7 %collective-permute-start.7 = (bf16[1024,128]{0,1:T(8,128)(2,1)S(1)}, bf16[1024,128]{0,1:T(8,128)(2,1)}, u32[]{:S(2)}, u32[]{:S(2)}) collective-permute-start(bf16[1024,128]{0,1:T(8,128)(2,1)S(1)} %copy.99), channel_id=1, source_target_pairs={{0,2},{2,0},{1,3},{3,1},{4,6},{6,4},{5,7},{7,5},{8,10},{10,8},{9,1... | collective-permute-start | bytes 786440 | tf_op jit(solution)/shard_map/ppermute | solution.py:20
  270.0 10.7 %collective-permute-start.8 = (bf16[552,1024]{1,0:T(8,128)(2,1)}, bf16[552,1024]{1,0:T(8,128)(2,1)S(1)}, u32[]{:S(2)}, u32[]{:S(2)}) collective-permute-start(bf16[552,1024]{1,0:T(8,128)(2,1)} %fusion.27), channel_id=1, source_target_pairs={{0,64},{64,0},{1,65},{65,1},{2,66},{66,2},{3,67},{67,3},{4,68},{68... | collective-permute-start | bytes 3391496 | tf_op jit(solution)/shard_map/ppermute | solution.py:20
  283.1 21.9 %all-to-all-start.5 = ((bf16[16,40,1024]{2,1,0:T(8,128)(2,1)}), bf16[16,40,1024]{2,1,0:T(8,128)(2,1)S(1)}, u32[]{:S(2)}, u32[]{:S(2)}) async-start(bf16[16,40,1024]{2,1,0:T(8,128)(2,1)} %maximum_maximum_fusion), calls=%async_computation.5 | async-start | bytes 2621440 | tf_op jit(solution)/shard_map/all_to_all | solution.py:24
  287.0 19.6 %copy-start.5 = (bf16[1024,1024]{1,0:T(8,128)(2,1)S(1)}, bf16[1024,1024]{1,0:T(8,128)(2,1)}, u32[]{:S(2)}) copy-start(bf16[1024,1024]{1,0:T(8,128)(2,1)} %pad_maximum_fusion) | copy-start | bytes 6291460
  305.2 0.7 copy-start.19
  331.9 8.3 %collective-permute-start.9 = (bf16[16,40,1024]{2,1,0:T(8,128)(2,1)S(1)}, bf16[16,40,1024]{2,1,0:T(8,128)(2,1)}, u32[]{:S(2)}, u32[]{:S(2)}) collective-permute-start(bf16[16,40,1024]{2,1,0:T(8,128)(2,1)S(1)} %all_to_all.36), channel_id=1, source_target_pairs={{0,64},{64,0},{1,65},{65,1},{2,66},{66,2},{3,67},{67,3},{4,68},{68... | collective-permute-start | bytes 3932168 | tf_op jit(solution)/shard_map/ppermute | solution.py:20
  341.8 3.8 %copy-start.10 = (bf16[16,32,1024]{2,1,0:T(8,128)(2,1)}, bf16[16,32,1024]{2,1,0:T(8,128)(2,1)S(1)}, u32[]{:S(2)}) copy-start(bf16[16,32,1024]{2,1,0:T(8,128)(2,1)S(1)} %slice.183) | copy-start | bytes 3145732
  342.0 1.2 copy-start.11
  347.5 2.5 copy-start.22
  350.0 1.2 copy-start.9
Sparse Core Ops, SparseCore 0:
  10.7 70.1 all-gather.4
  83.0 71.2 all-gather.6

commit v5 on v3

--- a/solution.py
+++ b/solution.py
@@ -61,7 +61,7 @@
             out_specs=pl.BlockSpec((2, tokens, 128), lambda i, c: (i, 0, 0)),
         ),
         out_shape=jax.ShapeDtypeStruct((8, tokens, 128), bf16),
-        compiler_params=pltpu.CompilerParams(vmem_limit_bytes=32 << 20),
+        compiler_params=pltpu.CompilerParams(vmem_limit_bytes=56 << 20),
         cost_estimate=pl.CostEstimate(
             flops=2 * tokens * depth * 1024, bytes_accessed=5_000_000, transcendentals=0
         ),
@@ -138,6 +138,8 @@
     chosen2 = jnp.concatenate([chosen & (student_of == z), chosen & (student_of == 16 + z)]).astype(bf16)
     chosen = (chosen & (student_of == xh * 16 + z)).astype(bf16)
 
+    slabs = weight[:, 896:]
+    far = swap(lax.dynamic_slice_in_dim(slabs, core * 8, 8), "xh")
     part_theirs = swap(parts_for(1 - core, hidden2, weight), "core")
     part_mine = parts_for(core, hidden2, weight)
     pair = (part_mine.astype(f32) + part_theirs.astype(f32)).astype(bf16)
@@ -145,8 +147,7 @@
 
     squares = jnp.sum(y * y, axis=1).reshape(7, 128)
     squares = jnp.sum(share(squares, PLANE, 32), axis=0).reshape(896)
-    squares, slabs = lax.optimization_barrier((squares, weight[:, 896:]))
-    far = swap(lax.dynamic_slice_in_dim(slabs, core * 8, 8), "xh")
+    squares, far = lax.optimization_barrier((squares, far))
     far = jnp.concatenate(ordered(core, far, swap(far, "core")))
     emb = jnp.concatenate(ordered(xh, slabs, far)).reshape(32, 8, 32, 128)
     emb = emb.transpose(0, 2, 1, 3).reshape(1024, 1024)
@@ -160,13 +161,9 @@
     u_own = jnp.where(low, u[:, :128], u[:, 128:])
     uu_hi, uu_lo = two_parts(jnp.sum(u_own * u_own, axis=1))
     first = core * 512 + lax.axis_index(CHIPS) * 32
+    image = jnp.dot(emb, product, preferred_element_type=f32).astype(bf16)
     gram_raw = lax.dot_general(
-        jnp.dot(
-            lax.dynamic_slice_in_dim(emb, first, 32), product, preferred_element_type=f32
-        ).astype(bf16),
-        emb,
-        NT,
-        preferred_element_type=f32,
+        lax.dynamic_slice_in_dim(image, first, 32), emb, NT, preferred_element_type=f32
     )
     image_d = jnp.dot(student_emb, product, preferred_element_type=f32)
 
@@ -207,7 +204,6 @@
         axis=1,
     )
     total = jnp.sum(exchange(pair, CHIPS).astype(f32), axis=0)
-    total, teach_other = lax.optimization_barrier((total, teach_other))
     sum_tt = total[32] + total[33]
     scale_t = 1.0 / (root * jnp.sqrt(sum_tt / D + 1e-06))
     inverse_u = 1.0 / (root * jnp.sqrt((total[34] + total[35]) / D + 1e-06))
@@ -229,6 +225,7 @@
             jnp.pad(jnp.concatenate([in_hi, in_lo])[None], ((0, 5), (0, 960))),
         ]
     )
+    block, teach_other = lax.optimization_barrier((block, teach_other))
     block = share(block, CHIPS, 16)
     even, odd = ordered(core, block, swap(block, "core"))
     diff_b = jnp.concatenate([even[:, :32].reshape(512, 1024), odd[:, :32].reshape(512, 1024)])
@@ -254,9 +251,8 @@
     scale_u_d = jnp.sum(mask * inverse_u[None, :], axis=1, keepdims=True)
     inner_d = jnp.sum(mask * inner[None, :], axis=1, keepdims=True)
     diff_d = jnp.dot(chosen, diff_b, preferred_element_type=f32) * inverse_u[None, :]
-    mixed = jnp.dot(diff_d.astype(bf16), emb, preferred_element_type=f32).astype(bf16)
     student = (
-        4.0 * jnp.dot(mixed, product, preferred_element_type=f32)
+        4.0 * jnp.dot(diff_d.astype(bf16), image, preferred_element_type=f32)
         - scale_t_d * image_t.astype(f32)
         - inner_d * scale_u_d * image_d
     )

time: 282 us -> 293 us (1.039)
  blocking collectives: 65.8 us -> 36.1 us
  starting transfers between devices: 78 us -> 91.7 us
  other arithmetic: 20.5 us -> 30.5 us
  matrix products: 18.7 us -> 25.2 us
  Pallas kernels: 5.58 us -> 11.1 us
    all_to_all x3 -> x2, blocking collectives: 65.8 us -> 36.1 us  [exchange(): return lax.all_to_all(value, axes, split_axis=0, concat_axis=0)]
    all_to_all x4 -> x5, waiting for transfers between devices: 23.4 us -> 42.9 us  [exchange(): return lax.all_to_all(value, axes, split_axis=0, concat_axis=0)]
    ppermute x10, waiting for transfers between devices: 34.9 us -> 18.5 us  [swap(): return lax.ppermute(value, axis, [(0, 1), (1, 0)])]
    ppermute x10, starting transfers between devices: 57.6 us -> 65 us  [swap(): return lax.ppermute(value, axis, [(0, 1), (1, 0)])]
    all_to_all x4 -> x5, starting transfers between devices: 20.4 us -> 26.7 us  [exchange(): return lax.all_to_all(value, axes, split_axis=0, concat_axis=0)]
    pallas_call x2, Pallas kernels: 5.58 us -> 11.1 us  [parts_for(): pl.pallas_call(part_kernel, grid_spec=pltpu.PrefetchScalarGridSpec(num_sc...]
    dot_general x3, matrix products: 6.94 us -> 10 us  [the longest x1 5.27 us: on_device(): image = jnp.dot(emb, product, preferred_element_type=f32).astype(bf16)]
  transfers between devices with their start and end apart: 15 -> 16, of which waited for: 11 -> 11; matrix products, arithmetic and copies ran while one was open for 5% -> 13% of each run, Pallas kernels for 1% -> 2%
where the time goes in v5:
time: 293 us; the launch traced here: 290 us
  starting transfers between devices  91.7 us (31%)
  waiting for transfers between devices  63.6 us (22%)
  blocking collectives  36.1 us (12%)
  other arithmetic  30.5 us (10%)
  matrix products  25.2 us (9%)
  between operations  17.2 us (6%)
  local copies, waits for them, and re-layouts  14.8 us (5%)
  Pallas kernels  11.1 us (4%)
    ppermute x10, starting transfers between devices, swap(): return lax.ppermute(value, axis, [(0, 1), (1, 0)])  65 us
    all_to_all x5, waiting for transfers between devices, exchange(): return lax.all_to_all(value, axes, split_axis=0, concat_axis=0)  42.9 us
    all_to_all x2, blocking collectives, exchange(): return lax.all_to_all(value, axes, split_axis=0, concat_axis=0)  36.1 us
    all_to_all x5, starting transfers between devices, exchange(): return lax.all_to_all(value, axes, split_axis=0, concat_axis=0)  26.7 us
    ppermute x10, waiting for transfers between devices, swap(): return lax.ppermute(value, axis, [(0, 1), (1, 0)])  18.5 us
    pallas_call x2, Pallas kernels, parts_for(): pl.pallas_call(part_kernel, grid_spec=pltpu.PrefetchScalarGridSpec(num_sc...  11.1 us
    select_n x8, other arithmetic, ordered(): return (jnp.where(first, own, other), jnp.where(first, other, own))  6.21 us
  transfers between devices with their start and end apart: 16, of which 11 were waited for; matrix products, arithmetic and copies ran while one was open for 13% of the time, Pallas kernels for 2%

profile of v5, /device:TPU:1, one launch (start us, length us, event | category | flops | bytes accessed | tf_op | source)
XLA Modules:
  0.0 290.3 jit_solution(5829819801619850268)
XLA Ops:
  8.1 1.7 pad_maximum_fusion.9
  12.3 5.5 %collective-permute-start.1 = (bf16[464,128]{1,0:T(8,128)(2,1)S(1)}, bf16[464,128]{1,0:T(8,128)(2,1)S(1)}, u32[]{:S(2)}, u32[]{:S(2)}) collective-permute-start(bf16[464,128]{1,0:T(8,128)(2,1)S(1)} %pad_maximum_fusion.12), channel_id=1, source_target_pairs={{0,2},{2,0},{1,3},{3,1},{4,6},{6,4},{5,7},{7,5},{8,10},{10,8},{9,1... | collective-permute-start | bytes 356360 | tf_op jit(solution)/shard_map/ppermute | solution.py:21
  18.3 5.2 %collective-permute-start = (bf16[512,1024]{1,0:T(8,128)(2,1)S(1)}, bf16[512,1024]{1,0:T(8,128)(2,1)S(1)}, u32[]{:S(2)}, u32[]{:S(2)}) collective-permute-start(bf16[512,1024]{1,0:T(8,128)(2,1)S(1)} %convolution_convert_fusion.4), channel_id=1, source_target_pairs={{0,64},{64,0},{1,65},{65,1},{2,66},{66,2},{3,67},{67,3},{4,68},{68... | collective-permute-start | bytes 3145736 | tf_op jit(solution)/shard_map/ppermute | solution.py:21
  26.2 15.3 %all_to_all.35 = bf16[8,64,1024]{2,1,0:T(8,128)(2,1)S(1)} all-to-all(bf16[8,64,1024]{2,1,0:T(8,128)(2,1)S(1)} %bitcast.100), channel_id=1, replica_groups=mesh['y'=4,'core'=2,'z'=16,'xh'=2,'xl'=2] {'y','xl'}, dimensions={0} | all-to-all | bytes 2097152 | tf_op jit(solution)/shard_map/all_to_all | solution.py:25
  42.8 3.6 %all-to-all-start.1 = ((bf16[8,64,1024]{2,1,0:T(8,128)(2,1)}), bf16[8,64,1024]{2,1,0:T(8,128)(2,1)S(1)}, u32[]{:S(2)}, u32[]{:S(2)}) async-start(bf16[8,64,1024]{2,1,0:T(8,128)(2,1)} %broadcast_in_dim.19), calls=%async_computation.1 | async-start | bytes 2097152 | tf_op jit(solution)/shard_map/all_to_all | solution.py:25
  46.4 7.7 %collective-permute-start.2 = (bf16[448,896]{1,0:T(8,128)(2,1)}, bf16[448,896]{1,0:T(8,128)(2,1)}, u32[]{:S(2)}, u32[]{:S(2)}) collective-permute-start(bf16[448,896]{1,0:T(8,128)(2,1)} %param.8), channel_id=1, source_target_pairs={{0,2},{2,0},{1,3},{3,1},{4,6},{6,4},{5,7},{7,5},{8,10},{10,8},{9,1... | collective-permute-start | bytes 2408456 | tf_op jit(solution)/shard_map/ppermute | solution.py:21
  54.1 4.3 %all-to-all-done.1 = bf16[8,64,1024]{2,1,0:T(8,128)(2,1)S(1)} async-done(((bf16[8,64,1024]{2,1,0:T(8,128)(2,1)}), bf16[8,64,1024]{2,1,0:T(8,128)(2,1)S(1)}, u32[]{:S(2)}, u32[]{:S(2)}) %all-to-all-start.1) | async-done | bytes 1048608 | tf_op jit(solution)/shard_map/all_to_all | solution.py:25
  58.4 10.7 %collective-permute-start.3 = (bf16[512,1024]{1,0:T(8,128)(2,1)S(1)}, bf16[512,1024]{1,0:T(8,128)(2,1)S(1)}, u32[]{:S(2)}, u32[]{:S(2)}) collective-permute-start(bf16[512,1024]{1,0:T(8,128)(2,1)S(1)} %bitcast.92), channel_id=1, source_target_pairs={{0,64},{64,0},{1,65},{65,1},{2,66},{66,2},{3,67},{67,3},{4,68},{68... | collective-permute-start | bytes 3145736 | tf_op jit(solution)/shard_map/ppermute | solution.py:21
  69.1 11.6 %collective-permute-done.2 = bf16[448,896]{1,0:T(8,128)(2,1)} collective-permute-done((bf16[448,896]{1,0:T(8,128)(2,1)}, bf16[448,896]{1,0:T(8,128)(2,1)}, u32[]{:S(2)}, u32[]{:S(2)}) %collective-permute-start.2) | collective-permute-done | bytes 802848 | tf_op jit(solution)/shard_map/ppermute | solution.py:21
  80.7 1.6 broadcast_select_fusion.7
  83.8 1.6 pad_maximum_fusion
  85.3 2.1 all-gather.3.cloned.1.call-done
  87.5 5.6 %shard_map.104 = bf16[8,896,128]{2,1,0:T(8,128)(2,1)} custom-call(s32[1]{0:T(128)} %bitcast.10.core_ref, bf16[896,896]{1,0:T(8,128)(2,1)} %pad_maximum_fusion.3.hidden_ref, bf16[16,1152,128]{2,1,0:T(8,128)(2,1)} %bitcast.83), custom_call_target="tpu_custom_call" | custom-call | flops 1644167168 | bytes 5000000 | tf_op jit(solution)/shard_map/pallas_call | solution.py:52
  93.0 10.0 %collective-permute-start.4 = (bf16[8,896,128]{2,1,0:T(8,128)(2,1)}, bf16[8,896,128]{2,1,0:T(8,128)(2,1)S(1)}, u32[]{:S(2)}, u32[]{:S(2)}) collective-permute-start(bf16[8,896,128]{2,1,0:T(8,128)(2,1)} %shard_map.104), channel_id=1, source_target_pairs={{0,64},{64,0},{1,65},{65,1},{2,66},{66,2},{3,67},{67,3},{4,68},{68... | collective-permute-start | bytes 5505032 | tf_op jit(solution)/shard_map/ppermute | solution.py:21
  103.0 5.6 %shard_map.103 = bf16[8,896,128]{2,1,0:T(8,128)(2,1)} custom-call(s32[1]{0:T(128)} %bitcast.3.core_ref, bf16[896,896]{1,0:T(8,128)(2,1)} %pad_maximum_fusion.3.hidden_ref, bf16[16,1152,128]{2,1,0:T(8,128)(2,1)} %bitcast.84), custom_call_target="tpu_custom_call" | custom-call | flops 1644167168 | bytes 5000000 | tf_op jit(solution)/shard_map/pallas_call | solution.py:52
  108.6 3.3 %add_convert_fusion = bf16[8,896,128]{2,1,0:T(8,128)(2,1)} fusion(bf16[8,896,128]{2,1,0:T(8,128)(2,1)S(1)} %collective-permute-done.4, bf16[8,896,128]{2,1,0:T(8,128)(2,1)} %shard_map.103), kind=kLoop, calls=%fused_computation.4 | loop fusion | flops 3670016 | bytes 5505024 | tf_op jit(solution)/shard_map/convert_element_type | solution.py:145
  111.9 5.2 %all-to-all-start.2 = ((bf16[8,896,128]{2,1,0:T(8,128)(2,1)}), bf16[8,896,128]{2,1,0:T(8,128)(2,1)S(1)}, u32[]{:S(2)}, u32[]{:S(2)}) async-start(bf16[8,896,128]{2,1,0:T(8,128)(2,1)} %add_convert_fusion), calls=%async_computation.2 | async-start | bytes 3670016 | tf_op jit(solution)/shard_map/all_to_all | solution.py:25
  120.0 4.4 %collective-permute-start.5 = (bf16[8,256,128]{2,1,0:T(8,128)(2,1)}, bf16[8,256,128]{2,1,0:T(8,128)(2,1)}, u32[]{:S(2)}, u32[]{:S(2)}) collective-permute-start(bf16[8,256,128]{2,1,0:T(8,128)(2,1)} %constant_dynamic-slice_fusion.4), channel_id=1, source_target_pairs={{0,2},{2,0},{1,3},{3,1},{4,6},{6,4},{5,7},{7,5},{8,10},{10,8},{9,1... | collective-permute-start | bytes 1572872 | tf_op jit(solution)/shard_map/ppermute | solution.py:21
  124.4 16.7 %all-to-all-done.2 = bf16[8,896,128]{2,1,0:T(8,128)(2,1)S(1)} async-done(((bf16[8,896,128]{2,1,0:T(8,128)(2,1)}), bf16[8,896,128]{2,1,0:T(8,128)(2,1)S(1)}, u32[]{:S(2)}, u32[]{:S(2)}) %all-to-all-start.2) | async-done | bytes 1835040 | tf_op jit(solution)/shard_map/all_to_all | solution.py:25
  142.2 6.9 %all-to-all-start.3 = ((f32[32,7,128]{2,1,0:T(8,128)}), f32[32,7,128]{2,1,0:T(8,128)S(1)}, u32[]{:S(2)}, u32[]{:S(2)}) async-start(f32[32,7,128]{2,1,0:T(8,128)} %broadcast_in_dim.21), calls=%async_computation.3 | async-start | bytes 262144 | tf_op jit(solution)/shard_map/all_to_all | solution.py:25
  149.1 7.6 %all-to-all-done.3 = f32[32,7,128]{2,1,0:T(8,128)S(1)} async-done(((f32[32,7,128]{2,1,0:T(8,128)}), f32[32,7,128]{2,1,0:T(8,128)S(1)}, u32[]{:S(2)}, u32[]{:S(2)}) %all-to-all-start.3) | async-done | bytes 114720 | tf_op jit(solution)/shard_map/all_to_all | solution.py:25
  156.8 2.2 collective-permute-start.6
  160.2 1.8 copy.111
  163.8 6.6 %all-to-all-start.4 = ((bf16[16,64,128]{2,1,0:T(8,128)(2,1)}), bf16[16,64,128]{2,1,0:T(8,128)(2,1)S(1)}, u32[]{:S(2)}, u32[]{:S(2)}) async-start(bf16[16,64,128]{2,1,0:T(8,128)(2,1)} %broadcast_in_dim.22), calls=%async_computation.4 | async-start | bytes 524288 | tf_op jit(solution)/shard_map/all_to_all | solution.py:25
  174.1 2.4 fusion.5
  176.5 1.7 fusion.128
  178.2 6.3 %all-to-all-done.4 = bf16[16,64,128]{2,1,0:T(8,128)(2,1)S(1)} async-done(((bf16[16,64,128]{2,1,0:T(8,128)(2,1)}), bf16[16,64,128]{2,1,0:T(8,128)(2,1)S(1)}, u32[]{:S(2)}, u32[]{:S(2)}) %all-to-all-start.4) | async-done | bytes 262176 | tf_op jit(solution)/shard_map/all_to_all | solution.py:25
  184.5 1.4 convolution_convert_fusion.1
  188.2 2.3 fusion.20
  190.5 6.9 %collective-permute-start.7 = (bf16[552,1024]{1,0:T(8,128)(2,1)}, bf16[552,1024]{1,0:T(8,128)(2,1)}, u32[]{:S(2)}, u32[]{:S(2)}) collective-permute-start(bf16[552,1024]{1,0:T(8,128)(2,1)} %fusion.20), channel_id=1, source_target_pairs={{0,64},{64,0},{1,65},{65,1},{2,66},{66,2},{3,67},{67,3},{4,68},{68... | collective-permute-start | bytes 3391496 | tf_op jit(solution)/shard_map/ppermute | solution.py:21
  198.0 2.2 collective-permute-done.7
  200.2 1.8 convert_add_fusion
  203.2 2.8 maximum_maximum_fusion
  206.0 4.4 %all-to-all-start.5 = ((bf16[16,40,1024]{2,1,0:T(8,128)(2,1)}), bf16[16,40,1024]{2,1,0:T(8,128)(2,1)}, u32[]{:S(2)}, u32[]{:S(2)}) async-start(bf16[16,40,1024]{2,1,0:T(8,128)(2,1)} %maximum_maximum_fusion), calls=%async_computation.5 | async-start | bytes 2621440 | tf_op jit(solution)/shard_map/all_to_all | solution.py:25
  210.4 5.3 %convolution_convert_fusion = bf16[1024,1024]{1,0:T(8,128)(2,1)} fusion(bf16[1024,1024]{1,0:T(8,128)(2,1)S(1)} %fusion.5, bf16[1024,1024]{1,0:T(8,128)(2,1)} %pad_maximum_fusion), kind=kOutput, calls=%fused_computation.17 | convolution fusion | flops 2148532224 | bytes 6291456 | tf_op jit(solution)/shard_map/dot_general | solution.py:164
  215.7 4.7 %collective-permute-start.8 = (bf16[1024,128]{0,1:T(8,128)(2,1)S(1)}, bf16[1024,128]{0,1:T(8,128)(2,1)S(1)}, u32[]{:S(2)}, u32[]{:S(2)}) collective-permute-start(bf16[1024,128]{0,1:T(8,128)(2,1)S(1)} %copy.99), channel_id=1, source_target_pairs={{0,2},{2,0},{1,3},{3,1},{4,6},{6,4},{5,7},{7,5},{8,10},{10,8},{9,1... | collective-permute-start | bytes 786440 | tf_op jit(solution)/shard_map/ppermute | solution.py:21
  220.4 8.0 %all-to-all-done.5 = bf16[16,40,1024]{2,1,0:T(8,128)(2,1)} async-done(((bf16[16,40,1024]{2,1,0:T(8,128)(2,1)}), bf16[16,40,1024]{2,1,0:T(8,128)(2,1)}, u32[]{:S(2)}, u32[]{:S(2)}) %all-to-all-start.5) | async-done | bytes 1310752 | tf_op jit(solution)/shard_map/all_to_all | solution.py:25
  228.4 1.6 convert_reduce_fusion.1
  230.8 1.7 multiply_reduce_fusion.5
  232.7 1.6 collective-permute-done.8
  234.4 20.8 %all_to_all.36 = bf16[16,40,1024]{2,1,0:T(8,128)(2,1)} all-to-all(bf16[16,40,1024]{2,1,0:T(8,128)(2,1)S(1)} %broadcast_in_dim.26), channel_id=1, replica_groups=mesh['y'=4,'core'=2,'z'=16,'xh'=2,'xl'=2] {'y','xl','xh'}, dimensions={0} | all-to-all | bytes 2621440 | tf_op jit(solution)/shard_map/all_to_all | solution.py:25
  255.3 7.8 %collective-permute-start.9 = (bf16[16,40,1024]{2,1,0:T(8,128)(2,1)}, bf16[16,40,1024]{2,1,0:T(8,128)(2,1)}, u32[]{:S(2)}, u32[]{:S(2)}) collective-permute-start(bf16[16,40,1024]{2,1,0:T(8,128)(2,1)} %all_to_all.36), channel_id=1, source_target_pairs={{0,64},{64,0},{1,65},{65,1},{2,66},{66,2},{3,67},{67,3},{4,68},{68... | collective-permute-start | bytes 3932168 | tf_op jit(solution)/shard_map/ppermute | solution.py:21
  263.7 2.1 collective-permute-done.9
  265.8 1.9 broadcast_select_fusion.1
  269.1 1.7 multiply_reduce_fusion
  271.8 3.1 %fusion.17 = f32[32,1024]{1,0:T(8,128)S(1)} fusion(bf16[1024,1024]{1,0:T(8,128)(2,1)} %convolution_convert_fusion, bf16[512,1024]{1,0:T(8,128)(2,1)} %bitcast.94, bf16[512,1024]{1,0:T(8,128)(2,1)} %bitcast.97, bf16[32,512]{1,0:T(8,128)(2,1)S(1)} %reshape.375, bf16[32,512]{1,0:T(8,128)(2,1)S(1)} %reshape.374, f32[32]{0:T(128)S(1)} %get-tuple-element.28, ...), kind=kOutput, calls=%fused_computation.39 | convolution fusion | flops 138772480 | bytes 4400256 | tf_op jit(solution)/shard_map/dot_general | solution.py:255
  274.9 2.7 fusion.16
  277.6 4.7 %fusion.23 = f32[1024,256]{1,0:T(8,128)} fusion(bf16[1024,1024]{1,0:T(8,128)(2,1)S(1)} %fusion.5, f32[1024,256]{0,1:T(8,128)} %fusion.128, bf16[512,1024]{1,0:T(8,128)(2,1)} %bitcast.95, bf16[512,1024]{1,0:T(8,128)(2,1)} %bitcast.98, bf16[1024,128]{0,1:T(8,128)(2,1)S(1)} %get-tuple-element.59, bf16[1024,128]{0,1:T(8,128)(2,1)S(1)} %get-tuple-element.58, ...), kind=kOutput, calls=%fused_computation.55 | convolution fusion | flops 1081868288 | bytes 6828032 | tf_op jit(solution)/shard_map/dot_general | solution.py:247
  (117 shorter events, 26.8 us)
Async XLA Ops:
  7.2 10.6 %copy-start = (bf16[1024,256]{1,0:T(8,128)(2,1)S(1)}, bf16[1024,256]{1,0:T(8,128)(2,1)}, u32[]{:S(2)}) copy-start(bf16[1024,256]{1,0:T(8,128)(2,1)} %param.15) | copy-start | bytes 1572868
  7.2 80.3 %all-gather.3.cloned.1.call-start = ((), (), s32[]{:S(2)}) async-start(), calls=%async_computation.7 | async-start | bytes 5013504 | tf_op jit(solution)/shard_map/all_gather | solution.py:80
  9.8 14.8 %copy-start.3 = (bf16[448,256]{1,0:T(8,128)(2,1)S(1)}, bf16[448,256]{1,0:T(8,128)(2,1)}, u32[]{:S(2)}) copy-start(bf16[448,256]{1,0:T(8,128)(2,1)} %param.9) | copy-start | bytes 688132
  12.3 11.2 %collective-permute-start.1 = (bf16[464,128]{1,0:T(8,128)(2,1)S(1)}, bf16[464,128]{1,0:T(8,128)(2,1)S(1)}, u32[]{:S(2)}, u32[]{:S(2)}) collective-permute-start(bf16[464,128]{1,0:T(8,128)(2,1)S(1)} %pad_maximum_fusion.12), channel_id=1, source_target_pairs={{0,2},{2,0},{1,3},{3,1},{4,6},{6,4},{5,7},{7,5},{8,10},{10,8},{9,1... | collective-permute-start | bytes 356360 | tf_op jit(solution)/shard_map/ppermute | solution.py:21
  18.3 7.5 %collective-permute-start = (bf16[512,1024]{1,0:T(8,128)(2,1)S(1)}, bf16[512,1024]{1,0:T(8,128)(2,1)S(1)}, u32[]{:S(2)}, u32[]{:S(2)}) collective-permute-start(bf16[512,1024]{1,0:T(8,128)(2,1)S(1)} %convolution_convert_fusion.4), channel_id=1, source_target_pairs={{0,64},{64,0},{1,65},{65,1},{2,66},{66,2},{3,67},{67,3},{4,68},{68... | collective-permute-start | bytes 3145736 | tf_op jit(solution)/shard_map/ppermute | solution.py:21
  42.8 15.6 %all-to-all-start.1 = ((bf16[8,64,1024]{2,1,0:T(8,128)(2,1)}), bf16[8,64,1024]{2,1,0:T(8,128)(2,1)S(1)}, u32[]{:S(2)}, u32[]{:S(2)}) async-start(bf16[8,64,1024]{2,1,0:T(8,128)(2,1)} %broadcast_in_dim.19), calls=%async_computation.1 | async-start | bytes 2097152 | tf_op jit(solution)/shard_map/all_to_all | solution.py:25
  46.4 34.3 %collective-permute-start.2 = (bf16[448,896]{1,0:T(8,128)(2,1)}, bf16[448,896]{1,0:T(8,128)(2,1)}, u32[]{:S(2)}, u32[]{:S(2)}) collective-permute-start(bf16[448,896]{1,0:T(8,128)(2,1)} %param.8), channel_id=1, source_target_pairs={{0,2},{2,0},{1,3},{3,1},{4,6},{6,4},{5,7},{7,5},{8,10},{10,8},{9,1... | collective-permute-start | bytes 2408456 | tf_op jit(solution)/shard_map/ppermute | solution.py:21
  58.4 25.1 %collective-permute-start.3 = (bf16[512,1024]{1,0:T(8,128)(2,1)S(1)}, bf16[512,1024]{1,0:T(8,128)(2,1)S(1)}, u32[]{:S(2)}, u32[]{:S(2)}) collective-permute-start(bf16[512,1024]{1,0:T(8,128)(2,1)S(1)} %bitcast.92), channel_id=1, source_target_pairs={{0,64},{64,0},{1,65},{65,1},{2,66},{66,2},{3,67},{67,3},{4,68},{68... | collective-permute-start | bytes 3145736 | tf_op jit(solution)/shard_map/ppermute | solution.py:21
  93.0 15.6 %collective-permute-start.4 = (bf16[8,896,128]{2,1,0:T(8,128)(2,1)}, bf16[8,896,128]{2,1,0:T(8,128)(2,1)S(1)}, u32[]{:S(2)}, u32[]{:S(2)}) collective-permute-start(bf16[8,896,128]{2,1,0:T(8,128)(2,1)} %shard_map.104), channel_id=1, source_target_pairs={{0,64},{64,0},{1,65},{65,1},{2,66},{66,2},{3,67},{67,3},{4,68},{68... | collective-permute-start | bytes 5505032 | tf_op jit(solution)/shard_map/ppermute | solution.py:21
  111.9 29.2 %all-to-all-start.2 = ((bf16[8,896,128]{2,1,0:T(8,128)(2,1)}), bf16[8,896,128]{2,1,0:T(8,128)(2,1)S(1)}, u32[]{:S(2)}, u32[]{:S(2)}) async-start(bf16[8,896,128]{2,1,0:T(8,128)(2,1)} %add_convert_fusion), calls=%async_computation.2 | async-start | bytes 3670016 | tf_op jit(solution)/shard_map/all_to_all | solution.py:25
  120.0 36.8 %collective-permute-start.5 = (bf16[8,256,128]{2,1,0:T(8,128)(2,1)}, bf16[8,256,128]{2,1,0:T(8,128)(2,1)}, u32[]{:S(2)}, u32[]{:S(2)}) collective-permute-start(bf16[8,256,128]{2,1,0:T(8,128)(2,1)} %constant_dynamic-slice_fusion.4), channel_id=1, source_target_pairs={{0,2},{2,0},{1,3},{3,1},{4,6},{6,4},{5,7},{7,5},{8,10},{10,8},{9,1... | collective-permute-start | bytes 1572872 | tf_op jit(solution)/shard_map/ppermute | solution.py:21
  142.2 14.5 %all-to-all-start.3 = ((f32[32,7,128]{2,1,0:T(8,128)}), f32[32,7,128]{2,1,0:T(8,128)S(1)}, u32[]{:S(2)}, u32[]{:S(2)}) async-start(f32[32,7,128]{2,1,0:T(8,128)} %broadcast_in_dim.21), calls=%async_computation.3 | async-start | bytes 262144 | tf_op jit(solution)/shard_map/all_to_all | solution.py:25
  156.8 13.6 %collective-permute-start.6 = (bf16[8,256,128]{2,1,0:T(8,128)(2,1)}, bf16[8,256,128]{2,1,0:T(8,128)(2,1)S(1)}, u32[]{:S(2)}, u32[]{:S(2)}) collective-permute-start(bf16[8,256,128]{2,1,0:T(8,128)(2,1)} %collective-permute-done.5), channel_id=1, source_target_pairs={{0,64},{64,0},{1,65},{65,1},{2,66},{66,2},{3,67},{67,3},{4,68},{68... | collective-permute-start | bytes 1572872 | tf_op jit(solution)/shard_map/ppermute | solution.py:21
  163.8 20.7 %all-to-all-start.4 = ((bf16[16,64,128]{2,1,0:T(8,128)(2,1)}), bf16[16,64,128]{2,1,0:T(8,128)(2,1)S(1)}, u32[]{:S(2)}, u32[]{:S(2)}) async-start(bf16[16,64,128]{2,1,0:T(8,128)(2,1)} %broadcast_in_dim.22), calls=%async_computation.4 | async-start | bytes 524288 | tf_op jit(solution)/shard_map/all_to_all | solution.py:25
  190.5 9.7 %collective-permute-start.7 = (bf16[552,1024]{1,0:T(8,128)(2,1)}, bf16[552,1024]{1,0:T(8,128)(2,1)}, u32[]{:S(2)}, u32[]{:S(2)}) collective-permute-start(bf16[552,1024]{1,0:T(8,128)(2,1)} %fusion.20), channel_id=1, source_target_pairs={{0,64},{64,0},{1,65},{65,1},{2,66},{66,2},{3,67},{67,3},{4,68},{68... | collective-permute-start | bytes 3391496 | tf_op jit(solution)/shard_map/ppermute | solution.py:21
  206.0 22.4 %all-to-all-start.5 = ((bf16[16,40,1024]{2,1,0:T(8,128)(2,1)}), bf16[16,40,1024]{2,1,0:T(8,128)(2,1)}, u32[]{:S(2)}, u32[]{:S(2)}) async-start(bf16[16,40,1024]{2,1,0:T(8,128)(2,1)} %maximum_maximum_fusion), calls=%async_computation.5 | async-start | bytes 2621440 | tf_op jit(solution)/shard_map/all_to_all | solution.py:25
  215.7 18.6 %collective-permute-start.8 = (bf16[1024,128]{0,1:T(8,128)(2,1)S(1)}, bf16[1024,128]{0,1:T(8,128)(2,1)S(1)}, u32[]{:S(2)}, u32[]{:S(2)}) collective-permute-start(bf16[1024,128]{0,1:T(8,128)(2,1)S(1)} %copy.99), channel_id=1, source_target_pairs={{0,2},{2,0},{1,3},{3,1},{4,6},{6,4},{5,7},{7,5},{8,10},{10,8},{9,1... | collective-permute-start | bytes 786440 | tf_op jit(solution)/shard_map/ppermute | solution.py:21
  255.3 10.5 %collective-permute-start.9 = (bf16[16,40,1024]{2,1,0:T(8,128)(2,1)}, bf16[16,40,1024]{2,1,0:T(8,128)(2,1)}, u32[]{:S(2)}, u32[]{:S(2)}) collective-permute-start(bf16[16,40,1024]{2,1,0:T(8,128)(2,1)} %all_to_all.36), channel_id=1, source_target_pairs={{0,64},{64,0},{1,65},{65,1},{2,66},{66,2},{3,67},{67,3},{4,68},{68... | collective-permute-start | bytes 3932168 | tf_op jit(solution)/shard_map/ppermute | solution.py:21
  267.8 1.0 copy-start.1
  268.0 1.1 copy-start.2
  271.8 3.1 %copy-start.4 = (bf16[32,1024]{1,0:T(8,128)(2,1)S(1)}, bf16[32,1024]{1,0:T(8,128)(2,1)}, u32[]{:S(2)}) copy-start(bf16[32,1024]{1,0:T(8,128)(2,1)} %param.14) | copy-start | bytes 196612
Sparse Core Ops, SparseCore 0:
  10.1 77.3 all-gather.2

commit v6 on v5

--- a/solution.py
+++ b/solution.py
@@ -32,6 +32,10 @@
 def two_parts(value):
     high = lax.reduce_precision(value, 8, 7)
     return high.astype(bf16), (value - high).astype(bf16)
+
+
+def slab_rows(slabs):
+    return slabs.reshape(-1, 8, 32, 128).transpose(0, 2, 1, 3).reshape(-1, 1024)
 
 
 def ordered(index, own, other):
@@ -61,7 +65,7 @@
             out_specs=pl.BlockSpec((2, tokens, 128), lambda i, c: (i, 0, 0)),
         ),
         out_shape=jax.ShapeDtypeStruct((8, tokens, 128), bf16),
-        compiler_params=pltpu.CompilerParams(vmem_limit_bytes=56 << 20),
+        compiler_params=pltpu.CompilerParams(vmem_limit_bytes=32 << 20),
         cost_estimate=pl.CostEstimate(
             flops=2 * tokens * depth * 1024, bytes_accessed=5_000_000, transcendentals=0
         ),
@@ -133,7 +137,12 @@
     place = pick // 2 % 32
     chosen = (pick // 64 * 2 + pick % 2)[None, :] == jnp.arange(32, dtype=jnp.int32)[:, None]
     student_of = place[None, :]
-    source = place * 32 + pick // 64 * 2 + pick % 2
+    block = jnp.where(
+        place // 16 == xh,
+        place % 16,
+        place % 8 + jnp.where(place % 16 // 8 == core, 16, 24),
+    )
+    source = block * 32 + pick // 64 * 2 + pick % 2
     order = (source[:, None] == pick[None, :]).astype(bf16)
     chosen2 = jnp.concatenate([chosen & (student_of == z), chosen & (student_of == 16 + z)]).astype(bf16)
     chosen = (chosen & (student_of == xh * 16 + z)).astype(bf16)
@@ -145,12 +154,11 @@
     pair = (part_mine.astype(f32) + part_theirs.astype(f32)).astype(bf16)
     y = jnp.sum(exchange(pair, HALF).astype(f32), axis=0) + residual2.astype(f32)
 
+    y, near = lax.optimization_barrier((y, slab_rows(slabs)))
     squares = jnp.sum(y * y, axis=1).reshape(7, 128)
     squares = jnp.sum(share(squares, PLANE, 32), axis=0).reshape(896)
     squares, far = lax.optimization_barrier((squares, far))
-    far = jnp.concatenate(ordered(core, far, swap(far, "core")))
-    emb = jnp.concatenate(ordered(xh, slabs, far)).reshape(32, 8, 32, 128)
-    emb = emb.transpose(0, 2, 1, 3).reshape(1024, 1024)
+    emb = jnp.concatenate([near, slab_rows(far), slab_rows(swap(far, "core"))])
     normed = (y * lax.rsqrt(squares / D + 1e-05)[:, None] * gain).astype(bf16)
     pooled = (jnp.dot(pool, normed, preferred_element_type=f32) / count).astype(bf16)
     teach = share(pooled, "z", 16).reshape(1024, 128)

time: 293 us -> 287 us (0.980)
  Pallas kernels: 11.1 us -> 5.58 us
  blocking collectives: 36.1 us -> 41 us
  other arithmetic: 30.5 us -> 25.7 us
    pallas_call x2, Pallas kernels: 11.1 us -> 5.58 us  [parts_for(): pl.pallas_call(part_kernel, grid_spec=pltpu.PrefetchScalarGridSpec(num_sc...]
    all_to_all x2, blocking collectives: 36.1 us -> 41 us  [exchange(): return lax.all_to_all(value, axes, split_axis=0, concat_axis=0)]
    select_n x8 -> x6, other arithmetic: 6.21 us -> 3.48 us  [ordered(): return (jnp.where(first, own, other), jnp.where(first, other, own))]
    unnamed x17 -> x28, local copies, waits for them, and re-layouts: 4.75 us -> 5.97 us
  transfers between devices with their start and end apart: 16 -> 16, of which waited for: 11 -> 12; matrix products, arithmetic and copies ran while one was open for 13% -> 11% of each run, Pallas kernels for 2% -> 1%
where the time goes in v6:
time: 287 us; the launch traced here: 286 us
  starting transfers between devices  90.7 us (32%)
  waiting for transfers between devices  64.2 us (22%)
  blocking collectives  41 us (14%)
  other arithmetic  25.7 us (9%)
  matrix products  25.2 us (9%)
  between operations  17.3 us (6%)
  local copies, waits for them, and re-layouts  16.2 us (6%)
  Pallas kernels  5.58 us (2%)
    ppermute x10, starting transfers between devices, swap(): return lax.ppermute(value, axis, [(0, 1), (1, 0)])  63.5 us
    all_to_all x2, blocking collectives, exchange(): return lax.all_to_all(value, axes, split_axis=0, concat_axis=0)  41 us
    all_to_all x5, waiting for transfers between devices, exchange(): return lax.all_to_all(value, axes, split_axis=0, concat_axis=0)  40.8 us
    all_to_all x5, starting transfers between devices, exchange(): return lax.all_to_all(value, axes, split_axis=0, concat_axis=0)  27.2 us
    ppermute x10, waiting for transfers between devices, swap(): return lax.ppermute(value, axis, [(0, 1), (1, 0)])  19.6 us
    unnamed x28, local copies, waits for them, and re-layouts  5.97 us
  transfers between devices with their start and end apart: 16, of which 12 were waited for; matrix products, arithmetic and copies ran while one was open for 11% of the time, Pallas kernels for 1%

profile of v6, /device:TPU:1, one launch (start us, length us, event | category | flops | bytes accessed | tf_op | source)
XLA Modules:
  0.0 286.0 jit_solution(4514272373741099386)
XLA Ops:
  8.1 1.7 pad_maximum_fusion.7
  12.3 5.5 %collective-permute-start.1 = (bf16[464,128]{1,0:T(8,128)(2,1)S(1)}, bf16[464,128]{1,0:T(8,128)(2,1)S(1)}, u32[]{:S(2)}, u32[]{:S(2)}) collective-permute-start(bf16[464,128]{1,0:T(8,128)(2,1)S(1)} %pad_maximum_fusion.10), channel_id=1, source_target_pairs={{0,2},{2,0},{1,3},{3,1},{4,6},{6,4},{5,7},{7,5},{8,10},{10,8},{9,1... | collective-permute-start | bytes 356360 | tf_op jit(solution)/shard_map/ppermute | solution.py:21
  18.3 5.2 %collective-permute-start = (bf16[512,1024]{1,0:T(8,128)(2,1)S(1)}, bf16[512,1024]{1,0:T(8,128)(2,1)S(1)}, u32[]{:S(2)}, u32[]{:S(2)}) collective-permute-start(bf16[512,1024]{1,0:T(8,128)(2,1)S(1)} %convolution_convert_fusion.4), channel_id=1, source_target_pairs={{0,64},{64,0},{1,65},{65,1},{2,66},{66,2},{3,67},{67,3},{4,68},{68... | collective-permute-start | bytes 3145736 | tf_op jit(solution)/shard_map/ppermute | solution.py:21
  26.3 14.4 %all_to_all.35 = bf16[8,64,1024]{2,1,0:T(8,128)(2,1)S(1)} all-to-all(bf16[8,64,1024]{2,1,0:T(8,128)(2,1)S(1)} %bitcast.111), channel_id=1, replica_groups=mesh['y'=4,'core'=2,'z'=16,'xh'=2,'xl'=2] {'y','xl'}, dimensions={0} | all-to-all | bytes 2097152 | tf_op jit(solution)/shard_map/all_to_all | solution.py:25
  42.0 3.6 %all-to-all-start.1 = ((bf16[8,64,1024]{2,1,0:T(8,128)(2,1)}), bf16[8,64,1024]{2,1,0:T(8,128)(2,1)S(1)}, u32[]{:S(2)}, u32[]{:S(2)}) async-start(bf16[8,64,1024]{2,1,0:T(8,128)(2,1)} %broadcast_in_dim.26), calls=%async_computation.1 | async-start | bytes 2097152 | tf_op jit(solution)/shard_map/all_to_all | solution.py:25
  45.5 8.6 %collective-permute-start.2 = (bf16[448,896]{1,0:T(8,128)(2,1)S(1)}, bf16[448,896]{1,0:T(8,128)(2,1)S(1)}, u32[]{:S(2)}, u32[]{:S(2)}) collective-permute-start(bf16[448,896]{1,0:T(8,128)(2,1)S(1)} %copy-done.7), channel_id=1, source_target_pairs={{0,2},{2,0},{1,3},{3,1},{4,6},{6,4},{5,7},{7,5},{8,10},{10,8},{9,1... | collective-permute-start | bytes 2408456 | tf_op jit(solution)/shard_map/ppermute | solution.py:21
  54.2 2.2 all-to-all-done.1
  56.3 11.2 %collective-permute-start.3 = (bf16[512,1024]{1,0:T(8,128)(2,1)S(1)}, bf16[512,1024]{1,0:T(8,128)(2,1)}, u32[]{:S(2)}, u32[]{:S(2)}) collective-permute-start(bf16[512,1024]{1,0:T(8,128)(2,1)S(1)} %bitcast.103), channel_id=1, source_target_pairs={{0,64},{64,0},{1,65},{65,1},{2,66},{66,2},{3,67},{67,3},{4,68},{68... | collective-permute-start | bytes 3145736 | tf_op jit(solution)/shard_map/ppermute | solution.py:21
  67.5 13.1 %collective-permute-done.2 = bf16[448,896]{1,0:T(8,128)(2,1)S(1)} collective-permute-done((bf16[448,896]{1,0:T(8,128)(2,1)S(1)}, bf16[448,896]{1,0:T(8,128)(2,1)S(1)}, u32[]{:S(2)}, u32[]{:S(2)}) %collective-permute-start.2) | collective-permute-done | bytes 802848 | tf_op jit(solution)/shard_map/ppermute | solution.py:21
  80.9 1.4 broadcast_select_fusion.3
  82.3 1.5 pad_maximum_fusion
  83.9 3.7 %all-gather.3.cloned.1.call-done = bf16[18432,128]{1,0:T(8,128)(2,1)} async-done(((bf16[1152,128]{1,0:T(8,128)(2,1)}), bf16[18432,128]{1,0:T(8,128)(2,1)}) %all-gather.3.cloned.1.call-update) | async-done | bytes 4718608 | tf_op jit(solution)/shard_map/all_gather | solution.py:84
  87.6 2.3 copy-done
  89.9 2.8 shard_map.104
  92.7 10.2 %collective-permute-start.4 = (bf16[8,896,128]{2,1,0:T(8,128)(2,1)S(1)}, bf16[8,896,128]{2,1,0:T(8,128)(2,1)S(1)}, u32[]{:S(2)}, u32[]{:S(2)}) collective-permute-start(bf16[8,896,128]{2,1,0:T(8,128)(2,1)S(1)} %shard_map.104), channel_id=1, source_target_pairs={{0,64},{64,0},{1,65},{65,1},{2,66},{66,2},{3,67},{67,3},{4,68},{68... | collective-permute-start | bytes 5505032 | tf_op jit(solution)/shard_map/ppermute | solution.py:21
  102.9 2.8 shard_map.103
  106.3 1.8 add_convert_fusion
  108.1 5.2 %all-to-all-start.2 = ((bf16[8,896,128]{2,1,0:T(8,128)(2,1)}), bf16[8,896,128]{2,1,0:T(8,128)(2,1)S(1)}, u32[]{:S(2)}, u32[]{:S(2)}) async-start(bf16[8,896,128]{2,1,0:T(8,128)(2,1)} %add_convert_fusion), calls=%async_computation.2 | async-start | bytes 3670016 | tf_op jit(solution)/shard_map/all_to_all | solution.py:25
  118.2 4.2 %collective-permute-start.5 = (bf16[8,256,128]{2,1,0:T(8,128)(2,1)}, bf16[8,256,128]{2,1,0:T(8,128)(2,1)}, u32[]{:S(2)}, u32[]{:S(2)}) collective-permute-start(bf16[8,256,128]{2,1,0:T(8,128)(2,1)} %constant_dynamic-slice_fusion.4), channel_id=1, source_target_pairs={{0,2},{2,0},{1,3},{3,1},{4,6},{6,4},{5,7},{7,5},{8,10},{10,8},{9,1... | collective-permute-start | bytes 1572872 | tf_op jit(solution)/shard_map/ppermute | solution.py:21
  122.4 14.4 %all-to-all-done.2 = bf16[8,896,128]{2,1,0:T(8,128)(2,1)S(1)} async-done(((bf16[8,896,128]{2,1,0:T(8,128)(2,1)}), bf16[8,896,128]{2,1,0:T(8,128)(2,1)S(1)}, u32[]{:S(2)}, u32[]{:S(2)}) %all-to-all-start.2) | async-done | bytes 1835040 | tf_op jit(solution)/shard_map/all_to_all | solution.py:25
  138.1 7.5 %all-to-all-start.3 = ((f32[32,7,128]{2,1,0:T(8,128)}), f32[32,7,128]{2,1,0:T(8,128)S(1)}, u32[]{:S(2)}, u32[]{:S(2)}) async-start(f32[32,7,128]{2,1,0:T(8,128)} %broadcast_in_dim.28), calls=%async_computation.3 | async-start | bytes 262144 | tf_op jit(solution)/shard_map/all_to_all | solution.py:25
  145.6 7.6 %all-to-all-done.3 = f32[32,7,128]{2,1,0:T(8,128)S(1)} async-done(((f32[32,7,128]{2,1,0:T(8,128)}), f32[32,7,128]{2,1,0:T(8,128)S(1)}, u32[]{:S(2)}, u32[]{:S(2)}) %all-to-all-start.3) | async-done | bytes 114720 | tf_op jit(solution)/shard_map/all_to_all | solution.py:25
  153.3 2.2 collective-permute-start.6
  156.6 6.5 %all-to-all-start.4 = ((bf16[16,64,128]{2,1,0:T(8,128)(2,1)}), bf16[16,64,128]{2,1,0:T(8,128)(2,1)S(1)}, u32[]{:S(2)}, u32[]{:S(2)}) async-start(bf16[16,64,128]{2,1,0:T(8,128)(2,1)} %broadcast_in_dim.29), calls=%async_computation.4 | async-start | bytes 524288 | tf_op jit(solution)/shard_map/all_to_all | solution.py:25
  163.1 1.3 copy.109
  164.9 2.4 fusion.8
  167.3 1.7 fusion.142
  169.0 8.2 %all-to-all-done.4 = bf16[16,64,128]{2,1,0:T(8,128)(2,1)S(1)} async-done(((bf16[16,64,128]{2,1,0:T(8,128)(2,1)}), bf16[16,64,128]{2,1,0:T(8,128)(2,1)S(1)}, u32[]{:S(2)}, u32[]{:S(2)}) %all-to-all-start.4) | async-done | bytes 262176 | tf_op jit(solution)/shard_map/all_to_all | solution.py:25
  177.2 1.4 convolution_convert_fusion.1
  180.8 2.3 fusion.23
  183.2 6.9 %collective-permute-start.7 = (bf16[552,1024]{1,0:T(8,128)(2,1)}, bf16[552,1024]{1,0:T(8,128)(2,1)}, u32[]{:S(2)}, u32[]{:S(2)}) collective-permute-start(bf16[552,1024]{1,0:T(8,128)(2,1)} %fusion.23), channel_id=1, source_target_pairs={{0,64},{64,0},{1,65},{65,1},{2,66},{66,2},{3,67},{67,3},{4,68},{68... | collective-permute-start | bytes 3391496 | tf_op jit(solution)/shard_map/ppermute | solution.py:21
  190.6 2.2 collective-permute-done.7
  192.8 1.8 convert_add_fusion
  195.8 2.8 maximum_maximum_fusion
  198.6 4.4 %all-to-all-start.5 = ((bf16[16,40,1024]{2,1,0:T(8,128)(2,1)}), bf16[16,40,1024]{2,1,0:T(8,128)(2,1)}, u32[]{:S(2)}, u32[]{:S(2)}) async-start(bf16[16,40,1024]{2,1,0:T(8,128)(2,1)} %maximum_maximum_fusion), calls=%async_computation.5 | async-start | bytes 2621440 | tf_op jit(solution)/shard_map/all_to_all | solution.py:25
  203.0 5.3 %convolution_convert_fusion = bf16[1024,1024]{1,0:T(8,128)(2,1)} fusion(bf16[1024,1024]{1,0:T(8,128)(2,1)S(1)} %fusion.8, bf16[1024,1024]{1,0:T(8,128)(2,1)} %pad_maximum_fusion), kind=kOutput, calls=%fused_computation.19 | convolution fusion | flops 2148532224 | bytes 6291456 | tf_op jit(solution)/shard_map/dot_general | solution.py:172
  208.3 4.6 %collective-permute-start.8 = (bf16[1024,128]{0,1:T(8,128)(2,1)S(1)}, bf16[1024,128]{0,1:T(8,128)(2,1)S(1)}, u32[]{:S(2)}, u32[]{:S(2)}) collective-permute-start(bf16[1024,128]{0,1:T(8,128)(2,1)S(1)} %copy.113), channel_id=1, source_target_pairs={{0,2},{2,0},{1,3},{3,1},{4,6},{6,4},{5,7},{7,5},{8,10},{10,8},{9,1... | collective-permute-start | bytes 786440 | tf_op jit(solution)/shard_map/ppermute | solution.py:21
  212.9 8.5 %all-to-all-done.5 = bf16[16,40,1024]{2,1,0:T(8,128)(2,1)} async-done(((bf16[16,40,1024]{2,1,0:T(8,128)(2,1)}), bf16[16,40,1024]{2,1,0:T(8,128)(2,1)}, u32[]{:S(2)}, u32[]{:S(2)}) %all-to-all-start.5) | async-done | bytes 1310752 | tf_op jit(solution)/shard_map/all_to_all | solution.py:25
  221.3 1.6 convert_reduce_fusion.1
  223.7 1.7 multiply_reduce_fusion.5
  227.1 26.6 %all_to_all.36 = bf16[16,40,1024]{2,1,0:T(8,128)(2,1)} all-to-all(bf16[16,40,1024]{2,1,0:T(8,128)(2,1)S(1)} %broadcast_in_dim.33), channel_id=1, replica_groups=mesh['y'=4,'core'=2,'z'=16,'xh'=2,'xl'=2] {'y','xl','xh'}, dimensions={0} | all-to-all | bytes 2621440 | tf_op jit(solution)/shard_map/all_to_all | solution.py:25
  253.7 5.0 %collective-permute-start.9 = (bf16[16,40,1024]{2,1,0:T(8,128)(2,1)}, bf16[16,40,1024]{2,1,0:T(8,128)(2,1)}, u32[]{:S(2)}, u32[]{:S(2)}) collective-permute-start(bf16[16,40,1024]{2,1,0:T(8,128)(2,1)} %all_to_all.36), channel_id=1, source_target_pairs={{0,64},{64,0},{1,65},{65,1},{2,66},{66,2},{3,67},{67,3},{4,68},{68... | collective-permute-start | bytes 3932168 | tf_op jit(solution)/shard_map/ppermute | solution.py:21
  259.4 2.1 collective-permute-done.9
  261.4 1.9 broadcast_select_fusion.1
  264.8 1.7 multiply_reduce_fusion
  267.5 3.1 %fusion.20 = f32[32,1024]{1,0:T(8,128)S(1)} fusion(bf16[1024,1024]{1,0:T(8,128)(2,1)} %convolution_convert_fusion, bf16[512,1024]{1,0:T(8,128)(2,1)} %bitcast.105, bf16[512,1024]{1,0:T(8,128)(2,1)} %bitcast.108, bf16[32,512]{1,0:T(8,128)(2,1)S(1)} %reshape.448, bf16[32,512]{1,0:T(8,128)(2,1)S(1)} %reshape.447, f32[32]{0:T(128)S(1)} %get-tuple-element.32, ...), kind=kOutput, calls=%fused_computation.41 | convolution fusion | flops 138772480 | bytes 4400256 | tf_op jit(solution)/shard_map/dot_general | solution.py:263
  270.6 2.7 fusion.19
  273.3 4.7 %fusion.26 = f32[1024,256]{1,0:T(8,128)} fusion(bf16[1024,1024]{1,0:T(8,128)(2,1)S(1)} %fusion.8, f32[1024,256]{0,1:T(8,128)} %fusion.142, bf16[512,1024]{1,0:T(8,128)(2,1)} %bitcast.106, bf16[512,1024]{1,0:T(8,128)(2,1)} %bitcast.109, bf16[1024,128]{0,1:T(8,128)(2,1)S(1)} %get-tuple-element.59, bf16[1024,128]{0,1:T(8,128)(2,1)S(1)} %get-tuple-element.58, ...), kind=kOutput, calls=%fused_computation.55 | convolution fusion | flops 1081868288 | bytes 6828032 | tf_op jit(solution)/shard_map/dot_general | solution.py:255
  (128 shorter events, 24.4 us)
Async XLA Ops:
  7.2 10.6 %copy-start.1 = (bf16[1024,256]{1,0:T(8,128)(2,1)S(1)}, bf16[1024,256]{1,0:T(8,128)(2,1)}, u32[]{:S(2)}) copy-start(bf16[1024,256]{1,0:T(8,128)(2,1)} %param.15) | copy-start | bytes 1572868
  7.2 80.4 %all-gather.3.cloned.1.call-start = ((), (), s32[]{:S(2)}) async-start(), calls=%async_computation.7 | async-start | bytes 5013504 | tf_op jit(solution)/shard_map/all_gather | solution.py:84
  9.8 14.8 %copy-start.5 = (bf16[448,256]{1,0:T(8,128)(2,1)S(1)}, bf16[448,256]{1,0:T(8,128)(2,1)}, u32[]{:S(2)}) copy-start(bf16[448,256]{1,0:T(8,128)(2,1)} %param.9) | copy-start | bytes 688132
  12.3 11.2 %collective-permute-start.1 = (bf16[464,128]{1,0:T(8,128)(2,1)S(1)}, bf16[464,128]{1,0:T(8,128)(2,1)S(1)}, u32[]{:S(2)}, u32[]{:S(2)}) collective-permute-start(bf16[464,128]{1,0:T(8,128)(2,1)S(1)} %pad_maximum_fusion.10), channel_id=1, source_target_pairs={{0,2},{2,0},{1,3},{3,1},{4,6},{6,4},{5,7},{7,5},{8,10},{10,8},{9,1... | collective-permute-start | bytes 356360 | tf_op jit(solution)/shard_map/ppermute | solution.py:21
  18.3 7.5 %collective-permute-start = (bf16[512,1024]{1,0:T(8,128)(2,1)S(1)}, bf16[512,1024]{1,0:T(8,128)(2,1)S(1)}, u32[]{:S(2)}, u32[]{:S(2)}) collective-permute-start(bf16[512,1024]{1,0:T(8,128)(2,1)S(1)} %convolution_convert_fusion.4), channel_id=1, source_target_pairs={{0,64},{64,0},{1,65},{65,1},{2,66},{66,2},{3,67},{67,3},{4,68},{68... | collective-permute-start | bytes 3145736 | tf_op jit(solution)/shard_map/ppermute | solution.py:21
  40.8 4.7 %copy-start.7 = (bf16[448,896]{1,0:T(8,128)(2,1)S(1)}, bf16[448,896]{1,0:T(8,128)(2,1)}, u32[]{:S(2)}) copy-start(bf16[448,896]{1,0:T(8,128)(2,1)} %param.8) | copy-start | bytes 2408452
  42.0 14.4 %all-to-all-start.1 = ((bf16[8,64,1024]{2,1,0:T(8,128)(2,1)}), bf16[8,64,1024]{2,1,0:T(8,128)(2,1)S(1)}, u32[]{:S(2)}, u32[]{:S(2)}) async-start(bf16[8,64,1024]{2,1,0:T(8,128)(2,1)} %broadcast_in_dim.26), calls=%async_computation.1 | async-start | bytes 2097152 | tf_op jit(solution)/shard_map/all_to_all | solution.py:25
  45.5 35.1 %collective-permute-start.2 = (bf16[448,896]{1,0:T(8,128)(2,1)S(1)}, bf16[448,896]{1,0:T(8,128)(2,1)S(1)}, u32[]{:S(2)}, u32[]{:S(2)}) collective-permute-start(bf16[448,896]{1,0:T(8,128)(2,1)S(1)} %copy-done.7), channel_id=1, source_target_pairs={{0,2},{2,0},{1,3},{3,1},{4,6},{6,4},{5,7},{7,5},{8,10},{10,8},{9,1... | collective-permute-start | bytes 2408456 | tf_op jit(solution)/shard_map/ppermute | solution.py:21
  56.3 24.6 %collective-permute-start.3 = (bf16[512,1024]{1,0:T(8,128)(2,1)S(1)}, bf16[512,1024]{1,0:T(8,128)(2,1)}, u32[]{:S(2)}, u32[]{:S(2)}) collective-permute-start(bf16[512,1024]{1,0:T(8,128)(2,1)S(1)} %bitcast.103), channel_id=1, source_target_pairs={{0,64},{64,0},{1,65},{65,1},{2,66},{66,2},{3,67},{67,3},{4,68},{68... | collective-permute-start | bytes 3145736 | tf_op jit(solution)/shard_map/ppermute | solution.py:21
  87.6 2.3 copy-start
  92.7 13.6 %collective-permute-start.4 = (bf16[8,896,128]{2,1,0:T(8,128)(2,1)S(1)}, bf16[8,896,128]{2,1,0:T(8,128)(2,1)S(1)}, u32[]{:S(2)}, u32[]{:S(2)}) collective-permute-start(bf16[8,896,128]{2,1,0:T(8,128)(2,1)S(1)} %shard_map.104), channel_id=1, source_target_pairs={{0,64},{64,0},{1,65},{65,1},{2,66},{66,2},{3,67},{67,3},{4,68},{68... | collective-permute-start | bytes 5505032 | tf_op jit(solution)/shard_map/ppermute | solution.py:21
  108.1 28.8 %all-to-all-start.2 = ((bf16[8,896,128]{2,1,0:T(8,128)(2,1)}), bf16[8,896,128]{2,1,0:T(8,128)(2,1)S(1)}, u32[]{:S(2)}, u32[]{:S(2)}) async-start(bf16[8,896,128]{2,1,0:T(8,128)(2,1)} %add_convert_fusion), calls=%async_computation.2 | async-start | bytes 3670016 | tf_op jit(solution)/shard_map/all_to_all | solution.py:25
  117.4 19.7 %copy-start.6 = (bf16[896,128]{1,0:T(8,128)(2,1)S(1)}, bf16[896,128]{1,0:T(8,128)(2,1)}, u32[]{:S(2)}) copy-start(bf16[896,128]{1,0:T(8,128)(2,1)} %pad_maximum_fusion.9) | copy-start | bytes 688132
  118.2 35.1 %collective-permute-start.5 = (bf16[8,256,128]{2,1,0:T(8,128)(2,1)}, bf16[8,256,128]{2,1,0:T(8,128)(2,1)}, u32[]{:S(2)}, u32[]{:S(2)}) collective-permute-start(bf16[8,256,128]{2,1,0:T(8,128)(2,1)} %constant_dynamic-slice_fusion.4), channel_id=1, source_target_pairs={{0,2},{2,0},{1,3},{3,1},{4,6},{6,4},{5,7},{7,5},{8,10},{10,8},{9,1... | collective-permute-start | bytes 1572872 | tf_op jit(solution)/shard_map/ppermute | solution.py:21
  138.1 15.2 %all-to-all-start.3 = ((f32[32,7,128]{2,1,0:T(8,128)}), f32[32,7,128]{2,1,0:T(8,128)S(1)}, u32[]{:S(2)}, u32[]{:S(2)}) async-start(f32[32,7,128]{2,1,0:T(8,128)} %broadcast_in_dim.28), calls=%async_computation.3 | async-start | bytes 262144 | tf_op jit(solution)/shard_map/all_to_all | solution.py:25
  153.3 11.3 %collective-permute-start.6 = (bf16[8,256,128]{2,1,0:T(8,128)(2,1)}, bf16[8,256,128]{2,1,0:T(8,128)(2,1)S(1)}, u32[]{:S(2)}, u32[]{:S(2)}) collective-permute-start(bf16[8,256,128]{2,1,0:T(8,128)(2,1)} %collective-permute-done.5), channel_id=1, source_target_pairs={{0,64},{64,0},{1,65},{65,1},{2,66},{66,2},{3,67},{67,3},{4,68},{68... | collective-permute-start | bytes 1572872 | tf_op jit(solution)/shard_map/ppermute | solution.py:21
  156.6 20.6 %all-to-all-start.4 = ((bf16[16,64,128]{2,1,0:T(8,128)(2,1)}), bf16[16,64,128]{2,1,0:T(8,128)(2,1)S(1)}, u32[]{:S(2)}, u32[]{:S(2)}) async-start(bf16[16,64,128]{2,1,0:T(8,128)(2,1)} %broadcast_in_dim.29), calls=%async_computation.4 | async-start | bytes 524288 | tf_op jit(solution)/shard_map/all_to_all | solution.py:25
  163.1 1.8 copy-start.4
  183.2 9.7 %collective-permute-start.7 = (bf16[552,1024]{1,0:T(8,128)(2,1)}, bf16[552,1024]{1,0:T(8,128)(2,1)}, u32[]{:S(2)}, u32[]{:S(2)}) collective-permute-start(bf16[552,1024]{1,0:T(8,128)(2,1)} %fusion.23), channel_id=1, source_target_pairs={{0,64},{64,0},{1,65},{65,1},{2,66},{66,2},{3,67},{67,3},{4,68},{68... | collective-permute-start | bytes 3391496 | tf_op jit(solution)/shard_map/ppermute | solution.py:21
  198.6 22.7 %all-to-all-start.5 = ((bf16[16,40,1024]{2,1,0:T(8,128)(2,1)}), bf16[16,40,1024]{2,1,0:T(8,128)(2,1)}, u32[]{:S(2)}, u32[]{:S(2)}) async-start(bf16[16,40,1024]{2,1,0:T(8,128)(2,1)} %maximum_maximum_fusion), calls=%async_computation.5 | async-start | bytes 2621440 | tf_op jit(solution)/shard_map/all_to_all | solution.py:25
  208.3 18.6 %collective-permute-start.8 = (bf16[1024,128]{0,1:T(8,128)(2,1)S(1)}, bf16[1024,128]{0,1:T(8,128)(2,1)S(1)}, u32[]{:S(2)}, u32[]{:S(2)}) collective-permute-start(bf16[1024,128]{0,1:T(8,128)(2,1)S(1)} %copy.113), channel_id=1, source_target_pairs={{0,2},{2,0},{1,3},{3,1},{4,6},{6,4},{5,7},{7,5},{8,10},{10,8},{9,1... | collective-permute-start | bytes 786440 | tf_op jit(solution)/shard_map/ppermute | solution.py:21
  253.7 7.8 %collective-permute-start.9 = (bf16[16,40,1024]{2,1,0:T(8,128)(2,1)}, bf16[16,40,1024]{2,1,0:T(8,128)(2,1)}, u32[]{:S(2)}, u32[]{:S(2)}) collective-permute-start(bf16[16,40,1024]{2,1,0:T(8,128)(2,1)} %all_to_all.36), channel_id=1, source_target_pairs={{0,64},{64,0},{1,65},{65,1},{2,66},{66,2},{3,67},{67,3},{4,68},{68... | collective-permute-start | bytes 3932168 | tf_op jit(solution)/shard_map/ppermute | solution.py:21
  263.4 1.0 copy-start.2
  263.6 1.1 copy-start.3
  267.5 3.1 %copy-start.8 = (bf16[32,1024]{1,0:T(8,128)(2,1)S(1)}, bf16[32,1024]{1,0:T(8,128)(2,1)}, u32[]{:S(2)}) copy-start(bf16[32,1024]{1,0:T(8,128)(2,1)} %param.14) | copy-start | bytes 196612
Sparse Core Ops, SparseCore 0:
  10.1 77.4 all-gather.2

commit v7 on v3

--- a/solution.py
+++ b/solution.py
@@ -32,6 +32,10 @@
 def two_parts(value):
     high = lax.reduce_precision(value, 8, 7)
     return high.astype(bf16), (value - high).astype(bf16)
+
+
+def slab_rows(slabs):
+    return slabs.reshape(-1, 8, 32, 128).transpose(0, 2, 1, 3).reshape(-1, 1024)
 
 
 def ordered(index, own, other):
@@ -133,7 +137,12 @@
     place = pick // 2 % 32
     chosen = (pick // 64 * 2 + pick % 2)[None, :] == jnp.arange(32, dtype=jnp.int32)[:, None]
     student_of = place[None, :]
-    source = place * 32 + pick // 64 * 2 + pick % 2
+    block = jnp.where(
+        place // 16 == xh,
+        place % 16,
+        place % 8 + jnp.where(place % 16 // 8 == core, 16, 24),
+    )
+    source = block * 32 + pick // 64 * 2 + pick % 2
     order = (source[:, None] == pick[None, :]).astype(bf16)
     chosen2 = jnp.concatenate([chosen & (student_of == z), chosen & (student_of == 16 + z)]).astype(bf16)
     chosen = (chosen & (student_of == xh * 16 + z)).astype(bf16)
@@ -147,9 +156,7 @@
     squares = jnp.sum(share(squares, PLANE, 32), axis=0).reshape(896)
     squares, slabs = lax.optimization_barrier((squares, weight[:, 896:]))
     far = swap(lax.dynamic_slice_in_dim(slabs, core * 8, 8), "xh")
-    far = jnp.concatenate(ordered(core, far, swap(far, "core")))
-    emb = jnp.concatenate(ordered(xh, slabs, far)).reshape(32, 8, 32, 128)
-    emb = emb.transpose(0, 2, 1, 3).reshape(1024, 1024)
+    emb = jnp.concatenate([slab_rows(slabs), slab_rows(far), slab_rows(swap(far, "core"))])
     normed = (y * lax.rsqrt(squares / D + 1e-05)[:, None] * gain).astype(bf16)
     pooled = (jnp.dot(pool, normed, preferred_element_type=f32) / count).astype(bf16)
     teach = share(pooled, "z", 16).reshape(1024, 128)
@@ -207,7 +214,6 @@
         axis=1,
     )
     total = jnp.sum(exchange(pair, CHIPS).astype(f32), axis=0)
-    total, teach_other = lax.optimization_barrier((total, teach_other))
     sum_tt = total[32] + total[33]
     scale_t = 1.0 / (root * jnp.sqrt(sum_tt / D + 1e-06))
     inverse_u = 1.0 / (root * jnp.sqrt((total[34] + total[35]) / D + 1e-06))
@@ -229,6 +235,7 @@
             jnp.pad(jnp.concatenate([in_hi, in_lo])[None], ((0, 5), (0, 960))),
         ]
     )
+    block, teach_other = lax.optimization_barrier((block, teach_other))
     block = share(block, CHIPS, 16)
     even, odd = ordered(core, block, swap(block, "core"))
     diff_b = jnp.concatenate([even[:, :32].reshape(512, 1024), odd[:, :32].reshape(512, 1024)])

time: 282 us -> 284 us (level)
  waiting for transfers between devices: 62 us -> 55.1 us
  blocking collectives: 65.8 us -> 70.7 us
  local copies, waits for them, and re-layouts: 12.5 us -> 17.4 us
    ppermute x10, waiting for transfers between devices: 34.9 us -> 28 us  [swap(): return lax.ppermute(value, axis, [(0, 1), (1, 0)])]
    all_to_all x3, blocking collectives: 65.8 us -> 70.7 us  [exchange(): return lax.all_to_all(value, axes, split_axis=0, concat_axis=0)]
    unnamed x33 -> x36, local copies, waits for them, and re-layouts: 5 us -> 7.1 us
    select_n x8 -> x6, other arithmetic: 6.32 us -> 4.91 us  [ordered(): return (jnp.where(first, own, other), jnp.where(first, other, own))]
  transfers between devices with their start and end apart: 15 -> 15, of which waited for: 11 -> 11; matrix products, arithmetic and copies ran while one was open for 5% -> 8% of each run, Pallas kernels for 1% -> 1%
where the time goes in v7:
time: 284 us; the launch traced here: 283 us
  starting transfers between devices  78 us (27%)
  blocking collectives  70.7 us (25%)
  waiting for transfers between devices  55.1 us (19%)
  matrix products  19.9 us (7%)
  other arithmetic  18.9 us (7%)
  local copies, waits for them, and re-layouts  17.4 us (6%)
  between operations  17.4 us (6%)
  Pallas kernels  5.57 us (2%)
    all_to_all x3, blocking collectives, exchange(): return lax.all_to_all(value, axes, split_axis=0, concat_axis=0)  70.7 us
    ppermute x10, starting transfers between devices, swap(): return lax.ppermute(value, axis, [(0, 1), (1, 0)])  57.4 us
    ppermute x10, waiting for transfers between devices, swap(): return lax.ppermute(value, axis, [(0, 1), (1, 0)])  28 us
    all_to_all x4, waiting for transfers between devices, exchange(): return lax.all_to_all(value, axes, split_axis=0, concat_axis=0)  23.5 us
    all_to_all x4, starting transfers between devices, exchange(): return lax.all_to_all(value, axes, split_axis=0, concat_axis=0)  20.5 us
    unnamed x36, local copies, waits for them, and re-layouts  7.1 us
  transfers between devices with their start and end apart: 15, of which 11 were waited for; matrix products, arithmetic and copies ran while one was open for 8% of the time, Pallas kernels for 1%

profile of v7, /device:TPU:1, one launch (start us, length us, event | category | flops | bytes accessed | tf_op | source)
XLA Modules:
  0.0 282.8 jit_solution(11651641254330203688)
XLA Ops:
  8.1 1.7 pad_maximum_fusion.6
  11.3 1.0 broadcast_select_fusion.11
  12.3 5.5 %collective-permute-start.1 = (bf16[464,128]{1,0:T(8,128)(2,1)S(1)}, bf16[464,128]{1,0:T(8,128)(2,1)S(1)}, u32[]{:S(2)}, u32[]{:S(2)}) collective-permute-start(bf16[464,128]{1,0:T(8,128)(2,1)S(1)} %pad_maximum_fusion.9), channel_id=1, source_target_pairs={{0,2},{2,0},{1,3},{3,1},{4,6},{6,4},{5,7},{7,5},{8,10},{10,8},{9,1... | collective-permute-start | bytes 356360 | tf_op jit(solution)/shard_map/ppermute | solution.py:21
  18.3 5.2 %collective-permute-start = (bf16[512,1024]{1,0:T(8,128)(2,1)S(1)}, bf16[512,1024]{1,0:T(8,128)(2,1)S(1)}, u32[]{:S(2)}, u32[]{:S(2)}) collective-permute-start(bf16[512,1024]{1,0:T(8,128)(2,1)S(1)} %convolution_convert_fusion.3), channel_id=1, source_target_pairs={{0,64},{64,0},{1,65},{65,1},{2,66},{66,2},{3,67},{67,3},{4,68},{68... | collective-permute-start | bytes 3145736 | tf_op jit(solution)/shard_map/ppermute | solution.py:21
  24.7 1.0 collective-permute-done
  26.3 15.3 %all_to_all.35 = bf16[8,64,1024]{2,1,0:T(8,128)(2,1)S(1)} all-to-all(bf16[8,64,1024]{2,1,0:T(8,128)(2,1)S(1)} %bitcast.112), channel_id=1, replica_groups=mesh['y'=4,'core'=2,'z'=16,'xh'=2,'xl'=2] {'y','xl'}, dimensions={0} | all-to-all | bytes 2097152 | tf_op jit(solution)/shard_map/all_to_all | solution.py:25
  41.8 1.1 broadcast_in_dim.26
  42.9 3.6 %all-to-all-start.1 = ((bf16[8,64,1024]{2,1,0:T(8,128)(2,1)}), bf16[8,64,1024]{2,1,0:T(8,128)(2,1)S(1)}, u32[]{:S(2)}, u32[]{:S(2)}) async-start(bf16[8,64,1024]{2,1,0:T(8,128)(2,1)} %broadcast_in_dim.26), calls=%async_computation.1 | async-start | bytes 2097152 | tf_op jit(solution)/shard_map/all_to_all | solution.py:25
  46.5 7.7 %collective-permute-start.2 = (bf16[448,896]{1,0:T(8,128)(2,1)S(1)}, bf16[448,896]{1,0:T(8,128)(2,1)S(1)}, u32[]{:S(2)}, u32[]{:S(2)}) collective-permute-start(bf16[448,896]{1,0:T(8,128)(2,1)S(1)} %copy-done.10), channel_id=1, source_target_pairs={{0,2},{2,0},{1,3},{3,1},{4,6},{6,4},{5,7},{7,5},{8,10},{10,8},{9,1... | collective-permute-start | bytes 2408456 | tf_op jit(solution)/shard_map/ppermute | solution.py:21
  54.2 4.3 %all-to-all-done.1 = bf16[8,64,1024]{2,1,0:T(8,128)(2,1)S(1)} async-done(((bf16[8,64,1024]{2,1,0:T(8,128)(2,1)}), bf16[8,64,1024]{2,1,0:T(8,128)(2,1)S(1)}, u32[]{:S(2)}, u32[]{:S(2)}) %all-to-all-start.1) | async-done | bytes 1048608 | tf_op jit(solution)/shard_map/all_to_all | solution.py:25
  58.5 10.7 %collective-permute-start.3 = (bf16[512,1024]{1,0:T(8,128)(2,1)S(1)}, bf16[512,1024]{1,0:T(8,128)(2,1)}, u32[]{:S(2)}, u32[]{:S(2)}) collective-permute-start(bf16[512,1024]{1,0:T(8,128)(2,1)S(1)} %bitcast.104), channel_id=1, source_target_pairs={{0,64},{64,0},{1,65},{65,1},{2,66},{66,2},{3,67},{67,3},{4,68},{68... | collective-permute-start | bytes 3145736 | tf_op jit(solution)/shard_map/ppermute | solution.py:21
  69.2 11.4 %collective-permute-done.2 = bf16[448,896]{1,0:T(8,128)(2,1)S(1)} collective-permute-done((bf16[448,896]{1,0:T(8,128)(2,1)S(1)}, bf16[448,896]{1,0:T(8,128)(2,1)S(1)}, u32[]{:S(2)}, u32[]{:S(2)}) %collective-permute-start.2) | collective-permute-done | bytes 802848 | tf_op jit(solution)/shard_map/ppermute | solution.py:21
  80.9 1.4 broadcast_select_fusion.3
  82.3 1.6 pad_maximum_fusion
  83.9 3.6 %all-gather.3.cloned.1.call-done = bf16[18432,128]{1,0:T(8,128)(2,1)} async-done(((bf16[1152,128]{1,0:T(8,128)(2,1)}), bf16[18432,128]{1,0:T(8,128)(2,1)}) %all-gather.3.cloned.1.call-update) | async-done | bytes 4718608 | tf_op jit(solution)/shard_map/all_gather | solution.py:84
  87.5 2.3 copy-done
  89.8 2.8 shard_map.104
  92.6 10.4 %collective-permute-start.4 = (bf16[8,896,128]{2,1,0:T(8,128)(2,1)S(1)}, bf16[8,896,128]{2,1,0:T(8,128)(2,1)S(1)}, u32[]{:S(2)}, u32[]{:S(2)}) collective-permute-start(bf16[8,896,128]{2,1,0:T(8,128)(2,1)S(1)} %shard_map.104), channel_id=1, source_target_pairs={{0,64},{64,0},{1,65},{65,1},{2,66},{66,2},{3,67},{67,3},{4,68},{68... | collective-permute-start | bytes 5505032 | tf_op jit(solution)/shard_map/ppermute | solution.py:21
  103.0 2.8 shard_map.103
  106.9 27.9 %all_to_all.36 = bf16[8,896,128]{2,1,0:T(8,128)(2,1)S(1)} all-to-all(bf16[8,896,128]{2,1,0:T(8,128)(2,1)S(1)} %add_convert_fusion), channel_id=1, replica_groups=mesh['y'=4,'core'=2,'z'=16,'xh'=2,'xl'=2] {'y','xl'}, dimensions={0} | all-to-all | bytes 3670016 | tf_op jit(solution)/shard_map/all_to_all | solution.py:25
  135.9 6.6 %all-to-all-start.3 = ((f32[32,7,128]{2,1,0:T(8,128)}), f32[32,7,128]{2,1,0:T(8,128)S(1)}, u32[]{:S(2)}, u32[]{:S(2)}) async-start(f32[32,7,128]{2,1,0:T(8,128)} %broadcast_in_dim.28), calls=%async_computation.3 | async-start | bytes 262144 | tf_op jit(solution)/shard_map/all_to_all | solution.py:25
  143.3 1.3 slice.161
  144.6 5.5 %all-to-all-done.3 = f32[32,7,128]{2,1,0:T(8,128)S(1)} async-done(((f32[32,7,128]{2,1,0:T(8,128)}), f32[32,7,128]{2,1,0:T(8,128)S(1)}, u32[]{:S(2)}, u32[]{:S(2)}) %all-to-all-start.3) | async-done | bytes 114720 | tf_op jit(solution)/shard_map/all_to_all | solution.py:25
  151.3 6.5 %all-to-all-start.4 = ((bf16[16,64,128]{2,1,0:T(8,128)(2,1)}), bf16[16,64,128]{2,1,0:T(8,128)(2,1)S(1)}, u32[]{:S(2)}, u32[]{:S(2)}) async-start(bf16[16,64,128]{2,1,0:T(8,128)(2,1)} %broadcast_in_dim.29), calls=%async_computation.4 | async-start | bytes 524288 | tf_op jit(solution)/shard_map/all_to_all | solution.py:25
  158.2 2.5 collective-permute-start.5
  161.3 1.2 copy.137
  162.5 12.1 %collective-permute-done.5 = bf16[8,256,128]{2,1,0:T(8,128)(2,1)} collective-permute-done((bf16[8,256,128]{2,1,0:T(8,128)(2,1)S(1)}, bf16[8,256,128]{2,1,0:T(8,128)(2,1)}, u32[]{:S(2)}, u32[]{:S(2)}) %collective-permute-start.5) | collective-permute-done | bytes 524320 | tf_op jit(solution)/shard_map/ppermute | solution.py:21
  174.7 1.3 copy.109
  176.0 3.5 %collective-permute-start.6 = (bf16[8,256,128]{2,1,0:T(8,128)(2,1)}, bf16[8,256,128]{2,1,0:T(8,128)(2,1)}, u32[]{:S(2)}, u32[]{:S(2)}) collective-permute-start(bf16[8,256,128]{2,1,0:T(8,128)(2,1)} %collective-permute-done.5), channel_id=1, source_target_pairs={{0,64},{64,0},{1,65},{65,1},{2,66},{66,2},{3,67},{67,3},{4,68},{68... | collective-permute-start | bytes 1572872 | tf_op jit(solution)/shard_map/ppermute | solution.py:21
  181.2 1.3 copy.110
  182.6 3.6 %fusion.8 = bf16[1024,1024]{1,0:T(8,128)(2,1)S(1)} fusion(bf16[256,1024]{1,0:T(8,128)(2,1)S(1)} %bitcast.118, bf16[256,1024]{1,0:T(8,128)(2,1)S(1)} %bitcast.117, bf16[512,1024]{1,0:T(8,128)(2,1)} %bitcast.116, s32[1024]{0:T(1024)S(1)} %get-tuple-element.77), kind=kOutput, calls=%fused_computation.18 | convolution fusion | flops 2155872256 | bytes 4198400 | tf_op jit(solution)/shard_map/dot_general | solution.py:165
  187.6 1.1 fusion.23
  188.7 2.3 collective-permute-start.7
  191.5 2.0 collective-permute-done.7
  194.3 1.6 maximum_maximum_fusion
  195.9 3.8 %all-to-all-start.5 = ((bf16[16,40,1024]{2,1,0:T(8,128)(2,1)}), bf16[16,40,1024]{2,1,0:T(8,128)(2,1)S(1)}, u32[]{:S(2)}, u32[]{:S(2)}) async-start(bf16[16,40,1024]{2,1,0:T(8,128)(2,1)} %maximum_maximum_fusion), calls=%async_computation.5 | async-start | bytes 2621440 | tf_op jit(solution)/shard_map/all_to_all | solution.py:25
  199.8 4.6 %collective-permute-start.8 = (bf16[1024,128]{0,1:T(8,128)(2,1)}, bf16[1024,128]{0,1:T(8,128)(2,1)}, u32[]{:S(2)}, u32[]{:S(2)}) collective-permute-start(bf16[1024,128]{0,1:T(8,128)(2,1)} %copy-done.8), channel_id=1, source_target_pairs={{0,2},{2,0},{1,3},{3,1},{4,6},{6,4},{5,7},{7,5},{8,10},{10,8},{9,1... | collective-permute-start | bytes 786440 | tf_op jit(solution)/shard_map/ppermute | solution.py:21
  204.4 13.6 %all-to-all-done.5 = bf16[16,40,1024]{2,1,0:T(8,128)(2,1)S(1)} async-done(((bf16[16,40,1024]{2,1,0:T(8,128)(2,1)}), bf16[16,40,1024]{2,1,0:T(8,128)(2,1)S(1)}, u32[]{:S(2)}, u32[]{:S(2)}) %all-to-all-start.5) | async-done | bytes 1310752 | tf_op jit(solution)/shard_map/all_to_all | solution.py:25
  219.7 2.8 multiply_reduce_fusion.5
  224.0 27.4 %all_to_all.37 = bf16[16,40,1024]{2,1,0:T(8,128)(2,1)S(1)} all-to-all(bf16[16,40,1024]{2,1,0:T(8,128)(2,1)S(1)} %broadcast_in_dim.33), channel_id=1, replica_groups=mesh['y'=4,'core'=2,'z'=16,'xh'=2,'xl'=2] {'y','xl','xh'}, dimensions={0} | all-to-all | bytes 2621440 | tf_op jit(solution)/shard_map/all_to_all | solution.py:25
  251.4 5.0 %collective-permute-start.9 = (bf16[16,40,1024]{2,1,0:T(8,128)(2,1)S(1)}, bf16[16,40,1024]{2,1,0:T(8,128)(2,1)}, u32[]{:S(2)}, u32[]{:S(2)}) collective-permute-start(bf16[16,40,1024]{2,1,0:T(8,128)(2,1)S(1)} %all_to_all.37), channel_id=1, source_target_pairs={{0,64},{64,0},{1,65},{65,1},{2,66},{66,2},{3,67},{67,3},{4,68},{68... | collective-permute-start | bytes 3932168 | tf_op jit(solution)/shard_map/ppermute | solution.py:21
  257.1 1.9 broadcast_select_fusion.7
  259.0 1.5 broadcast_select_fusion.1
  261.9 1.7 multiply_reduce_fusion
  264.4 1.7 fusion.24
  266.3 2.5 fusion.20
  268.8 1.1 fusion.19
  270.0 4.8 %fusion.26 = f32[1024,256]{1,0:T(8,128)} fusion(bf16[1024,1024]{1,0:T(8,128)(2,1)} %copy-done.2, f32[1024,256]{0,1:T(8,128)S(1)} %copy-done.5, bf16[512,1024]{1,0:T(8,128)(2,1)} %bitcast.107, bf16[512,1024]{1,0:T(8,128)(2,1)} %bitcast.110, bf16[1024,128]{0,1:T(8,128)(2,1)} %get-tuple-element.55, bf16[1024,128]{0,1:T(8,128)(2,1)} %get-tuple-element.54, ...), kind=kOutput, calls=%fused_computation.56 | convolution fusion | flops 1081868288 | bytes 6828032 | tf_op jit(solution)/shard_map/dot_general | solution.py:257
  (134 shorter events, 19.4 us)
Async XLA Ops:
  7.2 10.6 %copy-start.3 = (bf16[1024,256]{1,0:T(8,128)(2,1)S(1)}, bf16[1024,256]{1,0:T(8,128)(2,1)}, u32[]{:S(2)}) copy-start(bf16[1024,256]{1,0:T(8,128)(2,1)} %param.15) | copy-start | bytes 1572868
  7.2 80.3 %all-gather.3.cloned.1.call-start = ((), (), s32[]{:S(2)}) async-start(), calls=%async_computation.7 | async-start | bytes 5013504 | tf_op jit(solution)/shard_map/all_gather | solution.py:84
  9.9 14.8 %copy-start.9 = (bf16[448,256]{1,0:T(8,128)(2,1)S(1)}, bf16[448,256]{1,0:T(8,128)(2,1)}, u32[]{:S(2)}) copy-start(bf16[448,256]{1,0:T(8,128)(2,1)} %param.9) | copy-start | bytes 688132
  12.3 11.2 %collective-permute-start.1 = (bf16[464,128]{1,0:T(8,128)(2,1)S(1)}, bf16[464,128]{1,0:T(8,128)(2,1)S(1)}, u32[]{:S(2)}, u32[]{:S(2)}) collective-permute-start(bf16[464,128]{1,0:T(8,128)(2,1)S(1)} %pad_maximum_fusion.9), channel_id=1, source_target_pairs={{0,2},{2,0},{1,3},{3,1},{4,6},{6,4},{5,7},{7,5},{8,10},{10,8},{9,1... | collective-permute-start | bytes 356360 | tf_op jit(solution)/shard_map/ppermute | solution.py:21
  18.3 7.5 %collective-permute-start = (bf16[512,1024]{1,0:T(8,128)(2,1)S(1)}, bf16[512,1024]{1,0:T(8,128)(2,1)S(1)}, u32[]{:S(2)}, u32[]{:S(2)}) collective-permute-start(bf16[512,1024]{1,0:T(8,128)(2,1)S(1)} %convolution_convert_fusion.3), channel_id=1, source_target_pairs={{0,64},{64,0},{1,65},{65,1},{2,66},{66,2},{3,67},{67,3},{4,68},{68... | collective-permute-start | bytes 3145736 | tf_op jit(solution)/shard_map/ppermute | solution.py:21
  41.8 4.7 %copy-start.10 = (bf16[448,896]{1,0:T(8,128)(2,1)S(1)}, bf16[448,896]{1,0:T(8,128)(2,1)}, u32[]{:S(2)}) copy-start(bf16[448,896]{1,0:T(8,128)(2,1)} %param.8) | copy-start | bytes 2408452
  42.9 15.6 %all-to-all-start.1 = ((bf16[8,64,1024]{2,1,0:T(8,128)(2,1)}), bf16[8,64,1024]{2,1,0:T(8,128)(2,1)S(1)}, u32[]{:S(2)}, u32[]{:S(2)}) async-start(bf16[8,64,1024]{2,1,0:T(8,128)(2,1)} %broadcast_in_dim.26), calls=%async_computation.1 | async-start | bytes 2097152 | tf_op jit(solution)/shard_map/all_to_all | solution.py:25
  46.5 34.2 %collective-permute-start.2 = (bf16[448,896]{1,0:T(8,128)(2,1)S(1)}, bf16[448,896]{1,0:T(8,128)(2,1)S(1)}, u32[]{:S(2)}, u32[]{:S(2)}) collective-permute-start(bf16[448,896]{1,0:T(8,128)(2,1)S(1)} %copy-done.10), channel_id=1, source_target_pairs={{0,2},{2,0},{1,3},{3,1},{4,6},{6,4},{5,7},{7,5},{8,10},{10,8},{9,1... | collective-permute-start | bytes 2408456 | tf_op jit(solution)/shard_map/ppermute | solution.py:21
  58.5 22.5 %collective-permute-start.3 = (bf16[512,1024]{1,0:T(8,128)(2,1)S(1)}, bf16[512,1024]{1,0:T(8,128)(2,1)}, u32[]{:S(2)}, u32[]{:S(2)}) collective-permute-start(bf16[512,1024]{1,0:T(8,128)(2,1)S(1)} %bitcast.104), channel_id=1, source_target_pairs={{0,64},{64,0},{1,65},{65,1},{2,66},{66,2},{3,67},{67,3},{4,68},{68... | collective-permute-start | bytes 3145736 | tf_op jit(solution)/shard_map/ppermute | solution.py:21
  87.5 2.3 copy-start
  92.6 13.8 %collective-permute-start.4 = (bf16[8,896,128]{2,1,0:T(8,128)(2,1)S(1)}, bf16[8,896,128]{2,1,0:T(8,128)(2,1)S(1)}, u32[]{:S(2)}, u32[]{:S(2)}) collective-permute-start(bf16[8,896,128]{2,1,0:T(8,128)(2,1)S(1)} %shard_map.104), channel_id=1, source_target_pairs={{0,64},{64,0},{1,65},{65,1},{2,66},{66,2},{3,67},{67,3},{4,68},{68... | collective-permute-start | bytes 5505032 | tf_op jit(solution)/shard_map/ppermute | solution.py:21
  135.9 14.2 %all-to-all-start.3 = ((f32[32,7,128]{2,1,0:T(8,128)}), f32[32,7,128]{2,1,0:T(8,128)S(1)}, u32[]{:S(2)}, u32[]{:S(2)}) async-start(f32[32,7,128]{2,1,0:T(8,128)} %broadcast_in_dim.28), calls=%async_computation.3 | async-start | bytes 262144 | tf_op jit(solution)/shard_map/all_to_all | solution.py:25
  151.3 28.3 %all-to-all-start.4 = ((bf16[16,64,128]{2,1,0:T(8,128)(2,1)}), bf16[16,64,128]{2,1,0:T(8,128)(2,1)S(1)}, u32[]{:S(2)}, u32[]{:S(2)}) async-start(bf16[16,64,128]{2,1,0:T(8,128)(2,1)} %broadcast_in_dim.29), calls=%async_computation.4 | async-start | bytes 524288 | tf_op jit(solution)/shard_map/all_to_all | solution.py:25
  158.2 16.4 %collective-permute-start.5 = (bf16[8,256,128]{2,1,0:T(8,128)(2,1)S(1)}, bf16[8,256,128]{2,1,0:T(8,128)(2,1)}, u32[]{:S(2)}, u32[]{:S(2)}) collective-permute-start(bf16[8,256,128]{2,1,0:T(8,128)(2,1)S(1)} %constant_dynamic-slice_fusion.4), channel_id=1, source_target_pairs={{0,2},{2,0},{1,3},{3,1},{4,6},{6,4},{5,7},{7,5},{8,10},{10,8},{9,1... | collective-permute-start | bytes 1572872 | tf_op jit(solution)/shard_map/ppermute | solution.py:21
  176.0 5.2 %collective-permute-start.6 = (bf16[8,256,128]{2,1,0:T(8,128)(2,1)}, bf16[8,256,128]{2,1,0:T(8,128)(2,1)}, u32[]{:S(2)}, u32[]{:S(2)}) collective-permute-start(bf16[8,256,128]{2,1,0:T(8,128)(2,1)} %collective-permute-done.5), channel_id=1, source_target_pairs={{0,64},{64,0},{1,65},{65,1},{2,66},{66,2},{3,67},{67,3},{4,68},{68... | collective-permute-start | bytes 1572872 | tf_op jit(solution)/shard_map/ppermute | solution.py:21
  180.3 6.7 %copy-start.8 = (bf16[1024,128]{0,1:T(8,128)(2,1)}, bf16[1024,128]{0,1:T(8,128)(2,1)S(1)}, u32[]{:S(2)}) copy-start(bf16[1024,128]{0,1:T(8,128)(2,1)S(1)} %copy.113) | copy-start | bytes 786436
  186.2 1.3 copy-start.2
  187.0 4.5 %copy-start.4 = (f32[1024,256]{0,1:T(8,128)}, f32[1024,256]{0,1:T(8,128)S(1)}, u32[]{:S(2)}) copy-start(f32[1024,256]{0,1:T(8,128)S(1)} %fusion.141) | copy-start | bytes 3145732
  188.7 4.9 %collective-permute-start.7 = (bf16[552,1024]{1,0:T(8,128)(2,1)}, bf16[552,1024]{1,0:T(8,128)(2,1)S(1)}, u32[]{:S(2)}, u32[]{:S(2)}) collective-permute-start(bf16[552,1024]{1,0:T(8,128)(2,1)} %fusion.23), channel_id=1, source_target_pairs={{0,64},{64,0},{1,65},{65,1},{2,66},{66,2},{3,67},{67,3},{4,68},{68... | collective-permute-start | bytes 3391496 | tf_op jit(solution)/shard_map/ppermute | solution.py:21
  195.9 23.8 %copy-start.1 = (bf16[1024,1024]{1,0:T(8,128)(2,1)S(1)}, bf16[1024,1024]{1,0:T(8,128)(2,1)}, u32[]{:S(2)}) copy-start(bf16[1024,1024]{1,0:T(8,128)(2,1)} %pad_maximum_fusion) | copy-start | bytes 6291460
  195.9 22.1 %all-to-all-start.5 = ((bf16[16,40,1024]{2,1,0:T(8,128)(2,1)}), bf16[16,40,1024]{2,1,0:T(8,128)(2,1)S(1)}, u32[]{:S(2)}, u32[]{:S(2)}) async-start(bf16[16,40,1024]{2,1,0:T(8,128)(2,1)} %maximum_maximum_fusion), calls=%async_computation.5 | async-start | bytes 2621440 | tf_op jit(solution)/shard_map/all_to_all | solution.py:25
  199.8 24.1 %collective-permute-start.8 = (bf16[1024,128]{0,1:T(8,128)(2,1)}, bf16[1024,128]{0,1:T(8,128)(2,1)}, u32[]{:S(2)}, u32[]{:S(2)}) collective-permute-start(bf16[1024,128]{0,1:T(8,128)(2,1)} %copy-done.8), channel_id=1, source_target_pairs={{0,2},{2,0},{1,3},{3,1},{4,6},{6,4},{5,7},{7,5},{8,10},{10,8},{9,1... | collective-permute-start | bytes 786440 | tf_op jit(solution)/shard_map/ppermute | solution.py:21
  218.3 0.7 copy-start.11
  251.4 7.6 %collective-permute-start.9 = (bf16[16,40,1024]{2,1,0:T(8,128)(2,1)S(1)}, bf16[16,40,1024]{2,1,0:T(8,128)(2,1)}, u32[]{:S(2)}, u32[]{:S(2)}) collective-permute-start(bf16[16,40,1024]{2,1,0:T(8,128)(2,1)S(1)} %all_to_all.37), channel_id=1, source_target_pairs={{0,64},{64,0},{1,65},{65,1},{2,66},{66,2},{3,67},{67,3},{4,68},{68... | collective-permute-start | bytes 3932168 | tf_op jit(solution)/shard_map/ppermute | solution.py:21
  260.6 5.7 %copy-start.6 = (bf16[16,32,1024]{2,1,0:T(8,128)(2,1)}, bf16[16,32,1024]{2,1,0:T(8,128)(2,1)S(1)}, u32[]{:S(2)}) copy-start(bf16[16,32,1024]{2,1,0:T(8,128)(2,1)S(1)} %slice.181) | copy-start | bytes 3145732
  260.8 1.1 copy-start.7
  266.3 2.5 copy-start.12
  268.8 1.2 copy-start.5
Sparse Core Ops, SparseCore 0:
  10.1 77.3 all-gather.2
